TPU v7x, 1024 devices: a whole 8x8x8 slice. The times are simulated.
1024 devices in a mesh: grp: 16 (over x_hi, z), seq: 16 (over y, core), tp: 4 (over x_lo).
Axes of the slice: x: 8 (x_hi: 2, x_lo: 4; x = x_hi * 4 + x_lo), y: 8, z: 8, core: 2. Of those that a mesh axis runs over, the one named last changes fastest.
Arguments:
- queries: bfloat16 [32768, 8192], P(('grp', 'seq', 'tp')), may hold values from -108 to 108
- key_rows: bfloat16 [32768, 1024], P(('grp', 'seq', 'tp')), may hold values from -4 to 4
- value_rows: bfloat16 [32768, 1024], P(('grp', 'seq', 'tp')), may hold values from -6 to 6
- image_lengths: int32 [16, 4], P('grp'), may hold values from 1 to 1024, 2048 in all within a row
- block_table: int32 [256, 16], P(('grp', 'seq')), may hold values from 0 to 15, as said below
Outputs:
- attended: bfloat16 [32768, 8192], P(('grp', 'seq'), 'tp')
Inputs may be any that keep to these rules, and one draw needn't show every extreme that they name: `block_table`: for each shard index and each group, exactly one block of each encoder group's shard is destined to that group.
All inputs are finite; a program needn't handle non-finite values.
Results may differ from a plain program's by a relative error of at most 0.004.
Values may be sent and summed in bfloat16 or wider, within the bound.
No kernel may reach another device: no remote copies, remote signals or barrier semaphores. Data moves between devices by JAX's collectives and lax.ppermute only.
A program may use at most 32 MiB of HBM per device.

v0:
```python
import math

import jax
import jax.numpy as jnp
from jax import lax
from jax.sharding import PartitionSpec as P

HD = 128


MASKED_SCORE = -1e30


def in_one_piece(arrays, axis, dim, along):
    both = jnp.concatenate(arrays, axis=along)
    out, at, done = (lax.all_gather(both, axis, axis=dim, tiled=True), 0, [])
    for a in arrays:
        done.append(lax.slice_in_dim(out, at, at + a.shape[along], axis=along))
        at += a.shape[along]
    return tuple(done)


def image_index(position, bounds):
    return jnp.sum((position[:, None] >= bounds[None, :]).astype(jnp.int32), axis=1)


def absorb_block(
    carried,
    query_block,
    query_pos,
    query_img,
    key_block,
    value_block,
    key_pos,
    key_img,
    key_heads,
    group_ratio,
):
    running_max, running_sum, accumulated = carried
    query_count = query_block.shape[0]
    key_count = key_block.shape[0]
    score_scale = 1.0 / math.sqrt(HD)
    grouped = query_block.reshape(query_count, key_heads, group_ratio, HD)
    key_split = key_block.reshape(key_count, key_heads, HD)
    value_split = value_block.reshape(key_count, key_heads, HD)
    scores = (
        jnp.einsum("nkrd,mkd->krnm", grouped, key_split, preferred_element_type=jnp.float32)
        * score_scale
    )
    visible = (key_pos[None, :] <= query_pos[:, None]) & (key_img[None, :] == query_img[:, None])
    masked = jnp.where(visible, scores, MASKED_SCORE)
    new_max = jnp.maximum(running_max, jnp.max(masked, axis=3))
    weights = jnp.where(visible, jnp.exp(masked - new_max[..., None]), 0.0)
    shrink = jnp.exp(running_max - new_max)
    running_sum = running_sum * shrink + jnp.sum(weights, axis=3)
    accumulated = accumulated * shrink[..., None] + jnp.einsum(
        "krnm,mkd->krnd",
        weights.astype(jnp.bfloat16),
        value_split,
        preferred_element_type=jnp.float32,
    )
    return (new_max, running_sum, accumulated)


def sweep_keys(carried, query_block, query_pos, bounds, key_all, value_all, key_heads, group_ratio):
    key_total = key_all.shape[0]
    step_rows = math.gcd(key_total, 512)
    query_img = image_index(query_pos, bounds)
    first_img = query_img[0]
    last_pos = query_pos[-1]

    def visit(block_index, current):
        key_offset = block_index * step_rows
        key_block = lax.dynamic_slice_in_dim(key_all, key_offset, step_rows, 0)
        value_block = lax.dynamic_slice_in_dim(value_all, key_offset, step_rows, 0)
        key_pos = key_offset + jnp.arange(step_rows, dtype=jnp.int32)
        key_img = image_index(key_pos, bounds)
        needed = (key_pos[0] <= last_pos) & (key_img[-1] >= first_img)
        return lax.cond(
            needed,
            lambda state_in: absorb_block(
                state_in,
                query_block,
                query_pos,
                query_img,
                key_block,
                value_block,
                key_pos,
                key_img,
                key_heads,
                group_ratio,
            ),
            lambda state_in: state_in,
            current,
        )

    return lax.fori_loop(0, key_total // step_rows, visit, carried)


def initial_state(key_heads, group_ratio, query_count):
    return (
        jnp.full((key_heads, group_ratio, query_count), MASKED_SCORE, jnp.float32),
        jnp.zeros((key_heads, group_ratio, query_count), jnp.float32),
        jnp.zeros((key_heads, group_ratio, query_count, HD), jnp.float32),
    )


def finish_heads(running_sum, accumulated, query_count, head_count):
    normal = accumulated / running_sum[..., None]
    return normal.transpose(2, 0, 1, 3).reshape(query_count, head_count * HD).astype(jnp.bfloat16)


def shards(queries, key_rows, value_rows, image_lengths, block_table):
    query_heads, key_split_rows, value_split_rows = (
        lax.all_to_all(queries, "tp", split_axis=1, concat_axis=0, tiled=True),
        lax.all_to_all(key_rows, "tp", split_axis=1, concat_axis=0, tiled=True),
        lax.all_to_all(value_rows, "tp", split_axis=1, concat_axis=0, tiled=True),
    )
    local_rows = query_heads.shape[0]
    group_count = lax.axis_size("grp")
    block_rows = local_rows // group_count
    destination = block_table[0]
    slot_ids = jnp.arange(group_count, dtype=jnp.int32)
    chosen = jnp.sum(
        jnp.where(destination[None, :] == slot_ids[:, None], slot_ids[None, :], 0), axis=1
    )

    def arrange(matrix):
        blocks = matrix.reshape(group_count, block_rows, matrix.shape[1])
        return jnp.take(blocks, chosen, axis=0).reshape(local_rows, matrix.shape[1])

    query_local, key_local, value_local = (
        lax.all_to_all(arrange(query_heads), "grp", split_axis=0, concat_axis=0, tiled=True),
        lax.all_to_all(arrange(key_split_rows), "grp", split_axis=0, concat_axis=0, tiled=True),
        lax.all_to_all(arrange(value_split_rows), "grp", split_axis=0, concat_axis=0, tiled=True),
    )
    bounds = jnp.cumsum(image_lengths[0])[:-1]
    heads_local = query_local.shape[1] // HD
    kv_local = key_local.shape[1] // HD
    group_ratio = heads_local // kv_local
    query_pos = lax.axis_index("seq") * local_rows + jnp.arange(local_rows, dtype=jnp.int32)
    pieces = in_one_piece((key_local, value_local), "seq", 0, 1)
    running_max, running_sum, accumulated = sweep_keys(
        initial_state(kv_local, group_ratio, local_rows),
        query_local,
        query_pos,
        bounds,
        pieces[0],
        pieces[1],
        kv_local,
        group_ratio,
    )
    return finish_heads(running_sum, accumulated, local_rows, heads_local)


def solution(mesh):
    in_specs = (
        P(("grp", "seq", "tp"), None),
        P(("grp", "seq", "tp"), None),
        P(("grp", "seq", "tp"), None),
        P("grp", None),
        P(("grp", "seq"), None),
    )
    out_specs = P(("grp", "seq"), "tp")
    return jax.shard_map(shards, mesh=mesh, in_specs=in_specs, out_specs=out_specs, check_vma=False)
```

profile of v0, /device:TPU:120, one launch (start us, length us, event | category | flops | bytes accessed | tf_op | source)
XLA Modules:
  0.0 155.6 jit_solution(4666601750798588861)
XLA Ops:
  6.5 1.5 copy.69
  8.0 3.3 %all-to-all-start = ((bf16[32,4,256]{2,0,1:T(8,128)(2,1)}), bf16[32,4,256]{2,0,1:T(8,128)(2,1)S(1)}, u32[]{:S(2)}, u32[]{:S(2)}) async-start(bf16[32,4,256]{2,0,1:T(8,128)(2,1)} %bitcast.70), calls=%async_computation | async-start | bytes 131072 | tf_op jit(solution)/shard_map/all_to_all | solution.py:116
  12.1 1.5 copy.68
  13.6 3.5 %all-to-all-done = bf16[32,4,256]{2,0,1:T(8,128)(2,1)S(1)} async-done(((bf16[32,4,256]{2,0,1:T(8,128)(2,1)}), bf16[32,4,256]{2,0,1:T(8,128)(2,1)S(1)}, u32[]{:S(2)}, u32[]{:S(2)}) %all-to-all-start) | async-done | bytes 65568 | tf_op jit(solution)/shard_map/all_to_all | solution.py:116
  17.0 3.3 %all-to-all-start.2 = ((bf16[32,4,256]{2,0,1:T(8,128)(2,1)}), bf16[32,4,256]{2,0,1:T(8,128)(2,1)S(1)}, u32[]{:S(2)}, u32[]{:S(2)}) async-start(bf16[32,4,256]{2,0,1:T(8,128)(2,1)} %bitcast.69), calls=%async_computation.2 | async-start | bytes 131072 | tf_op jit(solution)/shard_map/all_to_all | solution.py:117
  20.9 5.1 %all-to-all-done.2 = bf16[32,4,256]{2,0,1:T(8,128)(2,1)S(1)} async-done(((bf16[32,4,256]{2,0,1:T(8,128)(2,1)}), bf16[32,4,256]{2,0,1:T(8,128)(2,1)S(1)}, u32[]{:S(2)}, u32[]{:S(2)}) %all-to-all-start.2) | async-done | bytes 65568 | tf_op jit(solution)/shard_map/all_to_all | solution.py:117
  27.3 29.2 %all_to_all.75 = bf16[16,8,256]{2,1,0:T(8,128)(2,1)S(1)} all-to-all(bf16[16,8,256]{2,1,0:T(8,128)(2,1)S(1)} %get-tuple-element.409), channel_id=1, replica_groups=mesh['grp'=16,'seq'=16,'tp'=4] {'grp'}, dimensions={0} | all-to-all | bytes 131072 | tf_op jit(solution)/shard_map/all_to_all | solution.py:134
  56.5 8.5 %all-to-all-start.3 = ((bf16[16,8,256]{2,1,0:T(8,128)(2,1)}), bf16[16,8,256]{2,1,0:T(8,128)(2,1)S(1)}, u32[]{:S(2)}, u32[]{:S(2)}) async-start(bf16[16,8,256]{2,1,0:T(8,128)(2,1)} %get-tuple-element.410), calls=%async_computation.3 | async-start | bytes 131072 | tf_op jit(solution)/shard_map/all_to_all | solution.py:135
  65.2 7.0 %all-to-all-done.3 = bf16[16,8,256]{2,1,0:T(8,128)(2,1)S(1)} async-done(((bf16[16,8,256]{2,1,0:T(8,128)(2,1)}), bf16[16,8,256]{2,1,0:T(8,128)(2,1)S(1)}, u32[]{:S(2)}, u32[]{:S(2)}) %all-to-all-start.3) | async-done | bytes 65568 | tf_op jit(solution)/shard_map/all_to_all | solution.py:135
  73.0 1.9 %copy.67 = bf16[4,4,8,2048]{3,2,0,1:T(8,128)(2,1)} copy(bf16[4,4,8,2048]{3,2,1,0:T(8,128)(2,1)} %bitcast.83) | data formatting | bytes 1048576 | tf_op jit(solution)/shard_map/all_to_all | solution.py:115
  74.9 3.5 %all-to-all-start.4 = ((bf16[32,4,2048]{2,0,1:T(8,128)(2,1)}), bf16[32,4,2048]{2,0,1:T(8,128)(2,1)S(1)}, u32[]{:S(2)}, u32[]{:S(2)}) async-start(bf16[32,4,2048]{2,0,1:T(8,128)(2,1)} %bitcast.68), calls=%async_computation.4 | async-start | bytes 1048576 | tf_op jit(solution)/shard_map/all_to_all | solution.py:115
  78.4 10.2 %all-to-all-done.4 = bf16[32,4,2048]{2,0,1:T(8,128)(2,1)S(1)} async-done(((bf16[32,4,2048]{2,0,1:T(8,128)(2,1)}), bf16[32,4,2048]{2,0,1:T(8,128)(2,1)S(1)}, u32[]{:S(2)}, u32[]{:S(2)}) %all-to-all-start.4) | async-done | bytes 524320 | tf_op jit(solution)/shard_map/all_to_all | solution.py:115
  90.1 8.8 %all-to-all-start.5 = ((bf16[16,8,2048]{2,1,0:T(8,128)(2,1)}), bf16[16,8,2048]{2,1,0:T(8,128)(2,1)S(1)}, u32[]{:S(2)}, u32[]{:S(2)}) async-start(bf16[16,8,2048]{2,1,0:T(8,128)(2,1)} %broadcast_select_fusion), calls=%async_computation.5 | async-start | bytes 1048576 | tf_op jit(solution)/shard_map/all_to_all | solution.py:133
  99.8 15.3 %all-gather.2.cloned.1.call-done = bf16[2048,512]{0,1:T(8,128)(2,1)} async-done(((bf16[128,512]{0,1:T(8,128)(2,1)}), bf16[2048,512]{0,1:T(8,128)(2,1)}) %all-gather.2.cloned.1.call-update) | async-done | bytes 2097168 | tf_op jit(solution)/shard_map/all_gather | solution.py:16
  115.1 1.8 %fusion.18 = (bf16[2048,256]{0,1:T(8,128)(2,1)S(1)}, bf16[2048,256]{0,1:T(8,128)(2,1)S(1)}) fusion(bf16[2048,512]{0,1:T(8,128)(2,1)} %all-gather.2.cloned.1.call-done), kind=kLoop, calls=%fused_computation.46 | loop fusion | bytes 4194304 | tf_op jit(solution)/shard_map/slice | solution.py:18
  116.9 1.1 broadcast_in_dim.80
  118.0 27.9 %while.18 = (s32[]{:T(128)}, f32[2,8,128]{2,1,0:T(8,128)S(1)}, f32[2,8,128]{2,1,0:T(8,128)S(1)}, f32[2,8,128,128]{3,2,1,0:T(8,128)}, s32[]{:T(128)}, /*index=5*/...) while((s32[]{:T(128)}, f32[2,8,128]{2,1,0:T(8,128)S(1)}, ...), condition=%wide.region_9.11_spmd.clone, body=%wide.region_3.10_spmd.clone.sunk | while | flops 551232128 | bytes 26620868 | solution.py:97
  124.4 5.0 %conditional.3 = ((f32[2,8,128]{2,1,0:T(8,128)S(1)}, f32[2,8,128]{2,1,0:T(8,128)S(1)}, f32[2,8,128,128]{3,2,1,0:T(8,128)})) conditional(s32[]{:T(128)} %convert_element_type.50, (f32[2,8,128]{2,1,0:T(8,128)S(1)}, f32[2,8,128]{2,1,0:T(8,128)S(1)}, f32[2,8,128,128]{3,2,1,0:T(8,128)}) %tuple.55, (s32[512]{0:T(512)S(1)}, s32[]{:T(128)}, ...), branch_computations={%region_5.6_spmd, %region_6.9_spmd} | conditional | flops 551227520 | bytes 26613890 | solution.py:79
  126.8 1.7 %fusion.8 = f32[2,8,128,128]{3,2,1,0:T(8,128)S(1)} fusion(bf16[512,2,128,1]{0,2,3,1:T(8,128)(2,1)S(1)} %bitcast.80, f32[2,512,128,8]{2,1,3,0:T(8,128)S(1)} %get-tuple-element.404, f32[2,8,128]{2,1,0:T(8,128)S(1)} %max.5, pred[128,512]{0,1:T(8,128)(4,1)S(1)} %compare_and_fusion, f32[2,8,128,128]{3,2,1,0:T(8,128)S(1)} %copy-done, ...), kind=kOutput, calls=%fused_computation.11 | convolution fusion | flops 274202624 | bytes 6635520 | tf_op jit(solution)/shard_map/while/body/eval_jaxpr/cond/branch_1_fun/krnm,mkd->krnd/dot_general | solution.py:56
  132.7 5.0 %conditional.3 = ((f32[2,8,128]{2,1,0:T(8,128)S(1)}, f32[2,8,128]{2,1,0:T(8,128)S(1)}, f32[2,8,128,128]{3,2,1,0:T(8,128)})) conditional(s32[]{:T(128)} %convert_element_type.50, (f32[2,8,128]{2,1,0:T(8,128)S(1)}, f32[2,8,128]{2,1,0:T(8,128)S(1)}, f32[2,8,128,128]{3,2,1,0:T(8,128)}) %tuple.55, (s32[512]{0:T(512)S(1)}, s32[]{:T(128)}, ...), branch_computations={%region_5.6_spmd, %region_6.9_spmd} | conditional | flops 551227520 | bytes 26613890 | solution.py:79
  135.0 1.7 %fusion.8 = f32[2,8,128,128]{3,2,1,0:T(8,128)S(1)} fusion(bf16[512,2,128,1]{0,2,3,1:T(8,128)(2,1)S(1)} %bitcast.80, f32[2,512,128,8]{2,1,3,0:T(8,128)S(1)} %get-tuple-element.404, f32[2,8,128]{2,1,0:T(8,128)S(1)} %max.5, pred[128,512]{0,1:T(8,128)(4,1)S(1)} %compare_and_fusion, f32[2,8,128,128]{3,2,1,0:T(8,128)S(1)} %copy-done, ...), kind=kOutput, calls=%fused_computation.11 | convolution fusion | flops 274202624 | bytes 6635520 | tf_op jit(solution)/shard_map/while/body/eval_jaxpr/cond/branch_1_fun/krnm,mkd->krnd/dot_general | solution.py:56
  140.9 5.0 %conditional.3 = ((f32[2,8,128]{2,1,0:T(8,128)S(1)}, f32[2,8,128]{2,1,0:T(8,128)S(1)}, f32[2,8,128,128]{3,2,1,0:T(8,128)})) conditional(s32[]{:T(128)} %convert_element_type.50, (f32[2,8,128]{2,1,0:T(8,128)S(1)}, f32[2,8,128]{2,1,0:T(8,128)S(1)}, f32[2,8,128,128]{3,2,1,0:T(8,128)}) %tuple.55, (s32[512]{0:T(512)S(1)}, s32[]{:T(128)}, ...), branch_computations={%region_5.6_spmd, %region_6.9_spmd} | conditional | flops 551227520 | bytes 26613890 | solution.py:79
  143.2 1.7 %fusion.8 = f32[2,8,128,128]{3,2,1,0:T(8,128)S(1)} fusion(bf16[512,2,128,1]{0,2,3,1:T(8,128)(2,1)S(1)} %bitcast.80, f32[2,512,128,8]{2,1,3,0:T(8,128)S(1)} %get-tuple-element.404, f32[2,8,128]{2,1,0:T(8,128)S(1)} %max.5, pred[128,512]{0,1:T(8,128)(4,1)S(1)} %compare_and_fusion, f32[2,8,128,128]{3,2,1,0:T(8,128)S(1)} %copy-done, ...), kind=kOutput, calls=%fused_computation.11 | convolution fusion | flops 274202624 | bytes 6635520 | tf_op jit(solution)/shard_map/while/body/eval_jaxpr/cond/branch_1_fun/krnm,mkd->krnd/dot_general | solution.py:56
  145.9 1.6 %fusion.16 = bf16[128,2,8,128]{3,0,2,1:T(8,128)(2,1)S(1)} fusion(f32[2,8,128,128]{3,2,1,0:T(8,128)} %get-tuple-element.342, f32[2,8,128]{2,1,0:T(8,128)S(1)} %get-tuple-element.343), kind=kLoop, calls=%fused_computation.28 | loop fusion | flops 524288 | bytes 1581056 | tf_op jit(solution)/shard_map/convert_element_type | solution.py:110
  (88 shorter events, 22.1 us)
Async XLA Ops:
  6.5 93.0 %copy-start.2 = (s32[1,4]{1,0:T(1,128)S(1)}, s32[1,4]{1,0:T(1,128)}, u32[]{:S(2)}) copy-start(s32[1,4]{1,0:T(1,128)} %param.14) | copy-start | bytes 52
  8.0 9.0 %all-to-all-start = ((bf16[32,4,256]{2,0,1:T(8,128)(2,1)}), bf16[32,4,256]{2,0,1:T(8,128)(2,1)S(1)}, u32[]{:S(2)}, u32[]{:S(2)}) async-start(bf16[32,4,256]{2,0,1:T(8,128)(2,1)} %bitcast.70), calls=%async_computation | async-start | bytes 131072 | tf_op jit(solution)/shard_map/all_to_all | solution.py:116
  17.0 9.0 %all-to-all-start.2 = ((bf16[32,4,256]{2,0,1:T(8,128)(2,1)}), bf16[32,4,256]{2,0,1:T(8,128)(2,1)S(1)}, u32[]{:S(2)}, u32[]{:S(2)}) async-start(bf16[32,4,256]{2,0,1:T(8,128)(2,1)} %bitcast.69), calls=%async_computation.2 | async-start | bytes 131072 | tf_op jit(solution)/shard_map/all_to_all | solution.py:117
  56.5 15.7 %all-to-all-start.3 = ((bf16[16,8,256]{2,1,0:T(8,128)(2,1)}), bf16[16,8,256]{2,1,0:T(8,128)(2,1)S(1)}, u32[]{:S(2)}, u32[]{:S(2)}) async-start(bf16[16,8,256]{2,1,0:T(8,128)(2,1)} %get-tuple-element.410), calls=%async_computation.3 | async-start | bytes 131072 | tf_op jit(solution)/shard_map/all_to_all | solution.py:135
  65.0 50.1 %all-gather.2.cloned.1.call-start = ((), (), s32[]{:S(2)}) async-start(), calls=%async_computation.6 | async-start | bytes 2228224 | tf_op jit(solution)/shard_map/all_gather | solution.py:16
  74.9 13.7 %all-to-all-start.4 = ((bf16[32,4,2048]{2,0,1:T(8,128)(2,1)}), bf16[32,4,2048]{2,0,1:T(8,128)(2,1)S(1)}, u32[]{:S(2)}, u32[]{:S(2)}) async-start(bf16[32,4,2048]{2,0,1:T(8,128)(2,1)} %bitcast.68), calls=%async_computation.4 | async-start | bytes 1048576 | tf_op jit(solution)/shard_map/all_to_all | solution.py:115
  90.1 26.8 %all-to-all-start.5 = ((bf16[16,8,2048]{2,1,0:T(8,128)(2,1)}), bf16[16,8,2048]{2,1,0:T(8,128)(2,1)S(1)}, u32[]{:S(2)}, u32[]{:S(2)}) async-start(bf16[16,8,2048]{2,1,0:T(8,128)(2,1)} %broadcast_select_fusion), calls=%async_computation.5 | async-start | bytes 1048576 | tf_op jit(solution)/shard_map/all_to_all | solution.py:133
  124.9 1.9 %copy-start = (f32[2,8,128,128]{3,2,1,0:T(8,128)S(1)}, f32[2,8,128,128]{3,2,1,0:T(8,128)}, u32[]{:S(2)}) copy-start(f32[2,8,128,128]{3,2,1,0:T(8,128)} %get-tuple-element.322) | copy-start | bytes 3145732 | tf_op jit(solution)/shard_map/while/body/eval_jaxpr/cond
  128.5 1.0 copy-start.1
  133.1 1.9 %copy-start = (f32[2,8,128,128]{3,2,1,0:T(8,128)S(1)}, f32[2,8,128,128]{3,2,1,0:T(8,128)}, u32[]{:S(2)}) copy-start(f32[2,8,128,128]{3,2,1,0:T(8,128)} %get-tuple-element.322) | copy-start | bytes 3145732 | tf_op jit(solution)/shard_map/while/body/eval_jaxpr/cond
  136.7 1.0 copy-start.1
  141.3 1.9 %copy-start = (f32[2,8,128,128]{3,2,1,0:T(8,128)S(1)}, f32[2,8,128,128]{3,2,1,0:T(8,128)}, u32[]{:S(2)}) copy-start(f32[2,8,128,128]{3,2,1,0:T(8,128)} %get-tuple-element.322) | copy-start | bytes 3145732 | tf_op jit(solution)/shard_map/while/body/eval_jaxpr/cond
  144.9 1.0 copy-start.1
Sparse Core Ops, SparseCore 0:
  73.1 41.9 all-gather.1
where the time goes:
time: 157 us; the launch traced here: 156 us
  waiting for transfers between devices  41.2 us (26%)
  blocking collectives  29.2 us (19%)
  starting transfers between devices  27.3 us (17%)
  local copies, waits for them, and re-layouts  19.7 us (13%)
  between operations  13.5 us (9%)
  other arithmetic  8.95 us (6%)
  loops' own time  7.92 us (5%)
  matrix products  7.7 us (5%)
    all_to_all x1, blocking collectives, shards(): lax.all_to_all(arrange(key_split_rows), 'grp', split_axis=0, concat_axis=...  29.2 us
    all_gather x1, waiting for transfers between devices, in_one_piece(): out, at, done = (lax.all_gather(both, axis, axis=dim, tiled=True), 0, [])  15.3 us
    all_to_all x1, waiting for transfers between devices, shards(): lax.all_to_all(queries, 'tp', split_axis=1, concat_axis=0, tiled=True)  10.2 us
    all_to_all x1, starting transfers between devices, shards(): lax.all_to_all(arrange(query_heads), 'grp', split_axis=0, concat_axis=0,...  8.77 us
    all_to_all x1, starting transfers between devices, shards(): lax.all_to_all(arrange(value_split_rows), 'grp', split_axis=0, concat_axi...  8.49 us
    another operation x1, loops' own time, sweep_keys(): return lax.fori_loop(0, key_total // step_rows, visit, carried)  7.57 us
    all_to_all x1, waiting for transfers between devices, shards(): lax.all_to_all(arrange(value_split_rows), 'grp', split_axis=0, concat_axi...  7.03 us
    all_to_all x1, waiting for transfers between devices, shards(): lax.all_to_all(value_rows, 'tp', split_axis=1, concat_axis=0, tiled=True)  5.13 us
  transfers between devices with their start and end apart: 6, of which 5 were waited for; matrix products, arithmetic and copies ran while one was open for 6% of the time, Pallas kernels for 0%

commit v1 on v0

v1 whole, which is shorter than its diff:
```python
import math

import jax
import jax.numpy as jnp
from jax import lax
from jax.experimental import pallas as pl
from jax.experimental.pallas import tpu as pltpu
from jax.sharding import PartitionSpec as P

HD = 128
HIDDEN = -1e30
CHUNK_HEADS = 4


def attend(scalars, q, own, sib, out, keys, values, bias):
    rows = q.shape[0]
    own_rows, sib_rows = own.shape[0], sib.shape[0]
    kv_heads = own.shape[1] // (2 * HD)
    ratio = q.shape[1] // (HD * kv_heads)
    shard = scalars[0]
    position = shard * rows + lax.broadcasted_iota(jnp.int32, (rows, HD), 0)
    start = jnp.zeros((rows, HD), jnp.int32)
    for j in range(3):
        start = jnp.maximum(start, jnp.where(position >= scalars[1 + j], scalars[1 + j], 0))
    lane = lax.broadcasted_iota(jnp.int32, (rows, HD), 1)
    own_blocks = own_rows // rows
    for b in range((own_rows + sib_rows) // rows):
        back = 2 * b if b < own_blocks else 2 * (b - own_blocks) + 1
        for part in range(rows // HD):
            key = (shard - back) * rows + part * HD + lane
            seen = (key >= start) & (key <= position)
            at = b * rows + part * HD
            bias[:, at : at + HD] = jnp.where(seen, 0.0, HIDDEN)
    factor = math.log2(math.e) / math.sqrt(HD)
    total = own_rows + sib_rows
    values[:, HD:] = jnp.ones((total, HD), jnp.bfloat16)
    for kv in range(kv_heads):
        keys[0:own_rows, :] = own[:, kv * HD : (kv + 1) * HD]
        keys[own_rows:, :] = sib[:, kv * HD : (kv + 1) * HD]
        at = (kv_heads + kv) * HD
        values[0:own_rows, :HD] = own[:, at : at + HD]
        values[own_rows:, :HD] = sib[:, at : at + HD]
        for first in range(0, ratio, CHUNK_HEADS):
            heads = range(kv * ratio + first, kv * ratio + first + CHUNK_HEADS)
            stack = jnp.concatenate([q[:, h * HD : (h + 1) * HD] for h in heads], axis=0)
            scores = lax.dot_general(
                stack, keys[...], (((1,), (1,)), ((), ())), preferred_element_type=jnp.float32
            )
            scores = scores.reshape(CHUNK_HEADS, rows, total) + bias[...][None]
            peak = jnp.max(scores, axis=2, keepdims=True)
            weights = jnp.exp2((scores - peak) * factor).astype(jnp.bfloat16)
            both = jnp.dot(
                weights.reshape(CHUNK_HEADS * rows, total),
                values[...],
                preferred_element_type=jnp.float32,
            )
            normal = (both[:, :HD] / both[:, HD:]).astype(jnp.bfloat16)
            for i, h in enumerate(heads):
                out[:, h * HD : (h + 1) * HD] = normal[i * rows : (i + 1) * rows, :]


def attention(scalars, q, own, sib):
    rows, total = q.shape[0], own.shape[0] + sib.shape[0]
    vmem = pl.BlockSpec(memory_space=pltpu.VMEM)
    return pl.pallas_call(
        attend,
        out_shape=jax.ShapeDtypeStruct(q.shape, jnp.bfloat16),
        in_specs=[pl.BlockSpec(memory_space=pltpu.SMEM), vmem, vmem, vmem],
        out_specs=vmem,
        scratch_shapes=[
            pltpu.VMEM((total, HD), jnp.bfloat16),
            pltpu.VMEM((total, 2 * HD), jnp.bfloat16),
            pltpu.VMEM((rows, total), jnp.float32),
        ],
        compiler_params=pltpu.CompilerParams(vmem_limit_bytes=40 << 20),
        cost_estimate=pl.CostEstimate(
            flops=4 * q.shape[1] * rows * total,
            bytes_accessed=2 * (2 * q.size + own.size + sib.size),
            transcendentals=q.shape[1] // HD * rows * total,
        ),
    )(scalars, q, own, sib)


def shards(queries, key_rows, value_rows, image_lengths, block_table):
    tp, groups, seq = lax.axis_size("tp"), lax.axis_size("grp"), lax.axis_size("seq")
    part = queries.shape[0]
    packed = jnp.stack(
        [
            jnp.concatenate(
                [
                    lax.slice_in_dim(a, t * a.shape[1] // tp, (t + 1) * a.shape[1] // tp, axis=1)
                    for a in (queries, key_rows, value_rows)
                ],
                axis=1,
            )
            for t in range(tp)
        ]
    )
    rows = part * tp
    held = lax.all_to_all(packed, "tp", 0, 0, tiled=True).reshape(rows, packed.shape[2])
    block = rows // groups
    destination = jnp.broadcast_to(block_table[0][:, None], (groups, block)).reshape(rows)
    row = lax.broadcasted_iota(jnp.int32, (rows, rows), 0)
    col = lax.broadcasted_iota(jnp.int32, (rows, rows), 1)
    order = (destination[None, :] == row // block) & (row % block == col % block)
    order = order.astype(jnp.bfloat16)
    q_width = queries.shape[1] // tp
    kv_sorted = jnp.dot(order, held[:, q_width:], preferred_element_type=jnp.float32).astype(jnp.bfloat16)
    q_sorted = jnp.dot(order, held[:, :q_width], preferred_element_type=jnp.float32).astype(jnp.bfloat16)
    kv = lax.all_to_all(kv_sorted.reshape(groups, block, -1), "grp", 0, 0, tiled=True).reshape(rows, -1)
    q = lax.all_to_all(q_sorted.reshape(groups, block, -1), "grp", 0, 0, tiled=True).reshape(rows, -1)

    def ahead(x, chips):
        return lax.ppermute(x, "seq", [(i, i + 2 * chips) for i in range(seq - 2 * chips)])

    back4 = ahead(kv, 4)
    back1 = ahead(kv, 1)
    back23 = ahead(jnp.concatenate([kv, back1], axis=0), 2)
    own = jnp.concatenate([kv, back1, back23, back4], axis=0)
    shard = lax.axis_index("seq")
    given = lax.dynamic_slice_in_dim(own, lax.rem(shard, 2) * rows, 4 * rows, 0)
    sib = lax.ppermute(given, "seq", [(i, i ^ 1) for i in range(seq)])
    lengths = image_lengths[0]
    first = lengths[0]
    second = first + lengths[1]
    third = second + lengths[2]
    scalars = jnp.stack([shard.astype(jnp.int32), first, second, third])
    return attention(scalars, q, own, sib)


def solution(mesh):
    in_specs = (
        P(("grp", "seq", "tp"), None),
        P(("grp", "seq", "tp"), None),
        P(("grp", "seq", "tp"), None),
        P("grp", None),
        P(("grp", "seq"), None),
    )
    out_specs = P(("grp", "seq"), "tp")
    return jax.shard_map(shards, mesh=mesh, in_specs=in_specs, out_specs=out_specs, check_vma=False)
```

time: 157 us -> 101 us (0.64)
  the two profiles are of different devices: /device:TPU:120 before, /device:TPU:97 now
where the time goes in v1:
time: 101 us; the launch traced here: 100 us
  waiting for transfers between devices  34.5 us (34%)
  blocking collectives  31.9 us (32%)
  starting transfers between devices  19.4 us (19%)
  Pallas kernels  5.35 us (5%)
  local copies, waits for them, and re-layouts  3.51 us (3%)
  between operations  2.09 us (2%)
  other arithmetic  1.82 us (2%)
  matrix products  1.47 us (1%)
    all_to_all x1, blocking collectives, shards(): lax.all_to_all(kv_sorted.reshape(groups, block, -1), 'grp', 0, 0, tiled=T...  31.9 us
    ppermute x3, waiting for transfers between devices, ahead(): lax.ppermute(x, 'seq', [(i, i + 2 * chips) for i in range(seq - 2 * chips)])  17.9 us
    all_to_all x1, waiting for transfers between devices, shards(): lax.all_to_all(packed, 'tp', 0, 0, tiled=True)  16.6 us
    ppermute x1, starting transfers between devices, shards(): sib = lax.ppermute(given, 'seq', [(i, i ^ 1) for i in range(seq)])  6.37 us
    pallas_call x1, Pallas kernels, attention(): pl.pallas_call(attend, out_shape=jax.ShapeDtypeStruct(q.shape, jnp.bfloat...  5.35 us
    ppermute x3, starting transfers between devices, ahead(): lax.ppermute(x, 'seq', [(i, i + 2 * chips) for i in range(seq - 2 * chips)])  4.99 us
    all_to_all x1, starting transfers between devices, shards(): lax.all_to_all(packed, 'tp', 0, 0, tiled=True)  4.47 us
    all_to_all x1, starting transfers between devices, shards(): lax.all_to_all(q_sorted.reshape(groups, block, -1), 'grp', 0, 0, tiled=True)  3.57 us
  transfers between devices with their start and end apart: 6, of which 3 were waited for; matrix products, arithmetic and copies ran while one was open for 3% of the time, Pallas kernels for 0%

profile of v1, /device:TPU:97, one launch (start us, length us, event | category | flops | bytes accessed | tf_op | source)
XLA Modules:
  0.0 100.1 jit_solution(18093010898520639194)
XLA Ops:
  0.0 0.8 fusion.8
  0.8 0.8 fusion.9
  1.5 1.1 %fusion.7 = (bf16[32,2048]{1,0:T(8,128)(2,1)S(1)}, bf16[32,2048]{1,0:T(8,128)(2,1)S(1)}, bf16[32,2048]{1,0:T(8,128)(2,1)S(1)}, bf16[32,2048]{1,0:T(8,128)(2,1)S(1)}) fusion(bf16[32,8192]{1,0:T(8,128)(2,1)} %param.5), kind=kLoop, calls=%fused_computation.25 | loop fusion | bytes 1048576 | tf_op jit(solution)/shard_map/slice | solution.py:91
  2.7 0.9 pad_maximum_fusion
  3.7 4.5 %all-to-all-start = ((bf16[4,32,2560]{2,1,0:T(8,128)(2,1)}), bf16[4,32,2560]{2,1,0:T(8,128)(2,1)S(1)}, u32[]{:S(2)}, u32[]{:S(2)}) async-start(bf16[4,32,2560]{2,1,0:T(8,128)(2,1)} %pad_maximum_fusion), calls=%async_computation | async-start | bytes 1310720 | tf_op jit(solution)/shard_map/all_to_all | solution.py:100
  8.1 0.1 broadcast_in_dim.8
  8.2 0.1 eq.16
  8.3 16.6 %all-to-all-done = bf16[4,32,2560]{2,1,0:T(8,128)(2,1)S(1)} async-done(((bf16[4,32,2560]{2,1,0:T(8,128)(2,1)}), bf16[4,32,2560]{2,1,0:T(8,128)(2,1)S(1)}, u32[]{:S(2)}, u32[]{:S(2)}) %all-to-all-start) | async-done | bytes 655392 | tf_op jit(solution)/shard_map/all_to_all | solution.py:100
  24.9 0.3 fusion.1
  25.2 31.9 %all_to_all.15 = bf16[16,8,512]{2,1,0:T(8,128)(2,1)S(1)} all-to-all(bf16[16,8,512]{2,1,0:T(8,128)(2,1)S(1)} %fusion.1), channel_id=1, replica_groups=mesh['grp'=16,'seq'=16,'tp'=4] {'grp'}, dimensions={0} | all-to-all | bytes 262144 | tf_op jit(solution)/shard_map/all_to_all | solution.py:110
  57.2 2.4 %collective-permute-start = (bf16[128,512]{1,0:T(8,128)(2,1)S(1)}, bf16[128,512]{1,0:T(8,128)(2,1)S(1)}, u32[]{:S(2)}, u32[]{:S(2)}) collective-permute-start(bf16[128,512]{1,0:T(8,128)(2,1)S(1)} %bitcast.23), channel_id=1, source_target_pairs={{0,8},{4,12},{8,16},{12,20},{16,24},{20,28},{24,32},{28,36},{32,40... | collective-permute-start | bytes 393224 | tf_op jit(solution)/shard_map/ppermute | solution.py:114
  59.6 3.3 %collective-permute-done = bf16[128,512]{1,0:T(8,128)(2,1)S(1)} collective-permute-done((bf16[128,512]{1,0:T(8,128)(2,1)S(1)}, bf16[128,512]{1,0:T(8,128)(2,1)S(1)}, u32[]{:S(2)}, u32[]{:S(2)}) %collective-permute-start) | collective-permute-done | bytes 131104 | tf_op jit(solution)/shard_map/ppermute | solution.py:114
  62.9 1.3 %collective-permute-start.1 = (bf16[256,512]{1,0:T(8,128)(2,1)S(1)}, bf16[256,512]{1,0:T(8,128)(2,1)S(1)}, u32[]{:S(2)}, u32[]{:S(2)}) collective-permute-start(bf16[256,512]{1,0:T(8,128)(2,1)S(1)} %pad_maximum_fusion.2), channel_id=1, source_target_pairs={{0,16},{4,20},{8,24},{12,28},{16,32},{20,36},{24,40},{28,44},{32,4... | collective-permute-start | bytes 786440 | tf_op jit(solution)/shard_map/ppermute | solution.py:114
  64.2 1.2 %fusion = bf16[16,8,2048]{2,1,0:T(8,128)(2,1)} fusion(bf16[128,2560]{1,0:T(8,128)(2,1)S(1)} %bitcast.22, s32[128]{0:T(128)S(1)} %get-tuple-element.27, s32[128]{0:T(128)S(1)} %get-tuple-element.28, s32[128]{0:T(128)S(1)} %get-tuple-element.26, s32[128]{0:T(128)S(1)} %get-tuple-element.29, s32[128]{0:T(128)S(1)} %eq.16, ...), kind=kOutput, calls=%fused_computation.1 | convolution fusion | flops 67469312 | bytes 1053696 | tf_op jit(solution)/shard_map/dot_general | solution.py:109
  65.4 3.6 %all-to-all-start.1 = ((bf16[16,8,2048]{2,1,0:T(8,128)(2,1)}), bf16[16,8,2048]{2,1,0:T(8,128)(2,1)S(1)}, u32[]{:S(2)}, u32[]{:S(2)}) async-start(bf16[16,8,2048]{2,1,0:T(8,128)(2,1)} %fusion), calls=%async_computation.1 | async-start | bytes 1048576 | tf_op jit(solution)/shard_map/all_to_all | solution.py:111
  69.0 1.3 %collective-permute-start.2 = (bf16[128,512]{1,0:T(8,128)(2,1)S(1)}, bf16[128,512]{1,0:T(8,128)(2,1)S(1)}, u32[]{:S(2)}, u32[]{:S(2)}) collective-permute-start(bf16[128,512]{1,0:T(8,128)(2,1)S(1)} %bitcast.25), channel_id=1, source_target_pairs={{0,32},{4,36},{8,40},{12,44},{16,48},{20,52},{24,56},{28,60},{1,33... | collective-permute-start | bytes 393224 | tf_op jit(solution)/shard_map/ppermute | solution.py:114
  70.3 14.6 %collective-permute-done.2 = bf16[128,512]{1,0:T(8,128)(2,1)S(1)} collective-permute-done((bf16[128,512]{1,0:T(8,128)(2,1)S(1)}, bf16[128,512]{1,0:T(8,128)(2,1)S(1)}, u32[]{:S(2)}, u32[]{:S(2)}) %collective-permute-start.2) | collective-permute-done | bytes 131104 | tf_op jit(solution)/shard_map/ppermute | solution.py:114
  84.9 0.0 copy-start
  85.0 6.4 %collective-permute-start.3 = (bf16[512,512]{1,0:T(8,128)(2,1)S(1)}, bf16[512,512]{1,0:T(8,128)(2,1)S(1)}, u32[]{:S(2)}, u32[]{:S(2)}) collective-permute-start(bf16[512,512]{1,0:T(8,128)(2,1)S(1)} %constant_dynamic-slice_fusion), channel_id=1, source_target_pairs={{0,4},{4,0},{8,12},{12,8},{16,20},{20,16},{24,28},{28,24},{32,36},... | collective-permute-start | bytes 1572872 | tf_op jit(solution)/shard_map/ppermute | solution.py:122
  91.4 0.6 fusion.10
  93.9 0.8 pad_add_fusion.scalars
  94.7 0.0 all-to-all-done.1
  94.7 0.0 collective-permute-done.3.sib
  94.7 5.3 %shard_map.55 = bf16[128,2048]{1,0:T(8,128)(2,1)} custom-call(s32[4]{0:T(128)S(1)} %pad_add_fusion.scalars, bf16[128,2048]{1,0:T(8,128)(2,1)S(1)} %bitcast.20, bf16[640,512]{1,0:T(8,128)(2,1)S(1)} %pad_maximum_fusion.1.own, bf16[512,512]{1,0:T(8,128)(2,1)S(1)} %collective-permute-done.3.sib), custom_call_target="tpu_custom_call" | custom-call | flops 1207959552 | bytes 2228224 | tf_op jit(solution)/shard_map/pallas_call | solution.py:65
  (12 shorter events, 0.2 us)
Async XLA Ops:
  3.7 4.5 %copy-start.1 = (s32[1,16]{1,0:T(1,128)S(1)}, s32[1,16]{1,0:T(1,128)}, u32[]{:S(2)}) copy-start(s32[1,16]{1,0:T(1,128)} %param.9) | copy-start | bytes 196
  3.7 21.3 %all-to-all-start = ((bf16[4,32,2560]{2,1,0:T(8,128)(2,1)}), bf16[4,32,2560]{2,1,0:T(8,128)(2,1)S(1)}, u32[]{:S(2)}, u32[]{:S(2)}) async-start(bf16[4,32,2560]{2,1,0:T(8,128)(2,1)} %pad_maximum_fusion), calls=%async_computation | async-start | bytes 1310720 | tf_op jit(solution)/shard_map/all_to_all | solution.py:100
  57.2 5.7 %collective-permute-start = (bf16[128,512]{1,0:T(8,128)(2,1)S(1)}, bf16[128,512]{1,0:T(8,128)(2,1)S(1)}, u32[]{:S(2)}, u32[]{:S(2)}) collective-permute-start(bf16[128,512]{1,0:T(8,128)(2,1)S(1)} %bitcast.23), channel_id=1, source_target_pairs={{0,8},{4,12},{8,16},{12,20},{16,24},{20,28},{24,32},{28,36},{32,40... | collective-permute-start | bytes 393224 | tf_op jit(solution)/shard_map/ppermute | solution.py:114
  62.9 22.0 %collective-permute-start.1 = (bf16[256,512]{1,0:T(8,128)(2,1)S(1)}, bf16[256,512]{1,0:T(8,128)(2,1)S(1)}, u32[]{:S(2)}, u32[]{:S(2)}) collective-permute-start(bf16[256,512]{1,0:T(8,128)(2,1)S(1)} %pad_maximum_fusion.2), channel_id=1, source_target_pairs={{0,16},{4,20},{8,24},{12,28},{16,32},{20,36},{24,40},{28,44},{32,4... | collective-permute-start | bytes 786440 | tf_op jit(solution)/shard_map/ppermute | solution.py:114
  65.4 29.3 %all-to-all-start.1 = ((bf16[16,8,2048]{2,1,0:T(8,128)(2,1)}), bf16[16,8,2048]{2,1,0:T(8,128)(2,1)S(1)}, u32[]{:S(2)}, u32[]{:S(2)}) async-start(bf16[16,8,2048]{2,1,0:T(8,128)(2,1)} %fusion), calls=%async_computation.1 | async-start | bytes 1048576 | tf_op jit(solution)/shard_map/all_to_all | solution.py:111
  69.0 15.9 %collective-permute-start.2 = (bf16[128,512]{1,0:T(8,128)(2,1)S(1)}, bf16[128,512]{1,0:T(8,128)(2,1)S(1)}, u32[]{:S(2)}, u32[]{:S(2)}) collective-permute-start(bf16[128,512]{1,0:T(8,128)(2,1)S(1)} %bitcast.25), channel_id=1, source_target_pairs={{0,32},{4,36},{8,40},{12,44},{16,48},{20,52},{24,56},{28,60},{1,33... | collective-permute-start | bytes 393224 | tf_op jit(solution)/shard_map/ppermute | solution.py:114
  84.9 6.4 %copy-start = (s32[1,4]{1,0:T(1,128)S(1)}, s32[1,4]{1,0:T(1,128)}, u32[]{:S(2)}) copy-start(s32[1,4]{1,0:T(1,128)} %param.8) | copy-start | bytes 52
  85.0 9.7 %collective-permute-start.3 = (bf16[512,512]{1,0:T(8,128)(2,1)S(1)}, bf16[512,512]{1,0:T(8,128)(2,1)S(1)}, u32[]{:S(2)}, u32[]{:S(2)}) collective-permute-start(bf16[512,512]{1,0:T(8,128)(2,1)S(1)} %constant_dynamic-slice_fusion), channel_id=1, source_target_pairs={{0,4},{4,0},{8,12},{12,8},{16,20},{20,16},{24,28},{28,24},{32,36},... | collective-permute-start | bytes 1572872 | tf_op jit(solution)/shard_map/ppermute | solution.py:122

commit v2 on v1

--- a/solution.py
+++ b/solution.py
@@ -12,16 +12,18 @@
 CHUNK_HEADS = 4
 
 
-def attend(scalars, q, own, sib, out, keys, values, bias):
+def attend(lengths, q, own, sib, out, keys, values, bias):
     rows = q.shape[0]
     own_rows, sib_rows = own.shape[0], sib.shape[0]
     kv_heads = own.shape[1] // (2 * HD)
     ratio = q.shape[1] // (HD * kv_heads)
-    shard = scalars[0]
+    shard = lax.axis_index("seq")
     position = shard * rows + lax.broadcasted_iota(jnp.int32, (rows, HD), 0)
     start = jnp.zeros((rows, HD), jnp.int32)
-    for j in range(3):
-        start = jnp.maximum(start, jnp.where(position >= scalars[1 + j], scalars[1 + j], 0))
+    bound = 0
+    for j in range(lengths.shape[1] - 1):
+        bound = bound + lengths[0, j]
+        start = jnp.where(position >= bound, bound, start)
     lane = lax.broadcasted_iota(jnp.int32, (rows, HD), 1)
     own_blocks = own_rows // rows
     for b in range((own_rows + sib_rows) // rows):
@@ -59,7 +61,7 @@
                 out[:, h * HD : (h + 1) * HD] = normal[i * rows : (i + 1) * rows, :]
 
 
-def attention(scalars, q, own, sib):
+def attention(lengths, q, own, sib):
     rows, total = q.shape[0], own.shape[0] + sib.shape[0]
     vmem = pl.BlockSpec(memory_space=pltpu.VMEM)
     return pl.pallas_call(
@@ -78,54 +80,73 @@
             bytes_accessed=2 * (2 * q.size + own.size + sib.size),
             transcendentals=q.shape[1] // HD * rows * total,
         ),
-    )(scalars, q, own, sib)
+    )(lengths, q, own, sib)
+
+
+def pack(arrays, parts):
+    widths = [a.shape[1] // parts for a in arrays]
+
+    def kernel(*refs):
+        out = refs[-1]
+        for t in range(parts):
+            at = 0
+            for a, width in zip(refs, widths):
+                out[t, :, at : at + width] = a[:, t * width : (t + 1) * width]
+                at += width
+
+    return pl.pallas_call(
+        kernel,
+        out_shape=jax.ShapeDtypeStruct((parts, arrays[0].shape[0], sum(widths)), arrays[0].dtype),
+        in_specs=[pl.BlockSpec(memory_space=pltpu.VMEM)] * len(arrays),
+        out_specs=pl.BlockSpec(memory_space=pltpu.VMEM),
+    )(*arrays)
 
 
 def shards(queries, key_rows, value_rows, image_lengths, block_table):
     tp, groups, seq = lax.axis_size("tp"), lax.axis_size("grp"), lax.axis_size("seq")
+    me = lax.axis_index("tp")
     part = queries.shape[0]
-    packed = jnp.stack(
-        [
-            jnp.concatenate(
-                [
-                    lax.slice_in_dim(a, t * a.shape[1] // tp, (t + 1) * a.shape[1] // tp, axis=1)
-                    for a in (queries, key_rows, value_rows)
-                ],
-                axis=1,
-            )
-            for t in range(tp)
-        ]
-    )
     rows = part * tp
-    held = lax.all_to_all(packed, "tp", 0, 0, tiled=True).reshape(rows, packed.shape[2])
     block = rows // groups
-    destination = jnp.broadcast_to(block_table[0][:, None], (groups, block)).reshape(rows)
-    row = lax.broadcasted_iota(jnp.int32, (rows, rows), 0)
-    col = lax.broadcasted_iota(jnp.int32, (rows, rows), 1)
-    order = (destination[None, :] == row // block) & (row % block == col % block)
-    order = order.astype(jnp.bfloat16)
+    blocks = part // block
+    packed = pack((key_rows, value_rows), tp)
+    held_kv = lax.all_to_all(packed, "tp", 0, 0, tiled=True).reshape(rows, -1)
     q_width = queries.shape[1] // tp
-    kv_sorted = jnp.dot(order, held[:, q_width:], preferred_element_type=jnp.float32).astype(jnp.bfloat16)
-    q_sorted = jnp.dot(order, held[:, :q_width], preferred_element_type=jnp.float32).astype(jnp.bfloat16)
-    kv = lax.all_to_all(kv_sorted.reshape(groups, block, -1), "grp", 0, 0, tiled=True).reshape(rows, -1)
-    q = lax.all_to_all(q_sorted.reshape(groups, block, -1), "grp", 0, 0, tiled=True).reshape(rows, -1)
+    pieces, arrived = [], []
+    for d in range(tp):
+        other = me ^ d
+        piece = lax.dynamic_slice_in_dim(queries, other * q_width, q_width, axis=1)
+        if d:
+            piece = lax.ppermute(piece, "tp", [(i, i ^ d) for i in range(tp)])
+        pieces.append(piece)
+        arrived.append(lax.dynamic_slice_in_dim(block_table[0], other * blocks, blocks))
+    held_q = jnp.concatenate(pieces, axis=0)
+
+    def order(destination):
+        wide = jnp.broadcast_to(destination[:, None], (groups, block)).reshape(rows)
+        row = lax.broadcasted_iota(jnp.int32, (rows, rows), 0)
+        col = lax.broadcasted_iota(jnp.int32, (rows, rows), 1)
+        return ((wide[None, :] == row // block) & (row % block == col % block)).astype(jnp.bfloat16)
+
+    def sort(matrix, rows_held):
+        out = jnp.dot(matrix, rows_held, preferred_element_type=jnp.float32).astype(jnp.bfloat16)
+        return out.reshape(groups, block, -1)
+
+    kv_sorted = sort(order(block_table[0]), held_kv)
+    q_sorted = sort(order(jnp.concatenate(arrived)), held_q)
+    kv = lax.all_to_all(kv_sorted, "grp", 0, 0, tiled=True).reshape(rows, -1)
+    kv, q_sorted = lax.optimization_barrier((kv, q_sorted))
+    q = lax.all_to_all(q_sorted, "grp", 0, 0, tiled=True).reshape(rows, -1)
 
     def ahead(x, chips):
         return lax.ppermute(x, "seq", [(i, i + 2 * chips) for i in range(seq - 2 * chips)])
 
-    back4 = ahead(kv, 4)
-    back1 = ahead(kv, 1)
-    back23 = ahead(jnp.concatenate([kv, back1], axis=0), 2)
-    own = jnp.concatenate([kv, back1, back23, back4], axis=0)
+    back1, back2, back4 = ahead(kv, 1), ahead(kv, 2), ahead(kv, 4)
+    own = jnp.concatenate([kv, back1, back2, ahead(back1, 2), back4], axis=0)
     shard = lax.axis_index("seq")
     given = lax.dynamic_slice_in_dim(own, lax.rem(shard, 2) * rows, 4 * rows, 0)
     sib = lax.ppermute(given, "seq", [(i, i ^ 1) for i in range(seq)])
-    lengths = image_lengths[0]
-    first = lengths[0]
-    second = first + lengths[1]
-    third = second + lengths[2]
-    scalars = jnp.stack([shard.astype(jnp.int32), first, second, third])
-    return attention(scalars, q, own, sib)
+    return attention(image_lengths, q, own, sib)
 
 
 def solution(mesh):

time: 101 us -> 92.9 us (0.920)
  the two profiles are of different devices: /device:TPU:97 before, /device:TPU:4 now
where the time goes in v2:
time: 92.9 us; the launch traced here: 92.3 us
  starting transfers between devices  55.7 us (60%)
  waiting for transfers between devices  26 us (28%)
  Pallas kernels  6.94 us (7%)
  matrix products  2.12 us (2%)
  local copies, waits for them, and re-layouts  1.2 us (1%)
    all_to_all x1, starting transfers between devices, shards(): held_kv = lax.all_to_all(packed, 'tp', 0, 0, tiled=True).reshape(rows, -1)  16.5 us
    ppermute x4, starting transfers between devices, ahead(): lax.ppermute(x, 'seq', [(i, i + 2 * chips) for i in range(seq - 2 * chips)])  15.1 us
    all_to_all x1, waiting for transfers between devices, shards(): kv = lax.all_to_all(kv_sorted, 'grp', 0, 0, tiled=True).reshape(rows, -1)  11.2 us
    all_to_all x1, waiting for transfers between devices, shards(): q = lax.all_to_all(q_sorted, 'grp', 0, 0, tiled=True).reshape(rows, -1)  10.5 us
    ppermute x3, starting transfers between devices, shards(): piece = lax.ppermute(piece, 'tp', [(i, i ^ d) for i in range(tp)])  9.56 us
    all_to_all x1, starting transfers between devices, shards(): kv = lax.all_to_all(kv_sorted, 'grp', 0, 0, tiled=True).reshape(rows, -1)  9.06 us
    pallas_call x1, Pallas kernels, attention(): pl.pallas_call(attend, out_shape=jax.ShapeDtypeStruct(q.shape, jnp.bfloat...  5.34 us
    all_to_all x1, starting transfers between devices, shards(): q = lax.all_to_all(q_sorted, 'grp', 0, 0, tiled=True).reshape(rows, -1)  3.59 us
  transfers between devices with their start and end apart: 11, of which 4 were waited for; matrix products, arithmetic and copies ran while one was open for 3% of the time, Pallas kernels for 0%

profile of v2, /device:TPU:4, one launch (start us, length us, event | category | flops | bytes accessed | tf_op | source)
XLA Modules:
  0.0 92.3 jit_solution(2763473807015892293)
XLA Ops:
  0.0 1.6 %shard_map.55 = bf16[4,32,512]{2,1,0:T(8,128)(2,1)} custom-call(bf16[32,1024]{1,0:T(8,128)(2,1)} %refs_0_.1, bf16[32,1024]{1,0:T(8,128)(2,1)} %refs_1_.1), custom_call_target="tpu_custom_call" | custom-call | tf_op jit(solution)/shard_map/pallas_call | solution.py:97
  1.6 16.5 %all-to-all-start = ((bf16[4,32,512]{2,1,0:T(8,128)(2,1)}), bf16[4,32,512]{2,1,0:T(8,128)(2,1)S(1)}, u32[]{:S(2)}, u32[]{:S(2)}) async-start(bf16[4,32,512]{2,1,0:T(8,128)(2,1)} %shard_map.55), calls=%async_computation | async-start | bytes 262144 | tf_op jit(solution)/shard_map/all_to_all | solution.py:113
  18.1 2.5 %collective-permute-start.2 = (bf16[32,2048]{1,0:T(8,128)(2,1)S(1)}, bf16[32,2048]{1,0:T(8,128)(2,1)S(1)}, u32[]{:S(2)}, u32[]{:S(2)}) collective-permute-start(bf16[32,2048]{1,0:T(8,128)(2,1)S(1)} %get-tuple-element.11), channel_id=1, source_target_pairs={{0,3},{1,2},{2,1},{3,0},{4,7},{5,6},{6,5},{7,4},{8,11},{9,10},{10,... | collective-permute-start | bytes 393224 | tf_op jit(solution)/shard_map/ppermute | solution.py:120
  20.6 5.2 %collective-permute-start.1 = (bf16[32,2048]{1,0:T(8,128)(2,1)S(1)}, bf16[32,2048]{1,0:T(8,128)(2,1)S(1)}, u32[]{:S(2)}, u32[]{:S(2)}) collective-permute-start(bf16[32,2048]{1,0:T(8,128)(2,1)S(1)} %get-tuple-element.12), channel_id=1, source_target_pairs={{0,2},{1,3},{2,0},{3,1},{4,6},{5,7},{6,4},{7,5},{8,10},{9,11},{10,... | collective-permute-start | bytes 393224 | tf_op jit(solution)/shard_map/ppermute | solution.py:120
  25.8 1.9 %collective-permute-start = (bf16[32,2048]{1,0:T(8,128)(2,1)S(1)}, bf16[32,2048]{1,0:T(8,128)(2,1)S(1)}, u32[]{:S(2)}, u32[]{:S(2)}) collective-permute-start(bf16[32,2048]{1,0:T(8,128)(2,1)S(1)} %get-tuple-element.10), channel_id=1, source_target_pairs={{0,1},{1,0},{2,3},{3,2},{4,5},{5,4},{6,7},{7,6},{8,9},{9,8},{10,11... | collective-permute-start | bytes 393224 | tf_op jit(solution)/shard_map/ppermute | solution.py:120
  27.7 0.6 copy-done.2
  28.5 0.1 eq.31
  28.6 0.1 fusion.33
  28.7 0.9 %fusion.1 = bf16[16,8,512]{2,1,0:T(8,128)(2,1)} fusion(bf16[128,512]{1,0:T(8,128)(2,1)S(1)} %bitcast.22, s32[128]{0:T(128)S(1)} %get-tuple-element.21, s32[128]{0:T(128)S(1)} %get-tuple-element.20, s32[128]{0:T(128)S(1)} %get-tuple-element.19, s32[128]{0:T(128)S(1)} %get-tuple-element.22, s32[128]{0:T(128)S(1)} %eq.31, ...), kind=kOutput, calls=%fused_computation.3 | convolution fusion | flops 16941056 | bytes 264960 | tf_op jit(solution)/shard_map/dot_general | solution.py:132
  29.6 9.1 %all-to-all-start.1 = ((bf16[16,8,512]{2,1,0:T(8,128)(2,1)}), bf16[16,8,512]{2,1,0:T(8,128)(2,1)S(1)}, u32[]{:S(2)}, u32[]{:S(2)}) async-start(bf16[16,8,512]{2,1,0:T(8,128)(2,1)} %fusion.1), calls=%async_computation.1 | async-start | bytes 262144 | tf_op jit(solution)/shard_map/all_to_all | solution.py:137
  38.7 0.1 pad_add_fusion
  38.8 0.1 eq.35
  38.9 1.2 %fusion = bf16[16,8,2048]{2,1,0:T(8,128)(2,1)} fusion(bf16[32,2048]{1,0:T(8,128)(2,1)S(1)} %collective-permute-done.2, bf16[32,2048]{1,0:T(8,128)(2,1)S(1)} %collective-permute-done.1, bf16[32,2048]{1,0:T(8,128)(2,1)S(1)} %collective-permute-done, bf16[32,2048]{1,0:T(8,128)(2,1)S(1)} %get-tuple-element.9, s32[128]{0:T(128)S(1)} %eq.35, ...), kind=kOutput, calls=%fused_computation.1 | convolution fusion | flops 69566464 | bytes 1051392 | tf_op jit(solution)/shard_map/dot_general | solution.py:132
  40.1 11.2 %all-to-all-done.1 = bf16[16,8,512]{2,1,0:T(8,128)(2,1)S(1)} async-done(((bf16[16,8,512]{2,1,0:T(8,128)(2,1)}), bf16[16,8,512]{2,1,0:T(8,128)(2,1)S(1)}, u32[]{:S(2)}, u32[]{:S(2)}) %all-to-all-start.1) | async-done | bytes 131104 | tf_op jit(solution)/shard_map/all_to_all | solution.py:137
  51.3 3.6 %collective-permute-start.3 = (bf16[128,512]{1,0:T(8,128)(2,1)S(1)}, bf16[128,512]{1,0:T(8,128)(2,1)S(1)}, u32[]{:S(2)}, u32[]{:S(2)}) collective-permute-start(bf16[128,512]{1,0:T(8,128)(2,1)S(1)} %bitcast.18), channel_id=1, source_target_pairs={{0,8},{4,12},{8,16},{12,20},{16,24},{20,28},{24,32},{28,36},{32,40... | collective-permute-start | bytes 393224 | tf_op jit(solution)/shard_map/ppermute | solution.py:142
  54.9 4.7 %collective-permute-start.4 = (bf16[128,512]{1,0:T(8,128)(2,1)S(1)}, bf16[128,512]{1,0:T(8,128)(2,1)S(1)}, u32[]{:S(2)}, u32[]{:S(2)}) collective-permute-start(bf16[128,512]{1,0:T(8,128)(2,1)S(1)} %bitcast.19), channel_id=1, source_target_pairs={{0,16},{4,20},{8,24},{12,28},{16,32},{20,36},{24,40},{28,44},{32,4... | collective-permute-start | bytes 393224 | tf_op jit(solution)/shard_map/ppermute | solution.py:142
  59.7 5.5 %collective-permute-start.6 = (bf16[128,512]{1,0:T(8,128)(2,1)S(1)}, bf16[128,512]{1,0:T(8,128)(2,1)S(1)}, u32[]{:S(2)}, u32[]{:S(2)}) collective-permute-start(bf16[128,512]{1,0:T(8,128)(2,1)S(1)} %bitcast.21), channel_id=1, source_target_pairs={{0,32},{4,36},{8,40},{12,44},{16,48},{20,52},{24,56},{28,60},{1,33... | collective-permute-start | bytes 393224 | tf_op jit(solution)/shard_map/ppermute | solution.py:142
  65.2 3.6 %all-to-all-start.2 = ((bf16[16,8,2048]{2,1,0:T(8,128)(2,1)}), bf16[16,8,2048]{2,1,0:T(8,128)(2,1)S(1)}, u32[]{:S(2)}, u32[]{:S(2)}) async-start(bf16[16,8,2048]{2,1,0:T(8,128)(2,1)} %fusion), calls=%async_computation.2 | async-start | bytes 1048576 | tf_op jit(solution)/shard_map/all_to_all | solution.py:139
  68.8 1.3 %collective-permute-start.5 = (bf16[128,512]{1,0:T(8,128)(2,1)S(1)}, bf16[128,512]{1,0:T(8,128)(2,1)S(1)}, u32[]{:S(2)}, u32[]{:S(2)}) collective-permute-start(bf16[128,512]{1,0:T(8,128)(2,1)S(1)} %collective-permute-done.3), channel_id=1, source_target_pairs={{0,16},{4,20},{8,24},{12,28},{16,32},{20,36},{24,40},{28,44},{32,4... | collective-permute-start | bytes 393224 | tf_op jit(solution)/shard_map/ppermute | solution.py:142
  70.1 2.5 %collective-permute-done.5 = bf16[128,512]{1,0:T(8,128)(2,1)S(1)} collective-permute-done((bf16[128,512]{1,0:T(8,128)(2,1)S(1)}, bf16[128,512]{1,0:T(8,128)(2,1)S(1)}, u32[]{:S(2)}, u32[]{:S(2)}) %collective-permute-start.5) | collective-permute-done | bytes 131104 | tf_op jit(solution)/shard_map/ppermute | solution.py:142
  72.7 1.9 %collective-permute-start.7 = (bf16[512,512]{1,0:T(8,128)(2,1)S(1)}, bf16[512,512]{1,0:T(8,128)(2,1)S(1)}, u32[]{:S(2)}, u32[]{:S(2)}) collective-permute-start(bf16[512,512]{1,0:T(8,128)(2,1)S(1)} %constant_dynamic-slice_fusion), channel_id=1, source_target_pairs={{0,4},{4,0},{8,12},{12,8},{16,20},{20,16},{24,28},{28,24},{32,36},... | collective-permute-start | bytes 1572872 | tf_op jit(solution)/shard_map/ppermute | solution.py:148
  74.6 1.9 %collective-permute-done.7.sib = bf16[512,512]{1,0:T(8,128)(2,1)S(1)} collective-permute-done((bf16[512,512]{1,0:T(8,128)(2,1)S(1)}, bf16[512,512]{1,0:T(8,128)(2,1)S(1)}, u32[]{:S(2)}, u32[]{:S(2)}) %collective-permute-start.7) | collective-permute-done | bytes 524320 | tf_op jit(solution)/shard_map/ppermute | solution.py:148
  76.5 10.5 %all-to-all-done.2 = bf16[16,8,2048]{2,1,0:T(8,128)(2,1)S(1)} async-done(((bf16[16,8,2048]{2,1,0:T(8,128)(2,1)}), bf16[16,8,2048]{2,1,0:T(8,128)(2,1)S(1)}, u32[]{:S(2)}, u32[]{:S(2)}) %all-to-all-start.2) | async-done | bytes 524320 | tf_op jit(solution)/shard_map/all_to_all | solution.py:139
  87.0 5.3 %shard_map.56 = bf16[128,2048]{1,0:T(8,128)(2,1)} custom-call(s32[1,4]{1,0:T(1,128)S(1)} %copy-done, bf16[128,2048]{1,0:T(8,128)(2,1)S(1)} %bitcast.17, bf16[640,512]{1,0:T(8,128)(2,1)S(1)} %constant_dynamic-update-slice_fusion.own, bf16[512,512]{1,0:T(8,128)(2,1)S(1)} %collective-permute-done.7.sib), custom_call_target="tpu_custom_call" | custom-call | flops 1207959552 | bytes 2228224 | tf_op jit(solution)/shard_map/pallas_call | solution.py:67
  (24 shorter events, 0.3 us)
Async XLA Ops:
  0.0 18.0 %copy-start.1 = (bf16[32,8192]{1,0:T(8,128)(2,1)S(1)}, bf16[32,8192]{1,0:T(8,128)(2,1)}, u32[]{:S(2)}) copy-start(bf16[32,8192]{1,0:T(8,128)(2,1)} %param.5) | copy-start | bytes 1572868
  1.6 27.1 %all-to-all-start = ((bf16[4,32,512]{2,1,0:T(8,128)(2,1)}), bf16[4,32,512]{2,1,0:T(8,128)(2,1)S(1)}, u32[]{:S(2)}, u32[]{:S(2)}) async-start(bf16[4,32,512]{2,1,0:T(8,128)(2,1)} %shard_map.55), calls=%async_computation | async-start | bytes 262144 | tf_op jit(solution)/shard_map/all_to_all | solution.py:113
  18.1 20.8 %collective-permute-start.2 = (bf16[32,2048]{1,0:T(8,128)(2,1)S(1)}, bf16[32,2048]{1,0:T(8,128)(2,1)S(1)}, u32[]{:S(2)}, u32[]{:S(2)}) collective-permute-start(bf16[32,2048]{1,0:T(8,128)(2,1)S(1)} %get-tuple-element.11), channel_id=1, source_target_pairs={{0,3},{1,2},{2,1},{3,0},{4,7},{5,6},{6,5},{7,4},{8,11},{9,10},{10,... | collective-permute-start | bytes 393224 | tf_op jit(solution)/shard_map/ppermute | solution.py:120
  20.6 18.3 %collective-permute-start.1 = (bf16[32,2048]{1,0:T(8,128)(2,1)S(1)}, bf16[32,2048]{1,0:T(8,128)(2,1)S(1)}, u32[]{:S(2)}, u32[]{:S(2)}) collective-permute-start(bf16[32,2048]{1,0:T(8,128)(2,1)S(1)} %get-tuple-element.12), channel_id=1, source_target_pairs={{0,2},{1,3},{2,0},{3,1},{4,6},{5,7},{6,4},{7,5},{8,10},{9,11},{10,... | collective-permute-start | bytes 393224 | tf_op jit(solution)/shard_map/ppermute | solution.py:120
  25.8 13.2 %collective-permute-start = (bf16[32,2048]{1,0:T(8,128)(2,1)S(1)}, bf16[32,2048]{1,0:T(8,128)(2,1)S(1)}, u32[]{:S(2)}, u32[]{:S(2)}) collective-permute-start(bf16[32,2048]{1,0:T(8,128)(2,1)S(1)} %get-tuple-element.10), channel_id=1, source_target_pairs={{0,1},{1,0},{2,3},{3,2},{4,5},{5,4},{6,7},{7,6},{8,9},{9,8},{10,11... | collective-permute-start | bytes 393224 | tf_op jit(solution)/shard_map/ppermute | solution.py:120
  27.7 0.7 copy-start.2
  29.6 21.7 %all-to-all-start.1 = ((bf16[16,8,512]{2,1,0:T(8,128)(2,1)}), bf16[16,8,512]{2,1,0:T(8,128)(2,1)S(1)}, u32[]{:S(2)}, u32[]{:S(2)}) async-start(bf16[16,8,512]{2,1,0:T(8,128)(2,1)} %fusion.1), calls=%async_computation.1 | async-start | bytes 262144 | tf_op jit(solution)/shard_map/all_to_all | solution.py:137
  51.3 17.5 %collective-permute-start.3 = (bf16[128,512]{1,0:T(8,128)(2,1)S(1)}, bf16[128,512]{1,0:T(8,128)(2,1)S(1)}, u32[]{:S(2)}, u32[]{:S(2)}) collective-permute-start(bf16[128,512]{1,0:T(8,128)(2,1)S(1)} %bitcast.18), channel_id=1, source_target_pairs={{0,8},{4,12},{8,16},{12,20},{16,24},{20,28},{24,32},{28,36},{32,40... | collective-permute-start | bytes 393224 | tf_op jit(solution)/shard_map/ppermute | solution.py:142
  54.9 15.2 %collective-permute-start.4 = (bf16[128,512]{1,0:T(8,128)(2,1)S(1)}, bf16[128,512]{1,0:T(8,128)(2,1)S(1)}, u32[]{:S(2)}, u32[]{:S(2)}) collective-permute-start(bf16[128,512]{1,0:T(8,128)(2,1)S(1)} %bitcast.19), channel_id=1, source_target_pairs={{0,16},{4,20},{8,24},{12,28},{16,32},{20,36},{24,40},{28,44},{32,4... | collective-permute-start | bytes 393224 | tf_op jit(solution)/shard_map/ppermute | solution.py:142
  59.7 12.9 %collective-permute-start.6 = (bf16[128,512]{1,0:T(8,128)(2,1)S(1)}, bf16[128,512]{1,0:T(8,128)(2,1)S(1)}, u32[]{:S(2)}, u32[]{:S(2)}) collective-permute-start(bf16[128,512]{1,0:T(8,128)(2,1)S(1)} %bitcast.21), channel_id=1, source_target_pairs={{0,32},{4,36},{8,40},{12,44},{16,48},{20,52},{24,56},{28,60},{1,33... | collective-permute-start | bytes 393224 | tf_op jit(solution)/shard_map/ppermute | solution.py:142
  65.2 21.8 %all-to-all-start.2 = ((bf16[16,8,2048]{2,1,0:T(8,128)(2,1)}), bf16[16,8,2048]{2,1,0:T(8,128)(2,1)S(1)}, u32[]{:S(2)}, u32[]{:S(2)}) async-start(bf16[16,8,2048]{2,1,0:T(8,128)(2,1)} %fusion), calls=%async_computation.2 | async-start | bytes 1048576 | tf_op jit(solution)/shard_map/all_to_all | solution.py:139
  68.8 3.8 %collective-permute-start.5 = (bf16[128,512]{1,0:T(8,128)(2,1)S(1)}, bf16[128,512]{1,0:T(8,128)(2,1)S(1)}, u32[]{:S(2)}, u32[]{:S(2)}) collective-permute-start(bf16[128,512]{1,0:T(8,128)(2,1)S(1)} %collective-permute-done.3), channel_id=1, source_target_pairs={{0,16},{4,20},{8,24},{12,28},{16,32},{20,36},{24,40},{28,44},{32,4... | collective-permute-start | bytes 393224 | tf_op jit(solution)/shard_map/ppermute | solution.py:142
  72.7 14.3 %copy-start = (s32[1,4]{1,0:T(1,128)S(1)}, s32[1,4]{1,0:T(1,128)}, u32[]{:S(2)}) copy-start(s32[1,4]{1,0:T(1,128)} %lengths.1) | copy-start | bytes 52
  72.7 3.8 %collective-permute-start.7 = (bf16[512,512]{1,0:T(8,128)(2,1)S(1)}, bf16[512,512]{1,0:T(8,128)(2,1)S(1)}, u32[]{:S(2)}, u32[]{:S(2)}) collective-permute-start(bf16[512,512]{1,0:T(8,128)(2,1)S(1)} %constant_dynamic-slice_fusion), channel_id=1, source_target_pairs={{0,4},{4,0},{8,12},{12,8},{16,20},{20,16},{24,28},{28,24},{32,36},... | collective-permute-start | bytes 1572872 | tf_op jit(solution)/shard_map/ppermute | solution.py:148

commit v3 on v2

--- a/solution.py
+++ b/solution.py
@@ -141,8 +141,8 @@
     def ahead(x, chips):
         return lax.ppermute(x, "seq", [(i, i + 2 * chips) for i in range(seq - 2 * chips)])
 
-    back1, back2, back4 = ahead(kv, 1), ahead(kv, 2), ahead(kv, 4)
-    own = jnp.concatenate([kv, back1, back2, ahead(back1, 2), back4], axis=0)
+    back2, back1 = ahead(kv, 2), ahead(kv, 1)
+    own = jnp.concatenate([kv, back1, back2, ahead(back2, 1), ahead(back2, 2)], axis=0)
     shard = lax.axis_index("seq")
     given = lax.dynamic_slice_in_dim(own, lax.rem(shard, 2) * rows, 4 * rows, 0)
     sib = lax.ppermute(given, "seq", [(i, i ^ 1) for i in range(seq)])

time: 92.9 us -> 88.6 us (0.954)
  the two profiles are of different devices: /device:TPU:4 before, /device:TPU:20 now
where the time goes in v3:
time: 88.6 us; the launch traced here: 88 us
  starting transfers between devices  57.4 us (65%)
  waiting for transfers between devices  20 us (23%)
  Pallas kernels  6.94 us (8%)
  matrix products  2.12 us (2%)
  local copies, waits for them, and re-layouts  1.2 us (1%)
    all_to_all x1, starting transfers between devices, shards(): kv = lax.all_to_all(kv_sorted, 'grp', 0, 0, tiled=True).reshape(rows, -1)  20.4 us
    ppermute x4, starting transfers between devices, ahead(): lax.ppermute(x, 'seq', [(i, i + 2 * chips) for i in range(seq - 2 * chips)])  16.8 us
    all_to_all x1, waiting for transfers between devices, shards(): kv = lax.all_to_all(kv_sorted, 'grp', 0, 0, tiled=True).reshape(rows, -1)  11.2 us
    ppermute x3, starting transfers between devices, shards(): piece = lax.ppermute(piece, 'tp', [(i, i ^ d) for i in range(tp)])  9.56 us
    pallas_call x1, Pallas kernels, attention(): pl.pallas_call(attend, out_shape=jax.ShapeDtypeStruct(q.shape, jnp.bfloat...  5.34 us
    all_to_all x1, starting transfers between devices, shards(): held_kv = lax.all_to_all(packed, 'tp', 0, 0, tiled=True).reshape(rows, -1)  5.12 us
    all_to_all x1, waiting for transfers between devices, shards(): q = lax.all_to_all(q_sorted, 'grp', 0, 0, tiled=True).reshape(rows, -1)  4.06 us
    all_to_all x1, starting transfers between devices, shards(): q = lax.all_to_all(q_sorted, 'grp', 0, 0, tiled=True).reshape(rows, -1)  3.59 us
  transfers between devices with their start and end apart: 11, of which 4 were waited for; matrix products, arithmetic and copies ran while one was open for 3% of the time, Pallas kernels for 0%

profile of v3, /device:TPU:20, one launch (start us, length us, event | category | flops | bytes accessed | tf_op | source)
XLA Modules:
  0.0 88.0 jit_solution(3208386789585548224)
XLA Ops:
  0.0 1.6 %shard_map.55 = bf16[4,32,512]{2,1,0:T(8,128)(2,1)} custom-call(bf16[32,1024]{1,0:T(8,128)(2,1)} %refs_0_.1, bf16[32,1024]{1,0:T(8,128)(2,1)} %refs_1_.1), custom_call_target="tpu_custom_call" | custom-call | tf_op jit(solution)/shard_map/pallas_call | solution.py:97
  1.6 5.1 %all-to-all-start = ((bf16[4,32,512]{2,1,0:T(8,128)(2,1)}), bf16[4,32,512]{2,1,0:T(8,128)(2,1)S(1)}, u32[]{:S(2)}, u32[]{:S(2)}) async-start(bf16[4,32,512]{2,1,0:T(8,128)(2,1)} %shard_map.55), calls=%async_computation | async-start | bytes 262144 | tf_op jit(solution)/shard_map/all_to_all | solution.py:113
  6.8 2.5 %collective-permute-start.2 = (bf16[32,2048]{1,0:T(8,128)(2,1)S(1)}, bf16[32,2048]{1,0:T(8,128)(2,1)S(1)}, u32[]{:S(2)}, u32[]{:S(2)}) collective-permute-start(bf16[32,2048]{1,0:T(8,128)(2,1)S(1)} %get-tuple-element.11), channel_id=1, source_target_pairs={{0,3},{1,2},{2,1},{3,0},{4,7},{5,6},{6,5},{7,4},{8,11},{9,10},{10,... | collective-permute-start | bytes 393224 | tf_op jit(solution)/shard_map/ppermute | solution.py:120
  9.2 5.2 %collective-permute-start.1 = (bf16[32,2048]{1,0:T(8,128)(2,1)S(1)}, bf16[32,2048]{1,0:T(8,128)(2,1)S(1)}, u32[]{:S(2)}, u32[]{:S(2)}) collective-permute-start(bf16[32,2048]{1,0:T(8,128)(2,1)S(1)} %get-tuple-element.12), channel_id=1, source_target_pairs={{0,2},{1,3},{2,0},{3,1},{4,6},{5,7},{6,4},{7,5},{8,10},{9,11},{10,... | collective-permute-start | bytes 393224 | tf_op jit(solution)/shard_map/ppermute | solution.py:120
  14.4 1.9 %collective-permute-start = (bf16[32,2048]{1,0:T(8,128)(2,1)S(1)}, bf16[32,2048]{1,0:T(8,128)(2,1)S(1)}, u32[]{:S(2)}, u32[]{:S(2)}) collective-permute-start(bf16[32,2048]{1,0:T(8,128)(2,1)S(1)} %get-tuple-element.10), channel_id=1, source_target_pairs={{0,1},{1,0},{2,3},{3,2},{4,5},{5,4},{6,7},{7,6},{8,9},{9,8},{10,11... | collective-permute-start | bytes 393224 | tf_op jit(solution)/shard_map/ppermute | solution.py:120
  16.4 0.6 copy-done.2
  17.1 0.1 eq.31
  17.2 0.1 fusion.33
  17.3 0.9 %fusion.1 = bf16[16,8,512]{2,1,0:T(8,128)(2,1)} fusion(bf16[128,512]{1,0:T(8,128)(2,1)S(1)} %bitcast.21, s32[128]{0:T(128)S(1)} %get-tuple-element.21, s32[128]{0:T(128)S(1)} %get-tuple-element.20, s32[128]{0:T(128)S(1)} %get-tuple-element.19, s32[128]{0:T(128)S(1)} %get-tuple-element.22, s32[128]{0:T(128)S(1)} %eq.31, ...), kind=kOutput, calls=%fused_computation.3 | convolution fusion | flops 16941056 | bytes 264960 | tf_op jit(solution)/shard_map/dot_general | solution.py:132
  18.3 20.4 %all-to-all-start.1 = ((bf16[16,8,512]{2,1,0:T(8,128)(2,1)}), bf16[16,8,512]{2,1,0:T(8,128)(2,1)S(1)}, u32[]{:S(2)}, u32[]{:S(2)}) async-start(bf16[16,8,512]{2,1,0:T(8,128)(2,1)} %fusion.1), calls=%async_computation.1 | async-start | bytes 262144 | tf_op jit(solution)/shard_map/all_to_all | solution.py:137
  38.7 0.1 pad_add_fusion
  38.8 0.1 eq.35
  38.9 1.2 %fusion = bf16[16,8,2048]{2,1,0:T(8,128)(2,1)} fusion(bf16[32,2048]{1,0:T(8,128)(2,1)S(1)} %collective-permute-done.2, bf16[32,2048]{1,0:T(8,128)(2,1)S(1)} %collective-permute-done.1, bf16[32,2048]{1,0:T(8,128)(2,1)S(1)} %collective-permute-done, bf16[32,2048]{1,0:T(8,128)(2,1)S(1)} %get-tuple-element.9, s32[128]{0:T(128)S(1)} %eq.35, ...), kind=kOutput, calls=%fused_computation.1 | convolution fusion | flops 69566464 | bytes 1051392 | tf_op jit(solution)/shard_map/dot_general | solution.py:132
  40.1 11.2 %all-to-all-done.1 = bf16[16,8,512]{2,1,0:T(8,128)(2,1)S(1)} async-done(((bf16[16,8,512]{2,1,0:T(8,128)(2,1)}), bf16[16,8,512]{2,1,0:T(8,128)(2,1)S(1)}, u32[]{:S(2)}, u32[]{:S(2)}) %all-to-all-start.1) | async-done | bytes 131104 | tf_op jit(solution)/shard_map/all_to_all | solution.py:137
  51.3 4.7 %collective-permute-start.4 = (bf16[128,512]{1,0:T(8,128)(2,1)S(1)}, bf16[128,512]{1,0:T(8,128)(2,1)S(1)}, u32[]{:S(2)}, u32[]{:S(2)}) collective-permute-start(bf16[128,512]{1,0:T(8,128)(2,1)S(1)} %bitcast.18), channel_id=1, source_target_pairs={{0,16},{4,20},{8,24},{12,28},{16,32},{20,36},{24,40},{28,44},{32,4... | collective-permute-start | bytes 393224 | tf_op jit(solution)/shard_map/ppermute | solution.py:142
  56.0 4.8 %collective-permute-start.3 = (bf16[128,512]{1,0:T(8,128)(2,1)S(1)}, bf16[128,512]{1,0:T(8,128)(2,1)S(1)}, u32[]{:S(2)}, u32[]{:S(2)}) collective-permute-start(bf16[128,512]{1,0:T(8,128)(2,1)S(1)} %bitcast.19), channel_id=1, source_target_pairs={{0,8},{4,12},{8,16},{12,20},{16,24},{20,28},{24,32},{28,36},{32,40... | collective-permute-start | bytes 393224 | tf_op jit(solution)/shard_map/ppermute | solution.py:142
  60.9 3.6 %all-to-all-start.2 = ((bf16[16,8,2048]{2,1,0:T(8,128)(2,1)}), bf16[16,8,2048]{2,1,0:T(8,128)(2,1)S(1)}, u32[]{:S(2)}, u32[]{:S(2)}) async-start(bf16[16,8,2048]{2,1,0:T(8,128)(2,1)} %fusion), calls=%async_computation.2 | async-start | bytes 1048576 | tf_op jit(solution)/shard_map/all_to_all | solution.py:139
  64.5 2.7 %collective-permute-start.5 = (bf16[128,512]{1,0:T(8,128)(2,1)S(1)}, bf16[128,512]{1,0:T(8,128)(2,1)S(1)}, u32[]{:S(2)}, u32[]{:S(2)}) collective-permute-start(bf16[128,512]{1,0:T(8,128)(2,1)S(1)} %collective-permute-done.4), channel_id=1, source_target_pairs={{0,8},{4,12},{8,16},{12,20},{16,24},{20,28},{24,32},{28,36},{32,40... | collective-permute-start | bytes 393224 | tf_op jit(solution)/shard_map/ppermute | solution.py:142
  67.2 4.6 %collective-permute-start.6 = (bf16[128,512]{1,0:T(8,128)(2,1)S(1)}, bf16[128,512]{1,0:T(8,128)(2,1)S(1)}, u32[]{:S(2)}, u32[]{:S(2)}) collective-permute-start(bf16[128,512]{1,0:T(8,128)(2,1)S(1)} %collective-permute-done.4), channel_id=1, source_target_pairs={{0,16},{4,20},{8,24},{12,28},{16,32},{20,36},{24,40},{28,44},{32,4... | collective-permute-start | bytes 393224 | tf_op jit(solution)/shard_map/ppermute | solution.py:142
  71.9 2.8 %collective-permute-done.6 = bf16[128,512]{1,0:T(8,128)(2,1)S(1)} collective-permute-done((bf16[128,512]{1,0:T(8,128)(2,1)S(1)}, bf16[128,512]{1,0:T(8,128)(2,1)S(1)}, u32[]{:S(2)}, u32[]{:S(2)}) %collective-permute-start.6) | collective-permute-done | bytes 131104 | tf_op jit(solution)/shard_map/ppermute | solution.py:142
  74.8 1.9 %collective-permute-start.7 = (bf16[512,512]{1,0:T(8,128)(2,1)S(1)}, bf16[512,512]{1,0:T(8,128)(2,1)S(1)}, u32[]{:S(2)}, u32[]{:S(2)}) collective-permute-start(bf16[512,512]{1,0:T(8,128)(2,1)S(1)} %constant_dynamic-slice_fusion), channel_id=1, source_target_pairs={{0,4},{4,0},{8,12},{12,8},{16,20},{20,16},{24,28},{28,24},{32,36},... | collective-permute-start | bytes 1572872 | tf_op jit(solution)/shard_map/ppermute | solution.py:148
  76.7 1.9 %collective-permute-done.7.sib = bf16[512,512]{1,0:T(8,128)(2,1)S(1)} collective-permute-done((bf16[512,512]{1,0:T(8,128)(2,1)S(1)}, bf16[512,512]{1,0:T(8,128)(2,1)S(1)}, u32[]{:S(2)}, u32[]{:S(2)}) %collective-permute-start.7) | collective-permute-done | bytes 524320 | tf_op jit(solution)/shard_map/ppermute | solution.py:148
  78.6 4.1 %all-to-all-done.2 = bf16[16,8,2048]{2,1,0:T(8,128)(2,1)S(1)} async-done(((bf16[16,8,2048]{2,1,0:T(8,128)(2,1)}), bf16[16,8,2048]{2,1,0:T(8,128)(2,1)S(1)}, u32[]{:S(2)}, u32[]{:S(2)}) %all-to-all-start.2) | async-done | bytes 524320 | tf_op jit(solution)/shard_map/all_to_all | solution.py:139
  82.7 5.3 %shard_map.56 = bf16[128,2048]{1,0:T(8,128)(2,1)} custom-call(s32[1,4]{1,0:T(1,128)S(1)} %copy-done, bf16[128,2048]{1,0:T(8,128)(2,1)S(1)} %bitcast.17, bf16[640,512]{1,0:T(8,128)(2,1)S(1)} %constant_dynamic-update-slice_fusion.own, bf16[512,512]{1,0:T(8,128)(2,1)S(1)} %collective-permute-done.7.sib), custom_call_target="tpu_custom_call" | custom-call | flops 1207959552 | bytes 2228224 | tf_op jit(solution)/shard_map/pallas_call | solution.py:67
  (24 shorter events, 0.3 us)
Async XLA Ops:
  0.0 6.7 %copy-start.1 = (bf16[32,8192]{1,0:T(8,128)(2,1)S(1)}, bf16[32,8192]{1,0:T(8,128)(2,1)}, u32[]{:S(2)}) copy-start(bf16[32,8192]{1,0:T(8,128)(2,1)} %param.5) | copy-start | bytes 1572868
  1.6 15.7 %all-to-all-start = ((bf16[4,32,512]{2,1,0:T(8,128)(2,1)}), bf16[4,32,512]{2,1,0:T(8,128)(2,1)S(1)}, u32[]{:S(2)}, u32[]{:S(2)}) async-start(bf16[4,32,512]{2,1,0:T(8,128)(2,1)} %shard_map.55), calls=%async_computation | async-start | bytes 262144 | tf_op jit(solution)/shard_map/all_to_all | solution.py:113
  6.8 32.1 %collective-permute-start.2 = (bf16[32,2048]{1,0:T(8,128)(2,1)S(1)}, bf16[32,2048]{1,0:T(8,128)(2,1)S(1)}, u32[]{:S(2)}, u32[]{:S(2)}) collective-permute-start(bf16[32,2048]{1,0:T(8,128)(2,1)S(1)} %get-tuple-element.11), channel_id=1, source_target_pairs={{0,3},{1,2},{2,1},{3,0},{4,7},{5,6},{6,5},{7,4},{8,11},{9,10},{10,... | collective-permute-start | bytes 393224 | tf_op jit(solution)/shard_map/ppermute | solution.py:120
  9.2 29.7 %collective-permute-start.1 = (bf16[32,2048]{1,0:T(8,128)(2,1)S(1)}, bf16[32,2048]{1,0:T(8,128)(2,1)S(1)}, u32[]{:S(2)}, u32[]{:S(2)}) collective-permute-start(bf16[32,2048]{1,0:T(8,128)(2,1)S(1)} %get-tuple-element.12), channel_id=1, source_target_pairs={{0,2},{1,3},{2,0},{3,1},{4,6},{5,7},{6,4},{7,5},{8,10},{9,11},{10,... | collective-permute-start | bytes 393224 | tf_op jit(solution)/shard_map/ppermute | solution.py:120
  14.4 24.5 %collective-permute-start = (bf16[32,2048]{1,0:T(8,128)(2,1)S(1)}, bf16[32,2048]{1,0:T(8,128)(2,1)S(1)}, u32[]{:S(2)}, u32[]{:S(2)}) collective-permute-start(bf16[32,2048]{1,0:T(8,128)(2,1)S(1)} %get-tuple-element.10), channel_id=1, source_target_pairs={{0,1},{1,0},{2,3},{3,2},{4,5},{5,4},{6,7},{7,6},{8,9},{9,8},{10,11... | collective-permute-start | bytes 393224 | tf_op jit(solution)/shard_map/ppermute | solution.py:120
  16.4 0.7 copy-start.2
  18.3 33.1 %all-to-all-start.1 = ((bf16[16,8,512]{2,1,0:T(8,128)(2,1)}), bf16[16,8,512]{2,1,0:T(8,128)(2,1)S(1)}, u32[]{:S(2)}, u32[]{:S(2)}) async-start(bf16[16,8,512]{2,1,0:T(8,128)(2,1)} %fusion.1), calls=%async_computation.1 | async-start | bytes 262144 | tf_op jit(solution)/shard_map/all_to_all | solution.py:137
  51.3 13.2 %collective-permute-start.4 = (bf16[128,512]{1,0:T(8,128)(2,1)S(1)}, bf16[128,512]{1,0:T(8,128)(2,1)S(1)}, u32[]{:S(2)}, u32[]{:S(2)}) collective-permute-start(bf16[128,512]{1,0:T(8,128)(2,1)S(1)} %bitcast.18), channel_id=1, source_target_pairs={{0,16},{4,20},{8,24},{12,28},{16,32},{20,36},{24,40},{28,44},{32,4... | collective-permute-start | bytes 393224 | tf_op jit(solution)/shard_map/ppermute | solution.py:142
  56.0 15.8 %collective-permute-start.3 = (bf16[128,512]{1,0:T(8,128)(2,1)S(1)}, bf16[128,512]{1,0:T(8,128)(2,1)S(1)}, u32[]{:S(2)}, u32[]{:S(2)}) collective-permute-start(bf16[128,512]{1,0:T(8,128)(2,1)S(1)} %bitcast.19), channel_id=1, source_target_pairs={{0,8},{4,12},{8,16},{12,20},{16,24},{20,28},{24,32},{28,36},{32,40... | collective-permute-start | bytes 393224 | tf_op jit(solution)/shard_map/ppermute | solution.py:142
  60.9 21.8 %all-to-all-start.2 = ((bf16[16,8,2048]{2,1,0:T(8,128)(2,1)}), bf16[16,8,2048]{2,1,0:T(8,128)(2,1)S(1)}, u32[]{:S(2)}, u32[]{:S(2)}) async-start(bf16[16,8,2048]{2,1,0:T(8,128)(2,1)} %fusion), calls=%async_computation.2 | async-start | bytes 1048576 | tf_op jit(solution)/shard_map/all_to_all | solution.py:139
  64.5 7.4 %collective-permute-start.5 = (bf16[128,512]{1,0:T(8,128)(2,1)S(1)}, bf16[128,512]{1,0:T(8,128)(2,1)S(1)}, u32[]{:S(2)}, u32[]{:S(2)}) collective-permute-start(bf16[128,512]{1,0:T(8,128)(2,1)S(1)} %collective-permute-done.4), channel_id=1, source_target_pairs={{0,8},{4,12},{8,16},{12,20},{16,24},{20,28},{24,32},{28,36},{32,40... | collective-permute-start | bytes 393224 | tf_op jit(solution)/shard_map/ppermute | solution.py:142
  67.2 7.5 %collective-permute-start.6 = (bf16[128,512]{1,0:T(8,128)(2,1)S(1)}, bf16[128,512]{1,0:T(8,128)(2,1)S(1)}, u32[]{:S(2)}, u32[]{:S(2)}) collective-permute-start(bf16[128,512]{1,0:T(8,128)(2,1)S(1)} %collective-permute-done.4), channel_id=1, source_target_pairs={{0,16},{4,20},{8,24},{12,28},{16,32},{20,36},{24,40},{28,44},{32,4... | collective-permute-start | bytes 393224 | tf_op jit(solution)/shard_map/ppermute | solution.py:142
  74.8 7.9 %copy-start = (s32[1,4]{1,0:T(1,128)S(1)}, s32[1,4]{1,0:T(1,128)}, u32[]{:S(2)}) copy-start(s32[1,4]{1,0:T(1,128)} %lengths.1) | copy-start | bytes 52
  74.8 3.8 %collective-permute-start.7 = (bf16[512,512]{1,0:T(8,128)(2,1)S(1)}, bf16[512,512]{1,0:T(8,128)(2,1)S(1)}, u32[]{:S(2)}, u32[]{:S(2)}) collective-permute-start(bf16[512,512]{1,0:T(8,128)(2,1)S(1)} %constant_dynamic-slice_fusion), channel_id=1, source_target_pairs={{0,4},{4,0},{8,12},{12,8},{16,20},{20,16},{24,28},{28,24},{32,36},... | collective-permute-start | bytes 1572872 | tf_op jit(solution)/shard_map/ppermute | solution.py:148

commit v4 on v3

--- a/solution.py
+++ b/solution.py
@@ -120,7 +120,6 @@
             piece = lax.ppermute(piece, "tp", [(i, i ^ d) for i in range(tp)])
         pieces.append(piece)
         arrived.append(lax.dynamic_slice_in_dim(block_table[0], other * blocks, blocks))
-    held_q = jnp.concatenate(pieces, axis=0)
 
     def order(destination):
         wide = jnp.broadcast_to(destination[:, None], (groups, block)).reshape(rows)
@@ -133,9 +132,10 @@
         return out.reshape(groups, block, -1)
 
     kv_sorted = sort(order(block_table[0]), held_kv)
+    kv = lax.all_to_all(kv_sorted, "grp", 0, 0, tiled=True).reshape(rows, -1)
+    kv, *pieces = lax.optimization_barrier((kv, *pieces))
+    held_q = jnp.concatenate(pieces, axis=0)
     q_sorted = sort(order(jnp.concatenate(arrived)), held_q)
-    kv = lax.all_to_all(kv_sorted, "grp", 0, 0, tiled=True).reshape(rows, -1)
-    kv, q_sorted = lax.optimization_barrier((kv, q_sorted))
     q = lax.all_to_all(q_sorted, "grp", 0, 0, tiled=True).reshape(rows, -1)
 
     def ahead(x, chips):

time: 88.6 us -> 95.8 us (1.081)
  starting transfers between devices: 57.4 us -> 63.4 us
  waiting for transfers between devices: 20 us -> 21.7 us
    all_to_all x1, waiting for transfers between devices: 11.2 us -> 0.01 us  [shards(): kv = lax.all_to_all(kv_sorted, 'grp', 0, 0, tiled=True).reshape(rows, -1)]
    ppermute x3, waiting for transfers between devices: 0.01 us -> 8.86 us  [shards(): piece = lax.ppermute(piece, 'tp', [(i, i ^ d) for i in range(tp)])]
    all_to_all x1, starting transfers between devices: 3.59 us -> 11.5 us  [shards(): q = lax.all_to_all(q_sorted, 'grp', 0, 0, tiled=True).reshape(rows, -1)]
    all_to_all x1, waiting for transfers between devices: 0.01 us -> 3.7 us  [shards(): held_kv = lax.all_to_all(packed, 'tp', 0, 0, tiled=True).reshape(rows, -1)]
    ppermute x4, waiting for transfers between devices: 2.85 us -> 4.68 us  [ahead(): lax.ppermute(x, 'seq', [(i, i + 2 * chips) for i in range(seq - 2 * chips)])]
    ppermute x4, starting transfers between devices: 16.8 us -> 15.2 us  [ahead(): lax.ppermute(x, 'seq', [(i, i + 2 * chips) for i in range(seq - 2 * chips)])]
    all_to_all x1, waiting for transfers between devices: 4.06 us -> 2.59 us  [shards(): q = lax.all_to_all(q_sorted, 'grp', 0, 0, tiled=True).reshape(rows, -1)]
  transfers between devices with their start and end apart: 11 -> 11, of which waited for: 4 -> 7; matrix products, arithmetic and copies ran while one was open for 3% -> 2% of each run, Pallas kernels for 0% -> 0%
where the time goes in v4:
time: 95.8 us; the launch traced here: 95 us
  starting transfers between devices  63.4 us (66%)
  waiting for transfers between devices  21.7 us (23%)
  Pallas kernels  6.89 us (7%)
  matrix products  2.13 us (2%)
    all_to_all x1, starting transfers between devices, shards(): kv = lax.all_to_all(kv_sorted, 'grp', 0, 0, tiled=True).reshape(rows, -1)  20.4 us
    ppermute x4, starting transfers between devices, ahead(): lax.ppermute(x, 'seq', [(i, i + 2 * chips) for i in range(seq - 2 * chips)])  15.2 us
    all_to_all x1, starting transfers between devices, shards(): q = lax.all_to_all(q_sorted, 'grp', 0, 0, tiled=True).reshape(rows, -1)  11.5 us
    ppermute x3, starting transfers between devices, shards(): piece = lax.ppermute(piece, 'tp', [(i, i ^ d) for i in range(tp)])  9.21 us
    ppermute x3, waiting for transfers between devices, shards(): piece = lax.ppermute(piece, 'tp', [(i, i ^ d) for i in range(tp)])  8.86 us
    pallas_call x1, Pallas kernels, attention(): pl.pallas_call(attend, out_shape=jax.ShapeDtypeStruct(q.shape, jnp.bfloat...  5.34 us
    all_to_all x1, starting transfers between devices, shards(): held_kv = lax.all_to_all(packed, 'tp', 0, 0, tiled=True).reshape(rows, -1)  5.25 us
    ppermute x4, waiting for transfers between devices, ahead(): lax.ppermute(x, 'seq', [(i, i + 2 * chips) for i in range(seq - 2 * chips)])  4.68 us
  transfers between devices with their start and end apart: 11, of which 7 were waited for; matrix products, arithmetic and copies ran while one was open for 2% of the time, Pallas kernels for 0%

profile of v4, /device:TPU:20, one launch (start us, length us, event | category | flops | bytes accessed | tf_op | source)
XLA Modules:
  0.0 95.0 jit_solution(13247946303581782278)
XLA Ops:
  0.0 1.5 %shard_map.55 = bf16[4,32,512]{2,1,0:T(8,128)(2,1)} custom-call(bf16[32,1024]{1,0:T(8,128)(2,1)} %refs_0_.1, bf16[32,1024]{1,0:T(8,128)(2,1)} %refs_1_.1), custom_call_target="tpu_custom_call" | custom-call | tf_op jit(solution)/shard_map/pallas_call | solution.py:97
  1.6 5.3 %all-to-all-start = ((bf16[4,32,512]{2,1,0:T(8,128)(2,1)}), bf16[4,32,512]{2,1,0:T(8,128)(2,1)S(1)}, u32[]{:S(2)}, u32[]{:S(2)}) async-start(bf16[4,32,512]{2,1,0:T(8,128)(2,1)} %shard_map.55), calls=%async_computation | async-start | bytes 262144 | tf_op jit(solution)/shard_map/all_to_all | solution.py:113
  6.9 0.1 eq.35
  7.0 3.7 %all-to-all-done = bf16[4,32,512]{2,1,0:T(8,128)(2,1)S(1)} async-done(((bf16[4,32,512]{2,1,0:T(8,128)(2,1)}), bf16[4,32,512]{2,1,0:T(8,128)(2,1)S(1)}, u32[]{:S(2)}, u32[]{:S(2)}) %all-to-all-start) | async-done | bytes 131104 | tf_op jit(solution)/shard_map/all_to_all | solution.py:113
  10.7 0.9 fusion.1
  11.7 20.4 %all-to-all-start.1 = ((bf16[16,8,512]{2,1,0:T(8,128)(2,1)}), bf16[16,8,512]{2,1,0:T(8,128)(2,1)S(1)}, u32[]{:S(2)}, u32[]{:S(2)}) async-start(bf16[16,8,512]{2,1,0:T(8,128)(2,1)} %fusion.1), calls=%async_computation.1 | async-start | bytes 262144 | tf_op jit(solution)/shard_map/all_to_all | solution.py:135
  32.1 3.4 %collective-permute-start = (bf16[32,2048]{1,0:T(8,128)(2,1)S(1)}, bf16[32,2048]{1,0:T(8,128)(2,1)S(1)}, u32[]{:S(2)}, u32[]{:S(2)}) collective-permute-start(bf16[32,2048]{1,0:T(8,128)(2,1)S(1)} %get-tuple-element.16), channel_id=1, source_target_pairs={{0,1},{1,0},{2,3},{3,2},{4,5},{5,4},{6,7},{7,6},{8,9},{9,8},{10,11... | collective-permute-start | bytes 393224 | tf_op jit(solution)/shard_map/ppermute | solution.py:120
  35.6 3.7 %collective-permute-start.1 = (bf16[32,2048]{1,0:T(8,128)(2,1)S(1)}, bf16[32,2048]{1,0:T(8,128)(2,1)S(1)}, u32[]{:S(2)}, u32[]{:S(2)}) collective-permute-start(bf16[32,2048]{1,0:T(8,128)(2,1)S(1)} %get-tuple-element.18), channel_id=1, source_target_pairs={{0,2},{1,3},{2,0},{3,1},{4,6},{5,7},{6,4},{7,5},{8,10},{9,11},{10,... | collective-permute-start | bytes 393224 | tf_op jit(solution)/shard_map/ppermute | solution.py:120
  39.2 2.1 %collective-permute-start.2 = (bf16[32,2048]{1,0:T(8,128)(2,1)S(1)}, bf16[32,2048]{1,0:T(8,128)(2,1)S(1)}, u32[]{:S(2)}, u32[]{:S(2)}) collective-permute-start(bf16[32,2048]{1,0:T(8,128)(2,1)S(1)} %get-tuple-element.15), channel_id=1, source_target_pairs={{0,3},{1,2},{2,1},{3,0},{4,7},{5,6},{6,5},{7,4},{8,11},{9,10},{10,... | collective-permute-start | bytes 393224 | tf_op jit(solution)/shard_map/ppermute | solution.py:120
  41.6 0.1 eq.31
  41.7 6.0 %collective-permute-done.1 = bf16[32,2048]{1,0:T(8,128)(2,1)S(1)} collective-permute-done((bf16[32,2048]{1,0:T(8,128)(2,1)S(1)}, bf16[32,2048]{1,0:T(8,128)(2,1)S(1)}, u32[]{:S(2)}, u32[]{:S(2)}) %collective-permute-start.1) | collective-permute-done | bytes 131104 | tf_op jit(solution)/shard_map/ppermute | solution.py:120
  47.7 2.9 %collective-permute-done.2 = bf16[32,2048]{1,0:T(8,128)(2,1)S(1)} collective-permute-done((bf16[32,2048]{1,0:T(8,128)(2,1)S(1)}, bf16[32,2048]{1,0:T(8,128)(2,1)S(1)}, u32[]{:S(2)}, u32[]{:S(2)}) %collective-permute-start.2) | collective-permute-done | bytes 131104 | tf_op jit(solution)/shard_map/ppermute | solution.py:120
  50.6 3.6 %collective-permute-start.3 = (bf16[128,512]{1,0:T(8,128)(2,1)S(1)}, bf16[128,512]{1,0:T(8,128)(2,1)S(1)}, u32[]{:S(2)}, u32[]{:S(2)}) collective-permute-start(bf16[128,512]{1,0:T(8,128)(2,1)S(1)} %bitcast.18), channel_id=1, source_target_pairs={{0,8},{4,12},{8,16},{12,20},{16,24},{20,28},{24,32},{28,36},{32,40... | collective-permute-start | bytes 393224 | tf_op jit(solution)/shard_map/ppermute | solution.py:142
  54.2 5.9 %collective-permute-start.4 = (bf16[128,512]{1,0:T(8,128)(2,1)S(1)}, bf16[128,512]{1,0:T(8,128)(2,1)S(1)}, u32[]{:S(2)}, u32[]{:S(2)}) collective-permute-start(bf16[128,512]{1,0:T(8,128)(2,1)S(1)} %bitcast.19), channel_id=1, source_target_pairs={{0,16},{4,20},{8,24},{12,28},{16,32},{20,36},{24,40},{28,44},{32,4... | collective-permute-start | bytes 393224 | tf_op jit(solution)/shard_map/ppermute | solution.py:142
  60.1 1.2 %fusion = bf16[16,8,2048]{2,1,0:T(8,128)(2,1)} fusion(bf16[32,2048]{1,0:T(8,128)(2,1)S(1)} %collective-permute-done.2, bf16[32,2048]{1,0:T(8,128)(2,1)S(1)} %collective-permute-done.1, bf16[32,2048]{1,0:T(8,128)(2,1)S(1)} %collective-permute-done, bf16[32,2048]{1,0:T(8,128)(2,1)S(1)} %get-tuple-element.10, s32[128]{0:T(128)S(1)} %get-tuple-element.26, ...), kind=kOutput, calls=%fused_computation.1 | convolution fusion | flops 69566464 | bytes 1051392 | tf_op jit(solution)/shard_map/dot_general | solution.py:131
  61.3 11.5 %all-to-all-start.2 = ((bf16[16,8,2048]{2,1,0:T(8,128)(2,1)}), bf16[16,8,2048]{2,1,0:T(8,128)(2,1)S(1)}, u32[]{:S(2)}, u32[]{:S(2)}) async-start(bf16[16,8,2048]{2,1,0:T(8,128)(2,1)} %fusion), calls=%async_computation.2 | async-start | bytes 1048576 | tf_op jit(solution)/shard_map/all_to_all | solution.py:139
  72.8 2.7 %collective-permute-start.5 = (bf16[128,512]{1,0:T(8,128)(2,1)S(1)}, bf16[128,512]{1,0:T(8,128)(2,1)S(1)}, u32[]{:S(2)}, u32[]{:S(2)}) collective-permute-start(bf16[128,512]{1,0:T(8,128)(2,1)S(1)} %collective-permute-done.4), channel_id=1, source_target_pairs={{0,8},{4,12},{8,16},{12,20},{16,24},{20,28},{24,32},{28,36},{32,40... | collective-permute-start | bytes 393224 | tf_op jit(solution)/shard_map/ppermute | solution.py:142
  75.5 2.9 %collective-permute-start.6 = (bf16[128,512]{1,0:T(8,128)(2,1)S(1)}, bf16[128,512]{1,0:T(8,128)(2,1)S(1)}, u32[]{:S(2)}, u32[]{:S(2)}) collective-permute-start(bf16[128,512]{1,0:T(8,128)(2,1)S(1)} %collective-permute-done.4), channel_id=1, source_target_pairs={{0,16},{4,20},{8,24},{12,28},{16,32},{20,36},{24,40},{28,44},{32,4... | collective-permute-start | bytes 393224 | tf_op jit(solution)/shard_map/ppermute | solution.py:142
  78.5 2.2 %collective-permute-done.5 = bf16[128,512]{1,0:T(8,128)(2,1)S(1)} collective-permute-done((bf16[128,512]{1,0:T(8,128)(2,1)S(1)}, bf16[128,512]{1,0:T(8,128)(2,1)S(1)}, u32[]{:S(2)}, u32[]{:S(2)}) %collective-permute-start.5) | collective-permute-done | bytes 131104 | tf_op jit(solution)/shard_map/ppermute | solution.py:142
  80.7 2.5 %collective-permute-done.6 = bf16[128,512]{1,0:T(8,128)(2,1)S(1)} collective-permute-done((bf16[128,512]{1,0:T(8,128)(2,1)S(1)}, bf16[128,512]{1,0:T(8,128)(2,1)S(1)}, u32[]{:S(2)}, u32[]{:S(2)}) %collective-permute-start.6) | collective-permute-done | bytes 131104 | tf_op jit(solution)/shard_map/ppermute | solution.py:142
  83.3 1.9 %collective-permute-start.7 = (bf16[512,512]{1,0:T(8,128)(2,1)S(1)}, bf16[512,512]{1,0:T(8,128)(2,1)S(1)}, u32[]{:S(2)}, u32[]{:S(2)}) collective-permute-start(bf16[512,512]{1,0:T(8,128)(2,1)S(1)} %constant_dynamic-slice_fusion), channel_id=1, source_target_pairs={{0,4},{4,0},{8,12},{12,8},{16,20},{20,16},{24,28},{28,24},{32,36},... | collective-permute-start | bytes 1572872 | tf_op jit(solution)/shard_map/ppermute | solution.py:148
  85.2 1.9 %collective-permute-done.7.sib = bf16[512,512]{1,0:T(8,128)(2,1)S(1)} collective-permute-done((bf16[512,512]{1,0:T(8,128)(2,1)S(1)}, bf16[512,512]{1,0:T(8,128)(2,1)S(1)}, u32[]{:S(2)}, u32[]{:S(2)}) %collective-permute-start.7) | collective-permute-done | bytes 524320 | tf_op jit(solution)/shard_map/ppermute | solution.py:148
  87.1 2.6 %all-to-all-done.2 = bf16[16,8,2048]{2,1,0:T(8,128)(2,1)S(1)} async-done(((bf16[16,8,2048]{2,1,0:T(8,128)(2,1)}), bf16[16,8,2048]{2,1,0:T(8,128)(2,1)S(1)}, u32[]{:S(2)}, u32[]{:S(2)}) %all-to-all-start.2) | async-done | bytes 524320 | tf_op jit(solution)/shard_map/all_to_all | solution.py:139
  89.7 5.3 %shard_map.56 = bf16[128,2048]{1,0:T(8,128)(2,1)} custom-call(s32[1,4]{1,0:T(1,128)S(1)} %copy-done, bf16[128,2048]{1,0:T(8,128)(2,1)S(1)} %bitcast.17, bf16[640,512]{1,0:T(8,128)(2,1)S(1)} %constant_dynamic-update-slice_fusion.own, bf16[512,512]{1,0:T(8,128)(2,1)S(1)} %collective-permute-done.7.sib), custom_call_target="tpu_custom_call" | custom-call | flops 1207959552 | bytes 2228224 | tf_op jit(solution)/shard_map/pallas_call | solution.py:67
  (24 shorter events, 0.5 us)
Async XLA Ops:
  0.0 6.8 %copy-start.2 = (s32[1,16]{1,0:T(1,128)S(1)}, s32[1,16]{1,0:T(1,128)}, u32[]{:S(2)}) copy-start(s32[1,16]{1,0:T(1,128)} %param.9) | copy-start | bytes 196
  1.6 30.5 %copy-start.1 = (bf16[32,8192]{1,0:T(8,128)(2,1)S(1)}, bf16[32,8192]{1,0:T(8,128)(2,1)}, u32[]{:S(2)}) copy-start(bf16[32,8192]{1,0:T(8,128)(2,1)} %param.5) | copy-start | bytes 1572868
  1.6 9.2 %all-to-all-start = ((bf16[4,32,512]{2,1,0:T(8,128)(2,1)}), bf16[4,32,512]{2,1,0:T(8,128)(2,1)S(1)}, u32[]{:S(2)}, u32[]{:S(2)}) async-start(bf16[4,32,512]{2,1,0:T(8,128)(2,1)} %shard_map.55), calls=%async_computation | async-start | bytes 262144 | tf_op jit(solution)/shard_map/all_to_all | solution.py:113
  11.7 38.9 %all-to-all-start.1 = ((bf16[16,8,512]{2,1,0:T(8,128)(2,1)}), bf16[16,8,512]{2,1,0:T(8,128)(2,1)S(1)}, u32[]{:S(2)}, u32[]{:S(2)}) async-start(bf16[16,8,512]{2,1,0:T(8,128)(2,1)} %fusion.1), calls=%async_computation.1 | async-start | bytes 262144 | tf_op jit(solution)/shard_map/all_to_all | solution.py:135
  32.1 9.6 %collective-permute-start = (bf16[32,2048]{1,0:T(8,128)(2,1)S(1)}, bf16[32,2048]{1,0:T(8,128)(2,1)S(1)}, u32[]{:S(2)}, u32[]{:S(2)}) collective-permute-start(bf16[32,2048]{1,0:T(8,128)(2,1)S(1)} %get-tuple-element.16), channel_id=1, source_target_pairs={{0,1},{1,0},{2,3},{3,2},{4,5},{5,4},{6,7},{7,6},{8,9},{9,8},{10,11... | collective-permute-start | bytes 393224 | tf_op jit(solution)/shard_map/ppermute | solution.py:120
  35.6 12.1 %collective-permute-start.1 = (bf16[32,2048]{1,0:T(8,128)(2,1)S(1)}, bf16[32,2048]{1,0:T(8,128)(2,1)S(1)}, u32[]{:S(2)}, u32[]{:S(2)}) collective-permute-start(bf16[32,2048]{1,0:T(8,128)(2,1)S(1)} %get-tuple-element.18), channel_id=1, source_target_pairs={{0,2},{1,3},{2,0},{3,1},{4,6},{5,7},{6,4},{7,5},{8,10},{9,11},{10,... | collective-permute-start | bytes 393224 | tf_op jit(solution)/shard_map/ppermute | solution.py:120
  39.2 11.3 %collective-permute-start.2 = (bf16[32,2048]{1,0:T(8,128)(2,1)S(1)}, bf16[32,2048]{1,0:T(8,128)(2,1)S(1)}, u32[]{:S(2)}, u32[]{:S(2)}) collective-permute-start(bf16[32,2048]{1,0:T(8,128)(2,1)S(1)} %get-tuple-element.15), channel_id=1, source_target_pairs={{0,3},{1,2},{2,1},{3,0},{4,7},{5,6},{6,5},{7,4},{8,11},{9,10},{10,... | collective-permute-start | bytes 393224 | tf_op jit(solution)/shard_map/ppermute | solution.py:120
  50.6 27.9 %collective-permute-start.3 = (bf16[128,512]{1,0:T(8,128)(2,1)S(1)}, bf16[128,512]{1,0:T(8,128)(2,1)S(1)}, u32[]{:S(2)}, u32[]{:S(2)}) collective-permute-start(bf16[128,512]{1,0:T(8,128)(2,1)S(1)} %bitcast.18), channel_id=1, source_target_pairs={{0,8},{4,12},{8,16},{12,20},{16,24},{20,28},{24,32},{28,36},{32,40... | collective-permute-start | bytes 393224 | tf_op jit(solution)/shard_map/ppermute | solution.py:142
  54.2 18.6 %collective-permute-start.4 = (bf16[128,512]{1,0:T(8,128)(2,1)S(1)}, bf16[128,512]{1,0:T(8,128)(2,1)S(1)}, u32[]{:S(2)}, u32[]{:S(2)}) collective-permute-start(bf16[128,512]{1,0:T(8,128)(2,1)S(1)} %bitcast.19), channel_id=1, source_target_pairs={{0,16},{4,20},{8,24},{12,28},{16,32},{20,36},{24,40},{28,44},{32,4... | collective-permute-start | bytes 393224 | tf_op jit(solution)/shard_map/ppermute | solution.py:142
  61.3 28.4 %all-to-all-start.2 = ((bf16[16,8,2048]{2,1,0:T(8,128)(2,1)}), bf16[16,8,2048]{2,1,0:T(8,128)(2,1)S(1)}, u32[]{:S(2)}, u32[]{:S(2)}) async-start(bf16[16,8,2048]{2,1,0:T(8,128)(2,1)} %fusion), calls=%async_computation.2 | async-start | bytes 1048576 | tf_op jit(solution)/shard_map/all_to_all | solution.py:139
  72.8 7.8 %collective-permute-start.5 = (bf16[128,512]{1,0:T(8,128)(2,1)S(1)}, bf16[128,512]{1,0:T(8,128)(2,1)S(1)}, u32[]{:S(2)}, u32[]{:S(2)}) collective-permute-start(bf16[128,512]{1,0:T(8,128)(2,1)S(1)} %collective-permute-done.4), channel_id=1, source_target_pairs={{0,8},{4,12},{8,16},{12,20},{16,24},{20,28},{24,32},{28,36},{32,40... | collective-permute-start | bytes 393224 | tf_op jit(solution)/shard_map/ppermute | solution.py:142
  75.5 7.7 %collective-permute-start.6 = (bf16[128,512]{1,0:T(8,128)(2,1)S(1)}, bf16[128,512]{1,0:T(8,128)(2,1)S(1)}, u32[]{:S(2)}, u32[]{:S(2)}) collective-permute-start(bf16[128,512]{1,0:T(8,128)(2,1)S(1)} %collective-permute-done.4), channel_id=1, source_target_pairs={{0,16},{4,20},{8,24},{12,28},{16,32},{20,36},{24,40},{28,44},{32,4... | collective-permute-start | bytes 393224 | tf_op jit(solution)/shard_map/ppermute | solution.py:142
  83.3 6.4 %copy-start = (s32[1,4]{1,0:T(1,128)S(1)}, s32[1,4]{1,0:T(1,128)}, u32[]{:S(2)}) copy-start(s32[1,4]{1,0:T(1,128)} %lengths.1) | copy-start | bytes 52
  83.3 3.8 %collective-permute-start.7 = (bf16[512,512]{1,0:T(8,128)(2,1)S(1)}, bf16[512,512]{1,0:T(8,128)(2,1)S(1)}, u32[]{:S(2)}, u32[]{:S(2)}) collective-permute-start(bf16[512,512]{1,0:T(8,128)(2,1)S(1)} %constant_dynamic-slice_fusion), channel_id=1, source_target_pairs={{0,4},{4,0},{8,12},{12,8},{16,20},{20,16},{24,28},{28,24},{32,36},... | collective-permute-start | bytes 1572872 | tf_op jit(solution)/shard_map/ppermute | solution.py:148

commit v5 on v4

--- a/solution.py
+++ b/solution.py
@@ -112,14 +112,18 @@
     packed = pack((key_rows, value_rows), tp)
     held_kv = lax.all_to_all(packed, "tp", 0, 0, tiled=True).reshape(rows, -1)
     q_width = queries.shape[1] // tp
-    pieces, arrived = [], []
-    for d in range(tp):
-        other = me ^ d
-        piece = lax.dynamic_slice_in_dim(queries, other * q_width, q_width, axis=1)
-        if d:
-            piece = lax.ppermute(piece, "tp", [(i, i ^ d) for i in range(tp)])
-        pieces.append(piece)
-        arrived.append(lax.dynamic_slice_in_dim(block_table[0], other * blocks, blocks))
+    def columns(device):
+        return lax.dynamic_slice_in_dim(queries, device * q_width, q_width, axis=1)
+
+    half = tp // 2
+    away = jnp.concatenate([columns(me ^ d) for d in range(half, tp)], axis=0)
+    come = lax.ppermute(away, "tp", [(i, i ^ half) for i in range(tp)])
+    near = [[columns(me ^ d), come[d * part : (d + 1) * part]] for d in range(half)]
+    distances, pieces = [0, half], list(near[0])
+    for d in range(1, half):
+        distances += [d, d ^ half]
+        pieces += [lax.ppermute(x, "tp", [(i, i ^ d) for i in range(tp)]) for x in near[d]]
+    arrived = [lax.dynamic_slice_in_dim(block_table[0], (me ^ d) * blocks, blocks) for d in distances]
 
     def order(destination):
         wide = jnp.broadcast_to(destination[:, None], (groups, block)).reshape(rows)

time: 95.8 us -> 89.4 us (0.933)
  the two profiles are of different devices: /device:TPU:20 before, /device:TPU:57 now
where the time goes in v5:
time: 89.4 us; the launch traced here: 88.8 us
  starting transfers between devices  66.1 us (74%)
  waiting for transfers between devices  11.9 us (13%)
  Pallas kernels  6.94 us (8%)
  matrix products  2.14 us (2%)
  local copies, waits for them, and re-layouts  1.23 us (1%)
    all_to_all x1, starting transfers between devices, shards(): kv = lax.all_to_all(kv_sorted, 'grp', 0, 0, tiled=True).reshape(rows, -1)  21.5 us
    ppermute x4, starting transfers between devices, ahead(): lax.ppermute(x, 'seq', [(i, i + 2 * chips) for i in range(seq - 2 * chips)])  11.6 us
    all_to_all x1, starting transfers between devices, shards(): q = lax.all_to_all(q_sorted, 'grp', 0, 0, tiled=True).reshape(rows, -1)  11.1 us
    ppermute x1, starting transfers between devices, shards(): sib = lax.ppermute(given, 'seq', [(i, i ^ 1) for i in range(seq)])  9.17 us
    ppermute x4, waiting for transfers between devices, ahead(): lax.ppermute(x, 'seq', [(i, i + 2 * chips) for i in range(seq - 2 * chips)])  6.32 us
    pallas_call x1, Pallas kernels, attention(): pl.pallas_call(attend, out_shape=jax.ShapeDtypeStruct(q.shape, jnp.bfloat...  5.34 us
    ppermute x2, starting transfers between devices, shards(): lax.ppermute(x, 'tp', [(i, i ^ d) for i in range(tp)])  5.28 us
    ppermute x1, starting transfers between devices, shards(): come = lax.ppermute(away, 'tp', [(i, i ^ half) for i in range(tp)])  4.2 us
  transfers between devices with their start and end apart: 11, of which 5 were waited for; matrix products, arithmetic and copies ran while one was open for 3% of the time, Pallas kernels for 0%

profile of v5, /device:TPU:57, one launch (start us, length us, event | category | flops | bytes accessed | tf_op | source)
XLA Modules:
  0.0 88.8 jit_solution(5402145624159387863)
XLA Ops:
  0.0 1.6 %shard_map.55 = bf16[4,32,512]{2,1,0:T(8,128)(2,1)} custom-call(bf16[32,1024]{1,0:T(8,128)(2,1)} %refs_0_.1, bf16[32,1024]{1,0:T(8,128)(2,1)} %refs_1_.1), custom_call_target="tpu_custom_call" | custom-call | tf_op jit(solution)/shard_map/pallas_call | solution.py:97
  1.6 3.3 %all-to-all-start = ((bf16[4,32,512]{2,1,0:T(8,128)(2,1)}), bf16[4,32,512]{2,1,0:T(8,128)(2,1)S(1)}, u32[]{:S(2)}, u32[]{:S(2)}) async-start(bf16[4,32,512]{2,1,0:T(8,128)(2,1)} %shard_map.55), calls=%async_computation | async-start | bytes 262144 | tf_op jit(solution)/shard_map/all_to_all | solution.py:113
  5.0 4.2 %collective-permute-start = (bf16[64,2048]{1,0:T(8,128)(2,1)S(1)}, bf16[64,2048]{1,0:T(8,128)(2,1)S(1)}, u32[]{:S(2)}, u32[]{:S(2)}) collective-permute-start(bf16[64,2048]{1,0:T(8,128)(2,1)S(1)} %pad_maximum_fusion), channel_id=1, source_target_pairs={{0,2},{1,3},{2,0},{3,1},{4,6},{5,7},{6,4},{7,5},{8,10},{9,11},{10,... | collective-permute-start | bytes 786440 | tf_op jit(solution)/shard_map/ppermute | solution.py:120
  9.2 3.1 %collective-permute-start.1 = (bf16[32,2048]{1,0:T(8,128)(2,1)S(1)}, bf16[32,2048]{1,0:T(8,128)(2,1)S(1)}, u32[]{:S(2)}, u32[]{:S(2)}) collective-permute-start(bf16[32,2048]{1,0:T(8,128)(2,1)S(1)} %get-tuple-element.15), channel_id=1, source_target_pairs={{0,1},{1,0},{2,3},{3,2},{4,5},{5,4},{6,7},{7,6},{8,9},{9,8},{10,11... | collective-permute-start | bytes 393224 | tf_op jit(solution)/shard_map/ppermute | solution.py:125
  12.4 0.6 copy-done.2
  13.1 0.1 eq.35
  13.3 0.9 %fusion.1 = bf16[16,8,512]{2,1,0:T(8,128)(2,1)} fusion(bf16[128,512]{1,0:T(8,128)(2,1)S(1)} %bitcast.21, s32[128]{0:T(128)S(1)} %eq.35, s32[128]{0:T(128)S(1)} %get-tuple-element.28, s32[128]{0:T(128)S(1)} %get-tuple-element.29, s32[128]{0:T(128)S(1)} %get-tuple-element.27, s32[128]{0:T(128)S(1)} %get-tuple-element.30, ...), kind=kOutput, calls=%fused_computation.3 | convolution fusion | flops 16941056 | bytes 264960 | tf_op jit(solution)/shard_map/dot_general | solution.py:135
  14.2 21.5 %all-to-all-start.1 = ((bf16[16,8,512]{2,1,0:T(8,128)(2,1)}), bf16[16,8,512]{2,1,0:T(8,128)(2,1)S(1)}, u32[]{:S(2)}, u32[]{:S(2)}) async-start(bf16[16,8,512]{2,1,0:T(8,128)(2,1)} %fusion.1), calls=%async_computation.1 | async-start | bytes 262144 | tf_op jit(solution)/shard_map/all_to_all | solution.py:139
  35.7 2.2 %collective-permute-start.2 = (bf16[32,2048]{1,0:T(8,128)(2,1)S(1)}, bf16[32,2048]{1,0:T(8,128)(2,1)S(1)}, u32[]{:S(2)}, u32[]{:S(2)}) collective-permute-start(bf16[32,2048]{1,0:T(8,128)(2,1)S(1)} %get-tuple-element.19), channel_id=1, source_target_pairs={{0,1},{1,0},{2,3},{3,2},{4,5},{5,4},{6,7},{7,6},{8,9},{9,8},{10,11... | collective-permute-start | bytes 393224 | tf_op jit(solution)/shard_map/ppermute | solution.py:125
  37.9 0.1 fusion.33
  38.2 0.1 eq.31
  38.3 4.0 %collective-permute-done.2 = bf16[32,2048]{1,0:T(8,128)(2,1)S(1)} collective-permute-done((bf16[32,2048]{1,0:T(8,128)(2,1)S(1)}, bf16[32,2048]{1,0:T(8,128)(2,1)S(1)}, u32[]{:S(2)}, u32[]{:S(2)}) %collective-permute-start.2) | collective-permute-done | bytes 131104 | tf_op jit(solution)/shard_map/ppermute | solution.py:125
  42.2 0.1 all-to-all-done.1
  42.4 4.5 %collective-permute-start.3 = (bf16[128,512]{1,0:T(8,128)(2,1)S(1)}, bf16[128,512]{1,0:T(8,128)(2,1)S(1)}, u32[]{:S(2)}, u32[]{:S(2)}) collective-permute-start(bf16[128,512]{1,0:T(8,128)(2,1)S(1)} %bitcast.18), channel_id=1, source_target_pairs={{0,8},{4,12},{8,16},{12,20},{16,24},{20,28},{24,32},{28,36},{32,40... | collective-permute-start | bytes 393224 | tf_op jit(solution)/shard_map/ppermute | solution.py:146
  46.9 2.7 %collective-permute-start.4 = (bf16[128,512]{1,0:T(8,128)(2,1)S(1)}, bf16[128,512]{1,0:T(8,128)(2,1)S(1)}, u32[]{:S(2)}, u32[]{:S(2)}) collective-permute-start(bf16[128,512]{1,0:T(8,128)(2,1)S(1)} %bitcast.19), channel_id=1, source_target_pairs={{0,16},{4,20},{8,24},{12,28},{16,32},{20,36},{24,40},{28,44},{32,4... | collective-permute-start | bytes 393224 | tf_op jit(solution)/shard_map/ppermute | solution.py:146
  49.6 1.2 %fusion = bf16[16,8,2048]{2,1,0:T(8,128)(2,1)} fusion(bf16[32,2048]{1,0:T(8,128)(2,1)S(1)} %collective-permute-done.2, bf16[32,2048]{1,0:T(8,128)(2,1)S(1)} %collective-permute-done.1, bf16[32,2048]{1,0:T(8,128)(2,1)S(1)} %get-tuple-element.11, bf16[32,2048]{1,0:T(8,128)(2,1)S(1)} %get-tuple-element.10, s32[128]{0:T(128)S(1)} %get-tuple-element.28, ...), kind=kOutput, calls=%fused_computation.1 | convolution fusion | flops 69566464 | bytes 1051392 | tf_op jit(solution)/shard_map/dot_general | solution.py:135
  50.8 11.1 %all-to-all-start.2 = ((bf16[16,8,2048]{2,1,0:T(8,128)(2,1)}), bf16[16,8,2048]{2,1,0:T(8,128)(2,1)S(1)}, u32[]{:S(2)}, u32[]{:S(2)}) async-start(bf16[16,8,2048]{2,1,0:T(8,128)(2,1)} %fusion), calls=%async_computation.2 | async-start | bytes 1048576 | tf_op jit(solution)/shard_map/all_to_all | solution.py:143
  61.9 2.4 %collective-permute-start.5 = (bf16[128,512]{1,0:T(8,128)(2,1)S(1)}, bf16[128,512]{1,0:T(8,128)(2,1)S(1)}, u32[]{:S(2)}, u32[]{:S(2)}) collective-permute-start(bf16[128,512]{1,0:T(8,128)(2,1)S(1)} %collective-permute-done.4), channel_id=1, source_target_pairs={{0,8},{4,12},{8,16},{12,20},{16,24},{20,28},{24,32},{28,36},{32,40... | collective-permute-start | bytes 393224 | tf_op jit(solution)/shard_map/ppermute | solution.py:146
  64.4 1.9 %collective-permute-start.6 = (bf16[128,512]{1,0:T(8,128)(2,1)S(1)}, bf16[128,512]{1,0:T(8,128)(2,1)S(1)}, u32[]{:S(2)}, u32[]{:S(2)}) collective-permute-start(bf16[128,512]{1,0:T(8,128)(2,1)S(1)} %collective-permute-done.4), channel_id=1, source_target_pairs={{0,16},{4,20},{8,24},{12,28},{16,32},{20,36},{24,40},{28,44},{32,4... | collective-permute-start | bytes 393224 | tf_op jit(solution)/shard_map/ppermute | solution.py:146
  66.3 1.6 %collective-permute-done.5 = bf16[128,512]{1,0:T(8,128)(2,1)S(1)} collective-permute-done((bf16[128,512]{1,0:T(8,128)(2,1)S(1)}, bf16[128,512]{1,0:T(8,128)(2,1)S(1)}, u32[]{:S(2)}, u32[]{:S(2)}) %collective-permute-start.5) | collective-permute-done | bytes 131104 | tf_op jit(solution)/shard_map/ppermute | solution.py:146
  68.0 4.7 %collective-permute-done.6 = bf16[128,512]{1,0:T(8,128)(2,1)S(1)} collective-permute-done((bf16[128,512]{1,0:T(8,128)(2,1)S(1)}, bf16[128,512]{1,0:T(8,128)(2,1)S(1)}, u32[]{:S(2)}, u32[]{:S(2)}) %collective-permute-start.6) | collective-permute-done | bytes 131104 | tf_op jit(solution)/shard_map/ppermute | solution.py:146
  72.8 9.2 %collective-permute-start.7 = (bf16[512,512]{1,0:T(8,128)(2,1)S(1)}, bf16[512,512]{1,0:T(8,128)(2,1)S(1)}, u32[]{:S(2)}, u32[]{:S(2)}) collective-permute-start(bf16[512,512]{1,0:T(8,128)(2,1)S(1)} %constant_dynamic-slice_fusion), channel_id=1, source_target_pairs={{0,4},{4,0},{8,12},{12,8},{16,20},{20,16},{24,28},{28,24},{32,36},... | collective-permute-start | bytes 1572872 | tf_op jit(solution)/shard_map/ppermute | solution.py:152
  81.9 1.5 %collective-permute-done.7.sib = bf16[512,512]{1,0:T(8,128)(2,1)S(1)} collective-permute-done((bf16[512,512]{1,0:T(8,128)(2,1)S(1)}, bf16[512,512]{1,0:T(8,128)(2,1)S(1)}, u32[]{:S(2)}, u32[]{:S(2)}) %collective-permute-start.7) | collective-permute-done | bytes 524320 | tf_op jit(solution)/shard_map/ppermute | solution.py:152
  83.4 5.3 %shard_map.56 = bf16[128,2048]{1,0:T(8,128)(2,1)} custom-call(s32[1,4]{1,0:T(1,128)S(1)} %copy-done, bf16[128,2048]{1,0:T(8,128)(2,1)S(1)} %bitcast.17, bf16[640,512]{1,0:T(8,128)(2,1)S(1)} %constant_dynamic-update-slice_fusion.own, bf16[512,512]{1,0:T(8,128)(2,1)S(1)} %collective-permute-done.7.sib), custom_call_target="tpu_custom_call" | custom-call | flops 1207959552 | bytes 2228224 | tf_op jit(solution)/shard_map/pallas_call | solution.py:67
  (26 shorter events, 0.5 us)
Async XLA Ops:
  0.0 5.0 %copy-start.1 = (bf16[32,8192]{1,0:T(8,128)(2,1)S(1)}, bf16[32,8192]{1,0:T(8,128)(2,1)}, u32[]{:S(2)}) copy-start(bf16[32,8192]{1,0:T(8,128)(2,1)} %param.5) | copy-start | bytes 1572868
  1.6 11.6 %all-to-all-start = ((bf16[4,32,512]{2,1,0:T(8,128)(2,1)}), bf16[4,32,512]{2,1,0:T(8,128)(2,1)S(1)}, u32[]{:S(2)}, u32[]{:S(2)}) async-start(bf16[4,32,512]{2,1,0:T(8,128)(2,1)} %shard_map.55), calls=%async_computation | async-start | bytes 262144 | tf_op jit(solution)/shard_map/all_to_all | solution.py:113
  5.0 30.7 %collective-permute-start = (bf16[64,2048]{1,0:T(8,128)(2,1)S(1)}, bf16[64,2048]{1,0:T(8,128)(2,1)S(1)}, u32[]{:S(2)}, u32[]{:S(2)}) collective-permute-start(bf16[64,2048]{1,0:T(8,128)(2,1)S(1)} %pad_maximum_fusion), channel_id=1, source_target_pairs={{0,2},{1,3},{2,0},{3,1},{4,6},{5,7},{6,4},{7,5},{8,10},{9,11},{10,... | collective-permute-start | bytes 786440 | tf_op jit(solution)/shard_map/ppermute | solution.py:120
  9.2 29.0 %collective-permute-start.1 = (bf16[32,2048]{1,0:T(8,128)(2,1)S(1)}, bf16[32,2048]{1,0:T(8,128)(2,1)S(1)}, u32[]{:S(2)}, u32[]{:S(2)}) collective-permute-start(bf16[32,2048]{1,0:T(8,128)(2,1)S(1)} %get-tuple-element.15), channel_id=1, source_target_pairs={{0,1},{1,0},{2,3},{3,2},{4,5},{5,4},{6,7},{7,6},{8,9},{9,8},{10,11... | collective-permute-start | bytes 393224 | tf_op jit(solution)/shard_map/ppermute | solution.py:125
  12.4 0.7 copy-start.2
  14.2 28.2 %all-to-all-start.1 = ((bf16[16,8,512]{2,1,0:T(8,128)(2,1)}), bf16[16,8,512]{2,1,0:T(8,128)(2,1)S(1)}, u32[]{:S(2)}, u32[]{:S(2)}) async-start(bf16[16,8,512]{2,1,0:T(8,128)(2,1)} %fusion.1), calls=%async_computation.1 | async-start | bytes 262144 | tf_op jit(solution)/shard_map/all_to_all | solution.py:139
  35.7 6.5 %collective-permute-start.2 = (bf16[32,2048]{1,0:T(8,128)(2,1)S(1)}, bf16[32,2048]{1,0:T(8,128)(2,1)S(1)}, u32[]{:S(2)}, u32[]{:S(2)}) collective-permute-start(bf16[32,2048]{1,0:T(8,128)(2,1)S(1)} %get-tuple-element.19), channel_id=1, source_target_pairs={{0,1},{1,0},{2,3},{3,2},{4,5},{5,4},{6,7},{7,6},{8,9},{9,8},{10,11... | collective-permute-start | bytes 393224 | tf_op jit(solution)/shard_map/ppermute | solution.py:125
  42.4 23.9 %collective-permute-start.3 = (bf16[128,512]{1,0:T(8,128)(2,1)S(1)}, bf16[128,512]{1,0:T(8,128)(2,1)S(1)}, u32[]{:S(2)}, u32[]{:S(2)}) collective-permute-start(bf16[128,512]{1,0:T(8,128)(2,1)S(1)} %bitcast.18), channel_id=1, source_target_pairs={{0,8},{4,12},{8,16},{12,20},{16,24},{20,28},{24,32},{28,36},{32,40... | collective-permute-start | bytes 393224 | tf_op jit(solution)/shard_map/ppermute | solution.py:146
  46.9 15.0 %collective-permute-start.4 = (bf16[128,512]{1,0:T(8,128)(2,1)S(1)}, bf16[128,512]{1,0:T(8,128)(2,1)S(1)}, u32[]{:S(2)}, u32[]{:S(2)}) collective-permute-start(bf16[128,512]{1,0:T(8,128)(2,1)S(1)} %bitcast.19), channel_id=1, source_target_pairs={{0,16},{4,20},{8,24},{12,28},{16,32},{20,36},{24,40},{28,44},{32,4... | collective-permute-start | bytes 393224 | tf_op jit(solution)/shard_map/ppermute | solution.py:146
  50.8 32.6 %all-to-all-start.2 = ((bf16[16,8,2048]{2,1,0:T(8,128)(2,1)}), bf16[16,8,2048]{2,1,0:T(8,128)(2,1)S(1)}, u32[]{:S(2)}, u32[]{:S(2)}) async-start(bf16[16,8,2048]{2,1,0:T(8,128)(2,1)} %fusion), calls=%async_computation.2 | async-start | bytes 1048576 | tf_op jit(solution)/shard_map/all_to_all | solution.py:143
  61.9 6.0 %collective-permute-start.5 = (bf16[128,512]{1,0:T(8,128)(2,1)S(1)}, bf16[128,512]{1,0:T(8,128)(2,1)S(1)}, u32[]{:S(2)}, u32[]{:S(2)}) collective-permute-start(bf16[128,512]{1,0:T(8,128)(2,1)S(1)} %collective-permute-done.4), channel_id=1, source_target_pairs={{0,8},{4,12},{8,16},{12,20},{16,24},{20,28},{24,32},{28,36},{32,40... | collective-permute-start | bytes 393224 | tf_op jit(solution)/shard_map/ppermute | solution.py:146
  64.4 8.3 %collective-permute-start.6 = (bf16[128,512]{1,0:T(8,128)(2,1)S(1)}, bf16[128,512]{1,0:T(8,128)(2,1)S(1)}, u32[]{:S(2)}, u32[]{:S(2)}) collective-permute-start(bf16[128,512]{1,0:T(8,128)(2,1)S(1)} %collective-permute-done.4), channel_id=1, source_target_pairs={{0,16},{4,20},{8,24},{12,28},{16,32},{20,36},{24,40},{28,44},{32,4... | collective-permute-start | bytes 393224 | tf_op jit(solution)/shard_map/ppermute | solution.py:146
  72.7 10.7 %copy-start = (s32[1,4]{1,0:T(1,128)S(1)}, s32[1,4]{1,0:T(1,128)}, u32[]{:S(2)}) copy-start(s32[1,4]{1,0:T(1,128)} %lengths.1) | copy-start | bytes 52
  72.8 10.7 %collective-permute-start.7 = (bf16[512,512]{1,0:T(8,128)(2,1)S(1)}, bf16[512,512]{1,0:T(8,128)(2,1)S(1)}, u32[]{:S(2)}, u32[]{:S(2)}) collective-permute-start(bf16[512,512]{1,0:T(8,128)(2,1)S(1)} %constant_dynamic-slice_fusion), channel_id=1, source_target_pairs={{0,4},{4,0},{8,12},{12,8},{16,20},{20,16},{24,28},{28,24},{32,36},... | collective-permute-start | bytes 1572872 | tf_op jit(solution)/shard_map/ppermute | solution.py:152

commit v6 on v4

--- a/solution.py
+++ b/solution.py
@@ -133,15 +133,15 @@
 
     kv_sorted = sort(order(block_table[0]), held_kv)
     kv = lax.all_to_all(kv_sorted, "grp", 0, 0, tiled=True).reshape(rows, -1)
-    kv, *pieces = lax.optimization_barrier((kv, *pieces))
+    def ahead(x, chips):
+        return lax.ppermute(x, "seq", [(i, i + 2 * chips) for i in range(seq - 2 * chips)])
+
+    back2, back1 = ahead(kv, 2), ahead(kv, 1)
+    back1, *pieces = lax.optimization_barrier((back1, *pieces))
     held_q = jnp.concatenate(pieces, axis=0)
     q_sorted = sort(order(jnp.concatenate(arrived)), held_q)
     q = lax.all_to_all(q_sorted, "grp", 0, 0, tiled=True).reshape(rows, -1)
 
-    def ahead(x, chips):
-        return lax.ppermute(x, "seq", [(i, i + 2 * chips) for i in range(seq - 2 * chips)])
-
-    back2, back1 = ahead(kv, 2), ahead(kv, 1)
     own = jnp.concatenate([kv, back1, back2, ahead(back2, 1), ahead(back2, 2)], axis=0)
     shard = lax.axis_index("seq")
     given = lax.dynamic_slice_in_dim(own, lax.rem(shard, 2) * rows, 4 * rows, 0)

time: 95.8 us -> 93 us (0.971)
  the two profiles are of different devices: /device:TPU:20 before, /device:TPU:63 now
where the time goes in v6:
time: 93 us; the launch traced here: 92.4 us
  starting transfers between devices  70.8 us (76%)
  waiting for transfers between devices  11.6 us (12%)
  Pallas kernels  6.89 us (7%)
  matrix products  2.14 us (2%)
    all_to_all x1, starting transfers between devices, shards(): kv = lax.all_to_all(kv_sorted, 'grp', 0, 0, tiled=True).reshape(rows, -1)  21.5 us
    ppermute x4, starting transfers between devices, ahead(): lax.ppermute(x, 'seq', [(i, i + 2 * chips) for i in range(seq - 2 * chips)])  13.4 us
    all_to_all x1, starting transfers between devices, shards(): q = lax.all_to_all(q_sorted, 'grp', 0, 0, tiled=True).reshape(rows, -1)  11.5 us
    ppermute x3, starting transfers between devices, shards(): piece = lax.ppermute(piece, 'tp', [(i, i ^ d) for i in range(tp)])  9.27 us
    ppermute x1, starting transfers between devices, shards(): sib = lax.ppermute(given, 'seq', [(i, i ^ 1) for i in range(seq)])  8.83 us
    ppermute x4, waiting for transfers between devices, ahead(): lax.ppermute(x, 'seq', [(i, i + 2 * chips) for i in range(seq - 2 * chips)])  6.5 us
    all_to_all x1, starting transfers between devices, shards(): held_kv = lax.all_to_all(packed, 'tp', 0, 0, tiled=True).reshape(rows, -1)  6.32 us
    pallas_call x1, Pallas kernels, attention(): pl.pallas_call(attend, out_shape=jax.ShapeDtypeStruct(q.shape, jnp.bfloat...  5.34 us
  transfers between devices with their start and end apart: 11, of which 3 were waited for; matrix products, arithmetic and copies ran while one was open for 2% of the time, Pallas kernels for 0%

profile of v6, /device:TPU:63, one launch (start us, length us, event | category | flops | bytes accessed | tf_op | source)
XLA Modules:
  0.0 92.4 jit_solution(13683326206096649170)
XLA Ops:
  0.0 1.5 %shard_map.55 = bf16[4,32,512]{2,1,0:T(8,128)(2,1)} custom-call(bf16[32,1024]{1,0:T(8,128)(2,1)} %refs_0_.1, bf16[32,1024]{1,0:T(8,128)(2,1)} %refs_1_.1), custom_call_target="tpu_custom_call" | custom-call | tf_op jit(solution)/shard_map/pallas_call | solution.py:97
  1.6 6.3 %all-to-all-start = ((bf16[4,32,512]{2,1,0:T(8,128)(2,1)}), bf16[4,32,512]{2,1,0:T(8,128)(2,1)S(1)}, u32[]{:S(2)}, u32[]{:S(2)}) async-start(bf16[4,32,512]{2,1,0:T(8,128)(2,1)} %shard_map.55), calls=%async_computation | async-start | bytes 262144 | tf_op jit(solution)/shard_map/all_to_all | solution.py:113
  7.9 0.1 broadcast_in_dim.15
  8.0 0.1 eq.35
  8.1 3.6 %all-to-all-done = bf16[4,32,512]{2,1,0:T(8,128)(2,1)S(1)} async-done(((bf16[4,32,512]{2,1,0:T(8,128)(2,1)}), bf16[4,32,512]{2,1,0:T(8,128)(2,1)S(1)}, u32[]{:S(2)}, u32[]{:S(2)}) %all-to-all-start) | async-done | bytes 131104 | tf_op jit(solution)/shard_map/all_to_all | solution.py:113
  11.7 0.9 %fusion.1 = bf16[16,8,512]{2,1,0:T(8,128)(2,1)} fusion(bf16[128,512]{1,0:T(8,128)(2,1)S(1)} %bitcast.21, s32[128]{0:T(128)S(1)} %eq.35, s32[128]{0:T(128)S(1)} %get-tuple-element.26, s32[128]{0:T(128)S(1)} %get-tuple-element.27, s32[128]{0:T(128)S(1)} %get-tuple-element.25, s32[128]{0:T(128)S(1)} %get-tuple-element.28, ...), kind=kOutput, calls=%fused_computation.3 | convolution fusion | flops 16941056 | bytes 264960 | tf_op jit(solution)/shard_map/dot_general | solution.py:131
  12.6 21.5 %all-to-all-start.1 = ((bf16[16,8,512]{2,1,0:T(8,128)(2,1)}), bf16[16,8,512]{2,1,0:T(8,128)(2,1)S(1)}, u32[]{:S(2)}, u32[]{:S(2)}) async-start(bf16[16,8,512]{2,1,0:T(8,128)(2,1)} %fusion.1), calls=%async_computation.1 | async-start | bytes 262144 | tf_op jit(solution)/shard_map/all_to_all | solution.py:135
  34.2 1.9 %collective-permute-start.1 = (bf16[32,2048]{1,0:T(8,128)(2,1)S(1)}, bf16[32,2048]{1,0:T(8,128)(2,1)S(1)}, u32[]{:S(2)}, u32[]{:S(2)}) collective-permute-start(bf16[32,2048]{1,0:T(8,128)(2,1)S(1)} %get-tuple-element.16), channel_id=1, source_target_pairs={{0,1},{1,0},{2,3},{3,2},{4,5},{5,4},{6,7},{7,6},{8,9},{9,8},{10,11... | collective-permute-start | bytes 393224 | tf_op jit(solution)/shard_map/ppermute | solution.py:120
  36.1 3.2 %collective-permute-start.2 = (bf16[32,2048]{1,0:T(8,128)(2,1)S(1)}, bf16[32,2048]{1,0:T(8,128)(2,1)S(1)}, u32[]{:S(2)}, u32[]{:S(2)}) collective-permute-start(bf16[32,2048]{1,0:T(8,128)(2,1)S(1)} %get-tuple-element.18), channel_id=1, source_target_pairs={{0,2},{1,3},{2,0},{3,1},{4,6},{5,7},{6,4},{7,5},{8,10},{9,11},{10,... | collective-permute-start | bytes 393224 | tf_op jit(solution)/shard_map/ppermute | solution.py:120
  39.3 4.2 %collective-permute-start.3 = (bf16[32,2048]{1,0:T(8,128)(2,1)S(1)}, bf16[32,2048]{1,0:T(8,128)(2,1)S(1)}, u32[]{:S(2)}, u32[]{:S(2)}) collective-permute-start(bf16[32,2048]{1,0:T(8,128)(2,1)S(1)} %get-tuple-element.15), channel_id=1, source_target_pairs={{0,3},{1,2},{2,1},{3,0},{4,7},{5,6},{6,5},{7,4},{8,11},{9,10},{10,... | collective-permute-start | bytes 393224 | tf_op jit(solution)/shard_map/ppermute | solution.py:120
  43.5 0.1 fusion.33
  43.6 0.1 pad_add_fusion
  43.7 0.1 broadcast_in_dim.6
  43.7 0.1 eq.31
  43.9 4.5 %collective-permute-start = (bf16[128,512]{1,0:T(8,128)(2,1)S(1)}, bf16[128,512]{1,0:T(8,128)(2,1)S(1)}, u32[]{:S(2)}, u32[]{:S(2)}) collective-permute-start(bf16[128,512]{1,0:T(8,128)(2,1)S(1)} %bitcast.19), channel_id=1, source_target_pairs={{0,8},{4,12},{8,16},{12,20},{16,24},{20,28},{24,32},{28,36},{32,40... | collective-permute-start | bytes 393224 | tf_op jit(solution)/shard_map/ppermute | solution.py:137
  48.4 2.6 %collective-permute-start.4 = (bf16[128,512]{1,0:T(8,128)(2,1)S(1)}, bf16[128,512]{1,0:T(8,128)(2,1)S(1)}, u32[]{:S(2)}, u32[]{:S(2)}) collective-permute-start(bf16[128,512]{1,0:T(8,128)(2,1)S(1)} %bitcast.20), channel_id=1, source_target_pairs={{0,16},{4,20},{8,24},{12,28},{16,32},{20,36},{24,40},{28,44},{32,4... | collective-permute-start | bytes 393224 | tf_op jit(solution)/shard_map/ppermute | solution.py:137
  51.1 1.2 %fusion = bf16[16,8,2048]{2,1,0:T(8,128)(2,1)} fusion(bf16[32,2048]{1,0:T(8,128)(2,1)S(1)} %collective-permute-done.3, bf16[32,2048]{1,0:T(8,128)(2,1)S(1)} %collective-permute-done.2, bf16[32,2048]{1,0:T(8,128)(2,1)S(1)} %collective-permute-done.1, bf16[32,2048]{1,0:T(8,128)(2,1)S(1)} %get-tuple-element.10, s32[128]{0:T(128)S(1)} %get-tuple-element.26, ...), kind=kOutput, calls=%fused_computation.1 | convolution fusion | flops 69566464 | bytes 1051392 | tf_op jit(solution)/shard_map/dot_general | solution.py:131
  52.3 11.5 %all-to-all-start.2 = ((bf16[16,8,2048]{2,1,0:T(8,128)(2,1)}), bf16[16,8,2048]{2,1,0:T(8,128)(2,1)S(1)}, u32[]{:S(2)}, u32[]{:S(2)}) async-start(bf16[16,8,2048]{2,1,0:T(8,128)(2,1)} %fusion), calls=%async_computation.2 | async-start | bytes 1048576 | tf_op jit(solution)/shard_map/all_to_all | solution.py:143
  63.8 4.3 %collective-permute-start.5 = (bf16[128,512]{1,0:T(8,128)(2,1)S(1)}, bf16[128,512]{1,0:T(8,128)(2,1)S(1)}, u32[]{:S(2)}, u32[]{:S(2)}) collective-permute-start(bf16[128,512]{1,0:T(8,128)(2,1)S(1)} %collective-permute-done.4), channel_id=1, source_target_pairs={{0,8},{4,12},{8,16},{12,20},{16,24},{20,28},{24,32},{28,36},{32,40... | collective-permute-start | bytes 393224 | tf_op jit(solution)/shard_map/ppermute | solution.py:137
  68.1 1.9 %collective-permute-start.6 = (bf16[128,512]{1,0:T(8,128)(2,1)S(1)}, bf16[128,512]{1,0:T(8,128)(2,1)S(1)}, u32[]{:S(2)}, u32[]{:S(2)}) collective-permute-start(bf16[128,512]{1,0:T(8,128)(2,1)S(1)} %collective-permute-done.4), channel_id=1, source_target_pairs={{0,16},{4,20},{8,24},{12,28},{16,32},{20,36},{24,40},{28,44},{32,4... | collective-permute-start | bytes 393224 | tf_op jit(solution)/shard_map/ppermute | solution.py:137
  70.1 6.5 %collective-permute-done.6 = bf16[128,512]{1,0:T(8,128)(2,1)S(1)} collective-permute-done((bf16[128,512]{1,0:T(8,128)(2,1)S(1)}, bf16[128,512]{1,0:T(8,128)(2,1)S(1)}, u32[]{:S(2)}, u32[]{:S(2)}) %collective-permute-start.6) | collective-permute-done | bytes 131104 | tf_op jit(solution)/shard_map/ppermute | solution.py:137
  76.7 8.8 %collective-permute-start.7 = (bf16[512,512]{1,0:T(8,128)(2,1)S(1)}, bf16[512,512]{1,0:T(8,128)(2,1)S(1)}, u32[]{:S(2)}, u32[]{:S(2)}) collective-permute-start(bf16[512,512]{1,0:T(8,128)(2,1)S(1)} %constant_dynamic-slice_fusion), channel_id=1, source_target_pairs={{0,4},{4,0},{8,12},{12,8},{16,20},{20,16},{24,28},{28,24},{32,36},... | collective-permute-start | bytes 1572872 | tf_op jit(solution)/shard_map/ppermute | solution.py:148
  85.5 1.5 %collective-permute-done.7.sib = bf16[512,512]{1,0:T(8,128)(2,1)S(1)} collective-permute-done((bf16[512,512]{1,0:T(8,128)(2,1)S(1)}, bf16[512,512]{1,0:T(8,128)(2,1)S(1)}, u32[]{:S(2)}, u32[]{:S(2)}) %collective-permute-start.7) | collective-permute-done | bytes 524320 | tf_op jit(solution)/shard_map/ppermute | solution.py:148
  87.0 5.3 %shard_map.56 = bf16[128,2048]{1,0:T(8,128)(2,1)} custom-call(s32[1,4]{1,0:T(1,128)S(1)} %copy-done, bf16[128,2048]{1,0:T(8,128)(2,1)S(1)} %bitcast.18, bf16[640,512]{1,0:T(8,128)(2,1)S(1)} %constant_dynamic-update-slice_fusion.own, bf16[512,512]{1,0:T(8,128)(2,1)S(1)} %collective-permute-done.7.sib), custom_call_target="tpu_custom_call" | custom-call | flops 1207959552 | bytes 2228224 | tf_op jit(solution)/shard_map/pallas_call | solution.py:67
  (24 shorter events, 0.2 us)
Async XLA Ops:
  0.0 7.9 %copy-start.2 = (s32[1,16]{1,0:T(1,128)S(1)}, s32[1,16]{1,0:T(1,128)}, u32[]{:S(2)}) copy-start(s32[1,16]{1,0:T(1,128)} %param.9) | copy-start | bytes 196
  1.6 32.6 %copy-start.1 = (bf16[32,8192]{1,0:T(8,128)(2,1)S(1)}, bf16[32,8192]{1,0:T(8,128)(2,1)}, u32[]{:S(2)}) copy-start(bf16[32,8192]{1,0:T(8,128)(2,1)} %param.5) | copy-start | bytes 1572868
  1.6 10.1 %all-to-all-start = ((bf16[4,32,512]{2,1,0:T(8,128)(2,1)}), bf16[4,32,512]{2,1,0:T(8,128)(2,1)S(1)}, u32[]{:S(2)}, u32[]{:S(2)}) async-start(bf16[4,32,512]{2,1,0:T(8,128)(2,1)} %shard_map.55), calls=%async_computation | async-start | bytes 262144 | tf_op jit(solution)/shard_map/all_to_all | solution.py:113
  12.6 31.2 %all-to-all-start.1 = ((bf16[16,8,512]{2,1,0:T(8,128)(2,1)}), bf16[16,8,512]{2,1,0:T(8,128)(2,1)S(1)}, u32[]{:S(2)}, u32[]{:S(2)}) async-start(bf16[16,8,512]{2,1,0:T(8,128)(2,1)} %fusion.1), calls=%async_computation.1 | async-start | bytes 262144 | tf_op jit(solution)/shard_map/all_to_all | solution.py:135
  34.2 16.9 %collective-permute-start.1 = (bf16[32,2048]{1,0:T(8,128)(2,1)S(1)}, bf16[32,2048]{1,0:T(8,128)(2,1)S(1)}, u32[]{:S(2)}, u32[]{:S(2)}) collective-permute-start(bf16[32,2048]{1,0:T(8,128)(2,1)S(1)} %get-tuple-element.16), channel_id=1, source_target_pairs={{0,1},{1,0},{2,3},{3,2},{4,5},{5,4},{6,7},{7,6},{8,9},{9,8},{10,11... | collective-permute-start | bytes 393224 | tf_op jit(solution)/shard_map/ppermute | solution.py:120
  36.1 15.0 %collective-permute-start.2 = (bf16[32,2048]{1,0:T(8,128)(2,1)S(1)}, bf16[32,2048]{1,0:T(8,128)(2,1)S(1)}, u32[]{:S(2)}, u32[]{:S(2)}) collective-permute-start(bf16[32,2048]{1,0:T(8,128)(2,1)S(1)} %get-tuple-element.18), channel_id=1, source_target_pairs={{0,2},{1,3},{2,0},{3,1},{4,6},{5,7},{6,4},{7,5},{8,10},{9,11},{10,... | collective-permute-start | bytes 393224 | tf_op jit(solution)/shard_map/ppermute | solution.py:120
  39.3 11.8 %collective-permute-start.3 = (bf16[32,2048]{1,0:T(8,128)(2,1)S(1)}, bf16[32,2048]{1,0:T(8,128)(2,1)S(1)}, u32[]{:S(2)}, u32[]{:S(2)}) collective-permute-start(bf16[32,2048]{1,0:T(8,128)(2,1)S(1)} %get-tuple-element.15), channel_id=1, source_target_pairs={{0,3},{1,2},{2,1},{3,0},{4,7},{5,6},{6,5},{7,4},{8,11},{9,10},{10,... | collective-permute-start | bytes 393224 | tf_op jit(solution)/shard_map/ppermute | solution.py:120
  43.9 7.2 %collective-permute-start = (bf16[128,512]{1,0:T(8,128)(2,1)S(1)}, bf16[128,512]{1,0:T(8,128)(2,1)S(1)}, u32[]{:S(2)}, u32[]{:S(2)}) collective-permute-start(bf16[128,512]{1,0:T(8,128)(2,1)S(1)} %bitcast.19), channel_id=1, source_target_pairs={{0,8},{4,12},{8,16},{12,20},{16,24},{20,28},{24,32},{28,36},{32,40... | collective-permute-start | bytes 393224 | tf_op jit(solution)/shard_map/ppermute | solution.py:137
  48.4 15.4 %collective-permute-start.4 = (bf16[128,512]{1,0:T(8,128)(2,1)S(1)}, bf16[128,512]{1,0:T(8,128)(2,1)S(1)}, u32[]{:S(2)}, u32[]{:S(2)}) collective-permute-start(bf16[128,512]{1,0:T(8,128)(2,1)S(1)} %bitcast.20), channel_id=1, source_target_pairs={{0,16},{4,20},{8,24},{12,28},{16,32},{20,36},{24,40},{28,44},{32,4... | collective-permute-start | bytes 393224 | tf_op jit(solution)/shard_map/ppermute | solution.py:137
  52.3 34.7 %all-to-all-start.2 = ((bf16[16,8,2048]{2,1,0:T(8,128)(2,1)}), bf16[16,8,2048]{2,1,0:T(8,128)(2,1)S(1)}, u32[]{:S(2)}, u32[]{:S(2)}) async-start(bf16[16,8,2048]{2,1,0:T(8,128)(2,1)} %fusion), calls=%async_computation.2 | async-start | bytes 1048576 | tf_op jit(solution)/shard_map/all_to_all | solution.py:143
  63.8 6.3 %collective-permute-start.5 = (bf16[128,512]{1,0:T(8,128)(2,1)S(1)}, bf16[128,512]{1,0:T(8,128)(2,1)S(1)}, u32[]{:S(2)}, u32[]{:S(2)}) collective-permute-start(bf16[128,512]{1,0:T(8,128)(2,1)S(1)} %collective-permute-done.4), channel_id=1, source_target_pairs={{0,8},{4,12},{8,16},{12,20},{16,24},{20,28},{24,32},{28,36},{32,40... | collective-permute-start | bytes 393224 | tf_op jit(solution)/shard_map/ppermute | solution.py:137
  68.1 8.5 %collective-permute-start.6 = (bf16[128,512]{1,0:T(8,128)(2,1)S(1)}, bf16[128,512]{1,0:T(8,128)(2,1)S(1)}, u32[]{:S(2)}, u32[]{:S(2)}) collective-permute-start(bf16[128,512]{1,0:T(8,128)(2,1)S(1)} %collective-permute-done.4), channel_id=1, source_target_pairs={{0,16},{4,20},{8,24},{12,28},{16,32},{20,36},{24,40},{28,44},{32,4... | collective-permute-start | bytes 393224 | tf_op jit(solution)/shard_map/ppermute | solution.py:137
  76.7 10.4 %copy-start = (s32[1,4]{1,0:T(1,128)S(1)}, s32[1,4]{1,0:T(1,128)}, u32[]{:S(2)}) copy-start(s32[1,4]{1,0:T(1,128)} %lengths.1) | copy-start | bytes 52
  76.7 10.4 %collective-permute-start.7 = (bf16[512,512]{1,0:T(8,128)(2,1)S(1)}, bf16[512,512]{1,0:T(8,128)(2,1)S(1)}, u32[]{:S(2)}, u32[]{:S(2)}) collective-permute-start(bf16[512,512]{1,0:T(8,128)(2,1)S(1)} %constant_dynamic-slice_fusion), channel_id=1, source_target_pairs={{0,4},{4,0},{8,12},{12,8},{16,20},{20,16},{24,28},{28,24},{32,36},... | collective-permute-start | bytes 1572872 | tf_op jit(solution)/shard_map/ppermute | solution.py:148

commit v7 on v3

--- a/solution.py
+++ b/solution.py
@@ -8,6 +8,7 @@
 from jax.sharding import PartitionSpec as P
 
 HD = 128
+BLOCK = 8
 HIDDEN = -1e30
 CHUNK_HEADS = 4
 
@@ -83,23 +84,41 @@
     )(lengths, q, own, sib)
 
 
-def pack(arrays, parts):
+def pack(arrays, table, parts):
     widths = [a.shape[1] // parts for a in arrays]
+    part = arrays[0].shape[0]
+    rows = part * parts
 
-    def kernel(*refs):
-        out = refs[-1]
+    def kernel(table, *refs):
+        *held, out, order, turned = refs
+        me = lax.axis_index("tp")
         for t in range(parts):
             at = 0
-            for a, width in zip(refs, widths):
+            for a, width in zip(held, widths):
                 out[t, :, at : at + width] = a[:, t * width : (t + 1) * width]
                 at += width
+        row = lax.broadcasted_iota(jnp.int32, (rows, rows), 0)
+        col = lax.broadcasted_iota(jnp.int32, (rows, rows), 1)
+        source = col // BLOCK
+        for matrix, first in ((order, 0), (turned, me)):
+            wanted = jnp.zeros((rows, rows), jnp.int32)
+            for b in range(rows // BLOCK):
+                d, inner = divmod(b, part // BLOCK)
+                wanted = jnp.where(source == b, table[0, (first ^ d) * (part // BLOCK) + inner] * BLOCK, wanted)
+            matrix[...] = jnp.where(row == wanted + col % BLOCK, 1.0, 0.0).astype(matrix.dtype)
 
+    dtype = arrays[0].dtype
+    vmem = pl.BlockSpec(memory_space=pltpu.VMEM)
     return pl.pallas_call(
         kernel,
-        out_shape=jax.ShapeDtypeStruct((parts, arrays[0].shape[0], sum(widths)), arrays[0].dtype),
-        in_specs=[pl.BlockSpec(memory_space=pltpu.VMEM)] * len(arrays),
-        out_specs=pl.BlockSpec(memory_space=pltpu.VMEM),
-    )(*arrays)
+        out_shape=[
+            jax.ShapeDtypeStruct((parts, part, sum(widths)), dtype),
+            jax.ShapeDtypeStruct((rows, rows), dtype),
+            jax.ShapeDtypeStruct((rows, rows), dtype),
+        ],
+        in_specs=[pl.BlockSpec(memory_space=pltpu.SMEM)] + [vmem] * len(arrays),
+        out_specs=[vmem] * 3,
+    )(table, *arrays)
 
 
 def shards(queries, key_rows, value_rows, image_lengths, block_table):
@@ -108,32 +127,24 @@
     part = queries.shape[0]
     rows = part * tp
     block = rows // groups
-    blocks = part // block
-    packed = pack((key_rows, value_rows), tp)
+    packed, kv_order, q_order = pack((key_rows, value_rows), block_table, tp)
     held_kv = lax.all_to_all(packed, "tp", 0, 0, tiled=True).reshape(rows, -1)
     q_width = queries.shape[1] // tp
-    pieces, arrived = [], []
+    pieces = []
     for d in range(tp):
         other = me ^ d
         piece = lax.dynamic_slice_in_dim(queries, other * q_width, q_width, axis=1)
         if d:
             piece = lax.ppermute(piece, "tp", [(i, i ^ d) for i in range(tp)])
         pieces.append(piece)
-        arrived.append(lax.dynamic_slice_in_dim(block_table[0], other * blocks, blocks))
     held_q = jnp.concatenate(pieces, axis=0)
-
-    def order(destination):
-        wide = jnp.broadcast_to(destination[:, None], (groups, block)).reshape(rows)
-        row = lax.broadcasted_iota(jnp.int32, (rows, rows), 0)
-        col = lax.broadcasted_iota(jnp.int32, (rows, rows), 1)
-        return ((wide[None, :] == row // block) & (row % block == col % block)).astype(jnp.bfloat16)
 
     def sort(matrix, rows_held):
         out = jnp.dot(matrix, rows_held, preferred_element_type=jnp.float32).astype(jnp.bfloat16)
         return out.reshape(groups, block, -1)
 
-    kv_sorted = sort(order(block_table[0]), held_kv)
-    q_sorted = sort(order(jnp.concatenate(arrived)), held_q)
+    kv_sorted = sort(kv_order, held_kv)
+    q_sorted = sort(q_order, held_q)
     kv = lax.all_to_all(kv_sorted, "grp", 0, 0, tiled=True).reshape(rows, -1)
     kv, q_sorted = lax.optimization_barrier((kv, q_sorted))
     q = lax.all_to_all(q_sorted, "grp", 0, 0, tiled=True).reshape(rows, -1)

time: 88.6 us -> 88.8 us (level)
    dynamic_slice x1, local copies, waits for them, and re-layouts: 0.04 us -> 1.14 us  [shards(): piece = lax.dynamic_slice_in_dim(queries, other * q_width, q_width, axis=1)]
  transfers between devices with their start and end apart: 11 -> 11, of which waited for: 4 -> 4; matrix products, arithmetic and copies ran while one was open for 3% -> 4% of each run, Pallas kernels for 0% -> 0%
where the time goes in v7:
time: 88.8 us; the launch traced here: 88.2 us
  starting transfers between devices  57.5 us (65%)
  waiting for transfers between devices  20.3 us (23%)
  Pallas kernels  6.9 us (8%)
  matrix products  1.93 us (2%)
  local copies, waits for them, and re-layouts  1.25 us (1%)
    all_to_all x1, starting transfers between devices, shards(): kv = lax.all_to_all(kv_sorted, 'grp', 0, 0, tiled=True).reshape(rows, -1)  20.5 us
    ppermute x4, starting transfers between devices, ahead(): lax.ppermute(x, 'seq', [(i, i + 2 * chips) for i in range(seq - 2 * chips)])  16.8 us
    all_to_all x1, waiting for transfers between devices, shards(): kv = lax.all_to_all(kv_sorted, 'grp', 0, 0, tiled=True).reshape(rows, -1)  11.5 us
    ppermute x3, starting transfers between devices, shards(): piece = lax.ppermute(piece, 'tp', [(i, i ^ d) for i in range(tp)])  9.56 us
    pallas_call x1, Pallas kernels, attention(): pl.pallas_call(attend, out_shape=jax.ShapeDtypeStruct(q.shape, jnp.bfloat...  5.34 us
    all_to_all x1, starting transfers between devices, shards(): held_kv = lax.all_to_all(packed, 'tp', 0, 0, tiled=True).reshape(rows, -1)  5.12 us
    all_to_all x1, waiting for transfers between devices, shards(): q = lax.all_to_all(q_sorted, 'grp', 0, 0, tiled=True).reshape(rows, -1)  4.06 us
    all_to_all x1, starting transfers between devices, shards(): q = lax.all_to_all(q_sorted, 'grp', 0, 0, tiled=True).reshape(rows, -1)  3.59 us
  transfers between devices with their start and end apart: 11, of which 4 were waited for; matrix products, arithmetic and copies ran while one was open for 4% of the time, Pallas kernels for 0%

profile of v7, /device:TPU:20, one launch (start us, length us, event | category | flops | bytes accessed | tf_op | source)
XLA Modules:
  0.0 88.2 jit_solution(14882432632132689783)
XLA Ops:
  0.0 1.6 %shard_map.55 = (bf16[4,32,512]{2,1,0:T(8,128)(2,1)}, bf16[128,128]{1,0:T(8,128)(2,1)}, bf16[128,128]{1,0:T(8,128)(2,1)}) custom-call(s32[1,16]{1,0:T(1,128)} %table.1, bf16[32,1024]{1,0:T(8,128)(2,1)} %refs_0_.1, bf16[32,1024]{1,0:T(8,128)(2,1)} %refs_1_.1), custom_call_target="tpu_custom_call" | custom-call | tf_op jit(solution)/shard_map/pallas_call | solution.py:112
  1.6 5.1 %all-to-all-start = ((bf16[4,32,512]{2,1,0:T(8,128)(2,1)}), bf16[4,32,512]{2,1,0:T(8,128)(2,1)S(1)}, u32[]{:S(2)}, u32[]{:S(2)}) async-start(bf16[4,32,512]{2,1,0:T(8,128)(2,1)} %get-tuple-element.11), calls=%async_computation | async-start | bytes 262144 | tf_op jit(solution)/shard_map/all_to_all | solution.py:131
  6.7 1.1 %constant_dynamic-slice_fusion.4 = (bf16[32,2048]{1,0:T(8,128)(2,1)S(1)}, bf16[32,2048]{1,0:T(8,128)(2,1)S(1)}, bf16[32,2048]{1,0:T(8,128)(2,1)S(1)}, bf16[32,2048]{1,0:T(8,128)(2,1)S(1)}) fusion(bf16[32,8192]{1,0:T(8,128)(2,1)} %param.5, s32[]{:T(128)S(6)} %select_n.15, s32[]{:T(128)S(6)} %select_n.16, s32[]{:T(128)S(6)} %select_n.18, s32[]{:T(128)S(6)} %select_n.17), kind=kLoop, calls=%fused_computation.20 | loop fusion | bytes 1048592 | tf_op jit(solution)/shard_map/dynamic_slice | solution.py:136
  7.8 2.5 %collective-permute-start.2 = (bf16[32,2048]{1,0:T(8,128)(2,1)S(1)}, bf16[32,2048]{1,0:T(8,128)(2,1)S(1)}, u32[]{:S(2)}, u32[]{:S(2)}) collective-permute-start(bf16[32,2048]{1,0:T(8,128)(2,1)S(1)} %get-tuple-element.17), channel_id=1, source_target_pairs={{0,3},{1,2},{2,1},{3,0},{4,7},{5,6},{6,5},{7,4},{8,11},{9,10},{10,... | collective-permute-start | bytes 393224 | tf_op jit(solution)/shard_map/ppermute | solution.py:138
  10.3 5.2 %collective-permute-start.1 = (bf16[32,2048]{1,0:T(8,128)(2,1)S(1)}, bf16[32,2048]{1,0:T(8,128)(2,1)S(1)}, u32[]{:S(2)}, u32[]{:S(2)}) collective-permute-start(bf16[32,2048]{1,0:T(8,128)(2,1)S(1)} %get-tuple-element.18), channel_id=1, source_target_pairs={{0,2},{1,3},{2,0},{3,1},{4,6},{5,7},{6,4},{7,5},{8,10},{9,11},{10,... | collective-permute-start | bytes 393224 | tf_op jit(solution)/shard_map/ppermute | solution.py:138
  15.5 1.9 %collective-permute-start = (bf16[32,2048]{1,0:T(8,128)(2,1)S(1)}, bf16[32,2048]{1,0:T(8,128)(2,1)S(1)}, u32[]{:S(2)}, u32[]{:S(2)}) collective-permute-start(bf16[32,2048]{1,0:T(8,128)(2,1)S(1)} %get-tuple-element.16), channel_id=1, source_target_pairs={{0,1},{1,0},{2,3},{3,2},{4,5},{5,4},{6,7},{7,6},{8,9},{9,8},{10,11... | collective-permute-start | bytes 393224 | tf_op jit(solution)/shard_map/ppermute | solution.py:138
  17.4 0.0 all-to-all-done
  17.4 0.8 fusion.1
  18.3 20.5 %all-to-all-start.1 = ((bf16[16,8,512]{2,1,0:T(8,128)(2,1)}), bf16[16,8,512]{2,1,0:T(8,128)(2,1)S(1)}, u32[]{:S(2)}, u32[]{:S(2)}) async-start(bf16[16,8,512]{2,1,0:T(8,128)(2,1)} %fusion.1), calls=%async_computation.1 | async-start | bytes 262144 | tf_op jit(solution)/shard_map/all_to_all | solution.py:148
  38.8 0.0 collective-permute-done.2
  38.8 0.0 collective-permute-done
  38.8 1.1 %fusion = bf16[16,8,2048]{2,1,0:T(8,128)(2,1)} fusion(bf16[128,128]{1,0:T(8,128)(2,1)S(1)} %copy-done.2, bf16[32,2048]{1,0:T(8,128)(2,1)S(1)} %collective-permute-done.2, bf16[32,2048]{1,0:T(8,128)(2,1)S(1)} %collective-permute-done.1, bf16[32,2048]{1,0:T(8,128)(2,1)S(1)} %collective-permute-done, bf16[32,2048]{1,0:T(8,128)(2,1)S(1)} %get-tuple-element.15), kind=kOutput, calls=%fused_computation.1 | convolution fusion | flops 69468160 | bytes 1081344 | tf_op jit(solution)/shard_map/dot_general | solution.py:143
  39.9 11.5 %all-to-all-done.1 = bf16[16,8,512]{2,1,0:T(8,128)(2,1)S(1)} async-done(((bf16[16,8,512]{2,1,0:T(8,128)(2,1)}), bf16[16,8,512]{2,1,0:T(8,128)(2,1)S(1)}, u32[]{:S(2)}, u32[]{:S(2)}) %all-to-all-start.1) | async-done | bytes 131104 | tf_op jit(solution)/shard_map/all_to_all | solution.py:148
  51.5 4.7 %collective-permute-start.4 = (bf16[128,512]{1,0:T(8,128)(2,1)S(1)}, bf16[128,512]{1,0:T(8,128)(2,1)S(1)}, u32[]{:S(2)}, u32[]{:S(2)}) collective-permute-start(bf16[128,512]{1,0:T(8,128)(2,1)S(1)} %bitcast.11), channel_id=1, source_target_pairs={{0,16},{4,20},{8,24},{12,28},{16,32},{20,36},{24,40},{28,44},{32,4... | collective-permute-start | bytes 393224 | tf_op jit(solution)/shard_map/ppermute | solution.py:153
  56.2 4.8 %collective-permute-start.3 = (bf16[128,512]{1,0:T(8,128)(2,1)S(1)}, bf16[128,512]{1,0:T(8,128)(2,1)S(1)}, u32[]{:S(2)}, u32[]{:S(2)}) collective-permute-start(bf16[128,512]{1,0:T(8,128)(2,1)S(1)} %bitcast.12), channel_id=1, source_target_pairs={{0,8},{4,12},{8,16},{12,20},{16,24},{20,28},{24,32},{28,36},{32,40... | collective-permute-start | bytes 393224 | tf_op jit(solution)/shard_map/ppermute | solution.py:153
  61.0 3.6 %all-to-all-start.2 = ((bf16[16,8,2048]{2,1,0:T(8,128)(2,1)}), bf16[16,8,2048]{2,1,0:T(8,128)(2,1)S(1)}, u32[]{:S(2)}, u32[]{:S(2)}) async-start(bf16[16,8,2048]{2,1,0:T(8,128)(2,1)} %fusion), calls=%async_computation.2 | async-start | bytes 1048576 | tf_op jit(solution)/shard_map/all_to_all | solution.py:150
  64.6 2.7 %collective-permute-start.5 = (bf16[128,512]{1,0:T(8,128)(2,1)S(1)}, bf16[128,512]{1,0:T(8,128)(2,1)S(1)}, u32[]{:S(2)}, u32[]{:S(2)}) collective-permute-start(bf16[128,512]{1,0:T(8,128)(2,1)S(1)} %collective-permute-done.4), channel_id=1, source_target_pairs={{0,8},{4,12},{8,16},{12,20},{16,24},{20,28},{24,32},{28,36},{32,40... | collective-permute-start | bytes 393224 | tf_op jit(solution)/shard_map/ppermute | solution.py:153
  67.3 4.6 %collective-permute-start.6 = (bf16[128,512]{1,0:T(8,128)(2,1)S(1)}, bf16[128,512]{1,0:T(8,128)(2,1)S(1)}, u32[]{:S(2)}, u32[]{:S(2)}) collective-permute-start(bf16[128,512]{1,0:T(8,128)(2,1)S(1)} %collective-permute-done.4), channel_id=1, source_target_pairs={{0,16},{4,20},{8,24},{12,28},{16,32},{20,36},{24,40},{28,44},{32,4... | collective-permute-start | bytes 393224 | tf_op jit(solution)/shard_map/ppermute | solution.py:153
  72.0 2.8 %collective-permute-done.6 = bf16[128,512]{1,0:T(8,128)(2,1)S(1)} collective-permute-done((bf16[128,512]{1,0:T(8,128)(2,1)S(1)}, bf16[128,512]{1,0:T(8,128)(2,1)S(1)}, u32[]{:S(2)}, u32[]{:S(2)}) %collective-permute-start.6) | collective-permute-done | bytes 131104 | tf_op jit(solution)/shard_map/ppermute | solution.py:153
  74.9 0.0 copy-start
  74.9 1.9 %collective-permute-start.7 = (bf16[512,512]{1,0:T(8,128)(2,1)S(1)}, bf16[512,512]{1,0:T(8,128)(2,1)S(1)}, u32[]{:S(2)}, u32[]{:S(2)}) collective-permute-start(bf16[512,512]{1,0:T(8,128)(2,1)S(1)} %constant_dynamic-slice_fusion), channel_id=1, source_target_pairs={{0,4},{4,0},{8,12},{12,8},{16,20},{20,16},{24,28},{28,24},{32,36},... | collective-permute-start | bytes 1572872 | tf_op jit(solution)/shard_map/ppermute | solution.py:159
  76.9 1.9 %collective-permute-done.7.sib = bf16[512,512]{1,0:T(8,128)(2,1)S(1)} collective-permute-done((bf16[512,512]{1,0:T(8,128)(2,1)S(1)}, bf16[512,512]{1,0:T(8,128)(2,1)S(1)}, u32[]{:S(2)}, u32[]{:S(2)}) %collective-permute-start.7) | collective-permute-done | bytes 524320 | tf_op jit(solution)/shard_map/ppermute | solution.py:159
  78.7 4.1 %all-to-all-done.2 = bf16[16,8,2048]{2,1,0:T(8,128)(2,1)S(1)} async-done(((bf16[16,8,2048]{2,1,0:T(8,128)(2,1)}), bf16[16,8,2048]{2,1,0:T(8,128)(2,1)S(1)}, u32[]{:S(2)}, u32[]{:S(2)}) %all-to-all-start.2) | async-done | bytes 524320 | tf_op jit(solution)/shard_map/all_to_all | solution.py:150
  82.8 5.3 %shard_map.56 = bf16[128,2048]{1,0:T(8,128)(2,1)} custom-call(s32[1,4]{1,0:T(1,128)S(1)} %copy-done, bf16[128,2048]{1,0:T(8,128)(2,1)S(1)} %bitcast.10, bf16[640,512]{1,0:T(8,128)(2,1)S(1)} %constant_dynamic-update-slice_fusion.own, bf16[512,512]{1,0:T(8,128)(2,1)S(1)} %collective-permute-done.7.sib), custom_call_target="tpu_custom_call" | custom-call | flops 1207959552 | bytes 2228224 | tf_op jit(solution)/shard_map/pallas_call | solution.py:68
  (15 shorter events, 0.1 us)
Async XLA Ops:
  1.6 15.8 %all-to-all-start = ((bf16[4,32,512]{2,1,0:T(8,128)(2,1)}), bf16[4,32,512]{2,1,0:T(8,128)(2,1)S(1)}, u32[]{:S(2)}, u32[]{:S(2)}) async-start(bf16[4,32,512]{2,1,0:T(8,128)(2,1)} %get-tuple-element.11), calls=%async_computation | async-start | bytes 262144 | tf_op jit(solution)/shard_map/all_to_all | solution.py:131
  6.7 10.7 %copy-start.1 = (bf16[128,128]{1,0:T(8,128)(2,1)S(1)}, bf16[128,128]{1,0:T(8,128)(2,1)}, u32[]{:S(2)}) copy-start(bf16[128,128]{1,0:T(8,128)(2,1)} %get-tuple-element.10) | copy-start | bytes 98308
  7.8 31.0 %collective-permute-start.2 = (bf16[32,2048]{1,0:T(8,128)(2,1)S(1)}, bf16[32,2048]{1,0:T(8,128)(2,1)S(1)}, u32[]{:S(2)}, u32[]{:S(2)}) collective-permute-start(bf16[32,2048]{1,0:T(8,128)(2,1)S(1)} %get-tuple-element.17), channel_id=1, source_target_pairs={{0,3},{1,2},{2,1},{3,0},{4,7},{5,6},{6,5},{7,4},{8,11},{9,10},{10,... | collective-permute-start | bytes 393224 | tf_op jit(solution)/shard_map/ppermute | solution.py:138
  10.3 28.5 %collective-permute-start.1 = (bf16[32,2048]{1,0:T(8,128)(2,1)S(1)}, bf16[32,2048]{1,0:T(8,128)(2,1)S(1)}, u32[]{:S(2)}, u32[]{:S(2)}) collective-permute-start(bf16[32,2048]{1,0:T(8,128)(2,1)S(1)} %get-tuple-element.18), channel_id=1, source_target_pairs={{0,2},{1,3},{2,0},{3,1},{4,6},{5,7},{6,4},{7,5},{8,10},{9,11},{10,... | collective-permute-start | bytes 393224 | tf_op jit(solution)/shard_map/ppermute | solution.py:138
  15.5 23.4 %collective-permute-start = (bf16[32,2048]{1,0:T(8,128)(2,1)S(1)}, bf16[32,2048]{1,0:T(8,128)(2,1)S(1)}, u32[]{:S(2)}, u32[]{:S(2)}) collective-permute-start(bf16[32,2048]{1,0:T(8,128)(2,1)S(1)} %get-tuple-element.16), channel_id=1, source_target_pairs={{0,1},{1,0},{2,3},{3,2},{4,5},{5,4},{6,7},{7,6},{8,9},{9,8},{10,11... | collective-permute-start | bytes 393224 | tf_op jit(solution)/shard_map/ppermute | solution.py:138
  18.3 20.6 %copy-start.2 = (bf16[128,128]{1,0:T(8,128)(2,1)S(1)}, bf16[128,128]{1,0:T(8,128)(2,1)}, u32[]{:S(2)}) copy-start(bf16[128,128]{1,0:T(8,128)(2,1)} %get-tuple-element.12) | copy-start | bytes 98308
  18.3 33.2 %all-to-all-start.1 = ((bf16[16,8,512]{2,1,0:T(8,128)(2,1)}), bf16[16,8,512]{2,1,0:T(8,128)(2,1)S(1)}, u32[]{:S(2)}, u32[]{:S(2)}) async-start(bf16[16,8,512]{2,1,0:T(8,128)(2,1)} %fusion.1), calls=%async_computation.1 | async-start | bytes 262144 | tf_op jit(solution)/shard_map/all_to_all | solution.py:148
  51.5 13.2 %collective-permute-start.4 = (bf16[128,512]{1,0:T(8,128)(2,1)S(1)}, bf16[128,512]{1,0:T(8,128)(2,1)S(1)}, u32[]{:S(2)}, u32[]{:S(2)}) collective-permute-start(bf16[128,512]{1,0:T(8,128)(2,1)S(1)} %bitcast.11), channel_id=1, source_target_pairs={{0,16},{4,20},{8,24},{12,28},{16,32},{20,36},{24,40},{28,44},{32,4... | collective-permute-start | bytes 393224 | tf_op jit(solution)/shard_map/ppermute | solution.py:153
  56.2 15.7 %collective-permute-start.3 = (bf16[128,512]{1,0:T(8,128)(2,1)S(1)}, bf16[128,512]{1,0:T(8,128)(2,1)S(1)}, u32[]{:S(2)}, u32[]{:S(2)}) collective-permute-start(bf16[128,512]{1,0:T(8,128)(2,1)S(1)} %bitcast.12), channel_id=1, source_target_pairs={{0,8},{4,12},{8,16},{12,20},{16,24},{20,28},{24,32},{28,36},{32,40... | collective-permute-start | bytes 393224 | tf_op jit(solution)/shard_map/ppermute | solution.py:153
  61.0 21.8 %all-to-all-start.2 = ((bf16[16,8,2048]{2,1,0:T(8,128)(2,1)}), bf16[16,8,2048]{2,1,0:T(8,128)(2,1)S(1)}, u32[]{:S(2)}, u32[]{:S(2)}) async-start(bf16[16,8,2048]{2,1,0:T(8,128)(2,1)} %fusion), calls=%async_computation.2 | async-start | bytes 1048576 | tf_op jit(solution)/shard_map/all_to_all | solution.py:150
  64.6 7.4 %collective-permute-start.5 = (bf16[128,512]{1,0:T(8,128)(2,1)S(1)}, bf16[128,512]{1,0:T(8,128)(2,1)S(1)}, u32[]{:S(2)}, u32[]{:S(2)}) collective-permute-start(bf16[128,512]{1,0:T(8,128)(2,1)S(1)} %collective-permute-done.4), channel_id=1, source_target_pairs={{0,8},{4,12},{8,16},{12,20},{16,24},{20,28},{24,32},{28,36},{32,40... | collective-permute-start | bytes 393224 | tf_op jit(solution)/shard_map/ppermute | solution.py:153
  67.3 7.5 %collective-permute-start.6 = (bf16[128,512]{1,0:T(8,128)(2,1)S(1)}, bf16[128,512]{1,0:T(8,128)(2,1)S(1)}, u32[]{:S(2)}, u32[]{:S(2)}) collective-permute-start(bf16[128,512]{1,0:T(8,128)(2,1)S(1)} %collective-permute-done.4), channel_id=1, source_target_pairs={{0,16},{4,20},{8,24},{12,28},{16,32},{20,36},{24,40},{28,44},{32,4... | collective-permute-start | bytes 393224 | tf_op jit(solution)/shard_map/ppermute | solution.py:153
  74.9 7.9 %copy-start = (s32[1,4]{1,0:T(1,128)S(1)}, s32[1,4]{1,0:T(1,128)}, u32[]{:S(2)}) copy-start(s32[1,4]{1,0:T(1,128)} %lengths.1) | copy-start | bytes 52
  74.9 3.8 %collective-permute-start.7 = (bf16[512,512]{1,0:T(8,128)(2,1)S(1)}, bf16[512,512]{1,0:T(8,128)(2,1)S(1)}, u32[]{:S(2)}, u32[]{:S(2)}) collective-permute-start(bf16[512,512]{1,0:T(8,128)(2,1)S(1)} %constant_dynamic-slice_fusion), channel_id=1, source_target_pairs={{0,4},{4,0},{8,12},{12,8},{16,20},{20,16},{24,28},{28,24},{32,36},... | collective-permute-start | bytes 1572872 | tf_op jit(solution)/shard_map/ppermute | solution.py:159

commit v8 on v7

--- a/solution.py
+++ b/solution.py
@@ -84,14 +84,18 @@
     )(lengths, q, own, sib)
 
 
-def pack(arrays, table, parts):
+def pack(arrays, queries, table, parts):
     widths = [a.shape[1] // parts for a in arrays]
     part = arrays[0].shape[0]
     rows = part * parts
 
-    def kernel(table, *refs):
-        *held, out, order, turned = refs
+    width_q = queries.shape[1] // parts
+
+    def kernel(table, q, *refs):
+        held, (out, order, turned, *pieces) = refs[: len(arrays)], refs[len(arrays) :]
         me = lax.axis_index("tp")
+        for d, piece in enumerate(pieces):
+            piece[...] = q[:, pl.ds(pl.multiple_of((me ^ d) * width_q, width_q), width_q)]
         for t in range(parts):
             at = 0
             for a, width in zip(held, widths):
@@ -115,25 +119,23 @@
             jax.ShapeDtypeStruct((parts, part, sum(widths)), dtype),
             jax.ShapeDtypeStruct((rows, rows), dtype),
             jax.ShapeDtypeStruct((rows, rows), dtype),
-        ],
-        in_specs=[pl.BlockSpec(memory_space=pltpu.SMEM)] + [vmem] * len(arrays),
-        out_specs=[vmem] * 3,
-    )(table, *arrays)
+        ]
+        + [jax.ShapeDtypeStruct((part, width_q), dtype)] * parts,
+        in_specs=[pl.BlockSpec(memory_space=pltpu.SMEM)] + [vmem] * (1 + len(arrays)),
+        out_specs=[vmem] * (3 + parts),
+    )(table, queries, *arrays)
 
 
 def shards(queries, key_rows, value_rows, image_lengths, block_table):
     tp, groups, seq = lax.axis_size("tp"), lax.axis_size("grp"), lax.axis_size("seq")
-    me = lax.axis_index("tp")
     part = queries.shape[0]
     rows = part * tp
     block = rows // groups
-    packed, kv_order, q_order = pack((key_rows, value_rows), block_table, tp)
+    packed, kv_order, q_order, *split = pack((key_rows, value_rows), queries, block_table, tp)
     held_kv = lax.all_to_all(packed, "tp", 0, 0, tiled=True).reshape(rows, -1)
-    q_width = queries.shape[1] // tp
     pieces = []
     for d in range(tp):
-        other = me ^ d
-        piece = lax.dynamic_slice_in_dim(queries, other * q_width, q_width, axis=1)
+        piece = split[d]
         if d:
             piece = lax.ppermute(piece, "tp", [(i, i ^ d) for i in range(tp)])
         pieces.append(piece)

time: 88.8 us -> 88.1 us (level)
  local copies, waits for them, and re-layouts: 1.25 us -> 0.12 us
    dynamic_slice x1 -> x0, local copies, waits for them, and re-layouts: 1.14 us -> none  [shards(): piece = lax.dynamic_slice_in_dim(queries, other * q_width, q_width, axis=1)]
  transfers between devices with their start and end apart: 11 -> 11, of which waited for: 4 -> 4; matrix products, arithmetic and copies ran while one was open for 4% -> 2% of each run, Pallas kernels for 0% -> 0%
where the time goes in v8:
time: 88.1 us; the launch traced here: 87.5 us
  starting transfers between devices  57.7 us (65%)
  waiting for transfers between devices  20.3 us (23%)
  Pallas kernels  7.3 us (8%)
  matrix products  1.9 us (2%)
    all_to_all x1, starting transfers between devices, shards(): kv = lax.all_to_all(kv_sorted, 'grp', 0, 0, tiled=True).reshape(rows, -1)  20.5 us
    ppermute x4, starting transfers between devices, ahead(): lax.ppermute(x, 'seq', [(i, i + 2 * chips) for i in range(seq - 2 * chips)])  16.8 us
    all_to_all x1, waiting for transfers between devices, shards(): kv = lax.all_to_all(kv_sorted, 'grp', 0, 0, tiled=True).reshape(rows, -1)  11.5 us
    ppermute x3, starting transfers between devices, shards(): piece = lax.ppermute(piece, 'tp', [(i, i ^ d) for i in range(tp)])  9.55 us
    pallas_call x1, Pallas kernels, attention(): pl.pallas_call(attend, out_shape=jax.ShapeDtypeStruct(q.shape, jnp.bfloat...  5.34 us
    all_to_all x1, starting transfers between devices, shards(): held_kv = lax.all_to_all(packed, 'tp', 0, 0, tiled=True).reshape(rows, -1)  5.26 us
    all_to_all x1, waiting for transfers between devices, shards(): q = lax.all_to_all(q_sorted, 'grp', 0, 0, tiled=True).reshape(rows, -1)  4.05 us
    all_to_all x1, starting transfers between devices, shards(): q = lax.all_to_all(q_sorted, 'grp', 0, 0, tiled=True).reshape(rows, -1)  3.59 us
  transfers between devices with their start and end apart: 11, of which 4 were waited for; matrix products, arithmetic and copies ran while one was open for 2% of the time, Pallas kernels for 0%

profile of v8, /device:TPU:20, one launch (start us, length us, event | category | flops | bytes accessed | tf_op | source)
XLA Modules:
  0.0 87.5 jit_solution(4114656880114969070)
XLA Ops:
  0.0 2.0 %shard_map.55 = (bf16[4,32,512]{2,1,0:T(8,128)(2,1)}, bf16[128,128]{1,0:T(8,128)(2,1)}, bf16[128,128]{1,0:T(8,128)(2,1)}, bf16[32,2048]{1,0:T(8,128)(2,1)}, bf16...) custom-call(s32[1,16]{1,0:T(1,128)} %table.1, bf16[32,8192]{1,0:T(8,128)(2,1)} %q.1, ...), custom_call_target="tpu_custom_call" | custom-call | tf_op jit(solution)/shard_map/pallas_call | solution.py:116
  2.0 5.3 %all-to-all-start = ((bf16[4,32,512]{2,1,0:T(8,128)(2,1)}), bf16[4,32,512]{2,1,0:T(8,128)(2,1)S(1)}, u32[]{:S(2)}, u32[]{:S(2)}) async-start(bf16[4,32,512]{2,1,0:T(8,128)(2,1)} %get-tuple-element.15), calls=%async_computation | async-start | bytes 262144 | tf_op jit(solution)/shard_map/all_to_all | solution.py:135
  7.2 2.5 %collective-permute-start.2 = (bf16[32,2048]{1,0:T(8,128)(2,1)}, bf16[32,2048]{1,0:T(8,128)(2,1)S(1)}, u32[]{:S(2)}, u32[]{:S(2)}) collective-permute-start(bf16[32,2048]{1,0:T(8,128)(2,1)} %get-tuple-element.20), channel_id=1, source_target_pairs={{0,3},{1,2},{2,1},{3,0},{4,7},{5,6},{6,5},{7,4},{8,11},{9,10},{10,... | collective-permute-start | bytes 393224 | tf_op jit(solution)/shard_map/ppermute | solution.py:140
  9.7 5.2 %collective-permute-start.1 = (bf16[32,2048]{1,0:T(8,128)(2,1)}, bf16[32,2048]{1,0:T(8,128)(2,1)S(1)}, u32[]{:S(2)}, u32[]{:S(2)}) collective-permute-start(bf16[32,2048]{1,0:T(8,128)(2,1)} %get-tuple-element.19), channel_id=1, source_target_pairs={{0,2},{1,3},{2,0},{3,1},{4,6},{5,7},{6,4},{7,5},{8,10},{9,11},{10,... | collective-permute-start | bytes 393224 | tf_op jit(solution)/shard_map/ppermute | solution.py:140
  14.9 1.9 %collective-permute-start = (bf16[32,2048]{1,0:T(8,128)(2,1)S(1)}, bf16[32,2048]{1,0:T(8,128)(2,1)S(1)}, u32[]{:S(2)}, u32[]{:S(2)}) collective-permute-start(bf16[32,2048]{1,0:T(8,128)(2,1)S(1)} %copy-done.3), channel_id=1, source_target_pairs={{0,1},{1,0},{2,3},{3,2},{4,5},{5,4},{6,7},{7,6},{8,9},{9,8},{10,11... | collective-permute-start | bytes 393224 | tf_op jit(solution)/shard_map/ppermute | solution.py:140
  16.8 0.8 fusion.1
  17.7 20.5 %all-to-all-start.1 = ((bf16[16,8,512]{2,1,0:T(8,128)(2,1)}), bf16[16,8,512]{2,1,0:T(8,128)(2,1)S(1)}, u32[]{:S(2)}, u32[]{:S(2)}) async-start(bf16[16,8,512]{2,1,0:T(8,128)(2,1)} %fusion.1), calls=%async_computation.1 | async-start | bytes 262144 | tf_op jit(solution)/shard_map/all_to_all | solution.py:150
  38.2 0.0 collective-permute-done.2
  38.2 0.0 collective-permute-done.1
  38.2 1.1 %fusion = bf16[16,8,2048]{2,1,0:T(8,128)(2,1)} fusion(bf16[128,128]{1,0:T(8,128)(2,1)S(1)} %copy-done.4, bf16[32,2048]{1,0:T(8,128)(2,1)S(1)} %collective-permute-done.2, bf16[32,2048]{1,0:T(8,128)(2,1)S(1)} %collective-permute-done.1, bf16[32,2048]{1,0:T(8,128)(2,1)S(1)} %collective-permute-done, bf16[32,2048]{1,0:T(8,128)(2,1)S(1)} %copy-done.2), kind=kOutput, calls=%fused_computation.1 | convolution fusion | flops 69468160 | bytes 1081344 | tf_op jit(solution)/shard_map/dot_general | solution.py:145
  39.3 11.5 %all-to-all-done.1 = bf16[16,8,512]{2,1,0:T(8,128)(2,1)S(1)} async-done(((bf16[16,8,512]{2,1,0:T(8,128)(2,1)}), bf16[16,8,512]{2,1,0:T(8,128)(2,1)S(1)}, u32[]{:S(2)}, u32[]{:S(2)}) %all-to-all-start.1) | async-done | bytes 131104 | tf_op jit(solution)/shard_map/all_to_all | solution.py:150
  50.9 4.7 %collective-permute-start.4 = (bf16[128,512]{1,0:T(8,128)(2,1)S(1)}, bf16[128,512]{1,0:T(8,128)(2,1)S(1)}, u32[]{:S(2)}, u32[]{:S(2)}) collective-permute-start(bf16[128,512]{1,0:T(8,128)(2,1)S(1)} %bitcast.11), channel_id=1, source_target_pairs={{0,16},{4,20},{8,24},{12,28},{16,32},{20,36},{24,40},{28,44},{32,4... | collective-permute-start | bytes 393224 | tf_op jit(solution)/shard_map/ppermute | solution.py:155
  55.6 4.8 %collective-permute-start.3 = (bf16[128,512]{1,0:T(8,128)(2,1)S(1)}, bf16[128,512]{1,0:T(8,128)(2,1)S(1)}, u32[]{:S(2)}, u32[]{:S(2)}) collective-permute-start(bf16[128,512]{1,0:T(8,128)(2,1)S(1)} %bitcast.12), channel_id=1, source_target_pairs={{0,8},{4,12},{8,16},{12,20},{16,24},{20,28},{24,32},{28,36},{32,40... | collective-permute-start | bytes 393224 | tf_op jit(solution)/shard_map/ppermute | solution.py:155
  60.4 3.6 %all-to-all-start.2 = ((bf16[16,8,2048]{2,1,0:T(8,128)(2,1)}), bf16[16,8,2048]{2,1,0:T(8,128)(2,1)S(1)}, u32[]{:S(2)}, u32[]{:S(2)}) async-start(bf16[16,8,2048]{2,1,0:T(8,128)(2,1)} %fusion), calls=%async_computation.2 | async-start | bytes 1048576 | tf_op jit(solution)/shard_map/all_to_all | solution.py:152
  64.0 0.0 collective-permute-done.4
  64.0 2.7 %collective-permute-start.5 = (bf16[128,512]{1,0:T(8,128)(2,1)S(1)}, bf16[128,512]{1,0:T(8,128)(2,1)S(1)}, u32[]{:S(2)}, u32[]{:S(2)}) collective-permute-start(bf16[128,512]{1,0:T(8,128)(2,1)S(1)} %collective-permute-done.4), channel_id=1, source_target_pairs={{0,8},{4,12},{8,16},{12,20},{16,24},{20,28},{24,32},{28,36},{32,40... | collective-permute-start | bytes 393224 | tf_op jit(solution)/shard_map/ppermute | solution.py:155
  66.7 4.6 %collective-permute-start.6 = (bf16[128,512]{1,0:T(8,128)(2,1)S(1)}, bf16[128,512]{1,0:T(8,128)(2,1)S(1)}, u32[]{:S(2)}, u32[]{:S(2)}) collective-permute-start(bf16[128,512]{1,0:T(8,128)(2,1)S(1)} %collective-permute-done.4), channel_id=1, source_target_pairs={{0,16},{4,20},{8,24},{12,28},{16,32},{20,36},{24,40},{28,44},{32,4... | collective-permute-start | bytes 393224 | tf_op jit(solution)/shard_map/ppermute | solution.py:155
  71.3 0.0 collective-permute-done.3
  71.4 2.8 %collective-permute-done.6 = bf16[128,512]{1,0:T(8,128)(2,1)S(1)} collective-permute-done((bf16[128,512]{1,0:T(8,128)(2,1)S(1)}, bf16[128,512]{1,0:T(8,128)(2,1)S(1)}, u32[]{:S(2)}, u32[]{:S(2)}) %collective-permute-start.6) | collective-permute-done | bytes 131104 | tf_op jit(solution)/shard_map/ppermute | solution.py:155
  74.3 0.0 copy-start
  74.3 1.9 %collective-permute-start.7 = (bf16[512,512]{1,0:T(8,128)(2,1)S(1)}, bf16[512,512]{1,0:T(8,128)(2,1)S(1)}, u32[]{:S(2)}, u32[]{:S(2)}) collective-permute-start(bf16[512,512]{1,0:T(8,128)(2,1)S(1)} %constant_dynamic-slice_fusion), channel_id=1, source_target_pairs={{0,4},{4,0},{8,12},{12,8},{16,20},{20,16},{24,28},{28,24},{32,36},... | collective-permute-start | bytes 1572872 | tf_op jit(solution)/shard_map/ppermute | solution.py:161
  76.3 1.9 %collective-permute-done.7.sib = bf16[512,512]{1,0:T(8,128)(2,1)S(1)} collective-permute-done((bf16[512,512]{1,0:T(8,128)(2,1)S(1)}, bf16[512,512]{1,0:T(8,128)(2,1)S(1)}, u32[]{:S(2)}, u32[]{:S(2)}) %collective-permute-start.7) | collective-permute-done | bytes 524320 | tf_op jit(solution)/shard_map/ppermute | solution.py:161
  78.1 4.1 %all-to-all-done.2 = bf16[16,8,2048]{2,1,0:T(8,128)(2,1)S(1)} async-done(((bf16[16,8,2048]{2,1,0:T(8,128)(2,1)}), bf16[16,8,2048]{2,1,0:T(8,128)(2,1)S(1)}, u32[]{:S(2)}, u32[]{:S(2)}) %all-to-all-start.2) | async-done | bytes 524320 | tf_op jit(solution)/shard_map/all_to_all | solution.py:152
  82.2 5.3 %shard_map.56 = bf16[128,2048]{1,0:T(8,128)(2,1)} custom-call(s32[1,4]{1,0:T(1,128)S(1)} %copy-done, bf16[128,2048]{1,0:T(8,128)(2,1)S(1)} %bitcast.10, bf16[640,512]{1,0:T(8,128)(2,1)S(1)} %constant_dynamic-update-slice_fusion.own, bf16[512,512]{1,0:T(8,128)(2,1)S(1)} %collective-permute-done.7.sib), custom_call_target="tpu_custom_call" | custom-call | flops 1207959552 | bytes 2228224 | tf_op jit(solution)/shard_map/pallas_call | solution.py:68
  (18 shorter events, 0.1 us)
Async XLA Ops:
  2.0 12.9 %copy-start.3 = (bf16[32,2048]{1,0:T(8,128)(2,1)S(1)}, bf16[32,2048]{1,0:T(8,128)(2,1)}, u32[]{:S(2)}) copy-start(bf16[32,2048]{1,0:T(8,128)(2,1)} %get-tuple-element.18) | copy-start | bytes 393220
  2.0 14.9 %copy-start.1 = (bf16[128,128]{1,0:T(8,128)(2,1)S(1)}, bf16[128,128]{1,0:T(8,128)(2,1)}, u32[]{:S(2)}) copy-start(bf16[128,128]{1,0:T(8,128)(2,1)} %get-tuple-element.14) | copy-start | bytes 98308
  2.0 14.8 %all-to-all-start = ((bf16[4,32,512]{2,1,0:T(8,128)(2,1)}), bf16[4,32,512]{2,1,0:T(8,128)(2,1)S(1)}, u32[]{:S(2)}, u32[]{:S(2)}) async-start(bf16[4,32,512]{2,1,0:T(8,128)(2,1)} %get-tuple-element.15), calls=%async_computation | async-start | bytes 262144 | tf_op jit(solution)/shard_map/all_to_all | solution.py:135
  7.2 31.0 %collective-permute-start.2 = (bf16[32,2048]{1,0:T(8,128)(2,1)}, bf16[32,2048]{1,0:T(8,128)(2,1)S(1)}, u32[]{:S(2)}, u32[]{:S(2)}) collective-permute-start(bf16[32,2048]{1,0:T(8,128)(2,1)} %get-tuple-element.20), channel_id=1, source_target_pairs={{0,3},{1,2},{2,1},{3,0},{4,7},{5,6},{6,5},{7,4},{8,11},{9,10},{10,... | collective-permute-start | bytes 393224 | tf_op jit(solution)/shard_map/ppermute | solution.py:140
  9.7 28.5 %collective-permute-start.1 = (bf16[32,2048]{1,0:T(8,128)(2,1)}, bf16[32,2048]{1,0:T(8,128)(2,1)S(1)}, u32[]{:S(2)}, u32[]{:S(2)}) collective-permute-start(bf16[32,2048]{1,0:T(8,128)(2,1)} %get-tuple-element.19), channel_id=1, source_target_pairs={{0,2},{1,3},{2,0},{3,1},{4,6},{5,7},{6,4},{7,5},{8,10},{9,11},{10,... | collective-permute-start | bytes 393224 | tf_op jit(solution)/shard_map/ppermute | solution.py:140
  14.9 23.3 %collective-permute-start = (bf16[32,2048]{1,0:T(8,128)(2,1)S(1)}, bf16[32,2048]{1,0:T(8,128)(2,1)S(1)}, u32[]{:S(2)}, u32[]{:S(2)}) collective-permute-start(bf16[32,2048]{1,0:T(8,128)(2,1)S(1)} %copy-done.3), channel_id=1, source_target_pairs={{0,1},{1,0},{2,3},{3,2},{4,5},{5,4},{6,7},{7,6},{8,9},{9,8},{10,11... | collective-permute-start | bytes 393224 | tf_op jit(solution)/shard_map/ppermute | solution.py:140
  17.7 20.6 %copy-start.2 = (bf16[32,2048]{1,0:T(8,128)(2,1)S(1)}, bf16[32,2048]{1,0:T(8,128)(2,1)}, u32[]{:S(2)}) copy-start(bf16[32,2048]{1,0:T(8,128)(2,1)} %get-tuple-element.17) | copy-start | bytes 393220
  17.7 20.6 %copy-start.4 = (bf16[128,128]{1,0:T(8,128)(2,1)S(1)}, bf16[128,128]{1,0:T(8,128)(2,1)}, u32[]{:S(2)}) copy-start(bf16[128,128]{1,0:T(8,128)(2,1)} %get-tuple-element.16) | copy-start | bytes 98308
  17.7 33.2 %all-to-all-start.1 = ((bf16[16,8,512]{2,1,0:T(8,128)(2,1)}), bf16[16,8,512]{2,1,0:T(8,128)(2,1)S(1)}, u32[]{:S(2)}, u32[]{:S(2)}) async-start(bf16[16,8,512]{2,1,0:T(8,128)(2,1)} %fusion.1), calls=%async_computation.1 | async-start | bytes 262144 | tf_op jit(solution)/shard_map/all_to_all | solution.py:150
  50.9 13.2 %collective-permute-start.4 = (bf16[128,512]{1,0:T(8,128)(2,1)S(1)}, bf16[128,512]{1,0:T(8,128)(2,1)S(1)}, u32[]{:S(2)}, u32[]{:S(2)}) collective-permute-start(bf16[128,512]{1,0:T(8,128)(2,1)S(1)} %bitcast.11), channel_id=1, source_target_pairs={{0,16},{4,20},{8,24},{12,28},{16,32},{20,36},{24,40},{28,44},{32,4... | collective-permute-start | bytes 393224 | tf_op jit(solution)/shard_map/ppermute | solution.py:155
  55.6 15.8 %collective-permute-start.3 = (bf16[128,512]{1,0:T(8,128)(2,1)S(1)}, bf16[128,512]{1,0:T(8,128)(2,1)S(1)}, u32[]{:S(2)}, u32[]{:S(2)}) collective-permute-start(bf16[128,512]{1,0:T(8,128)(2,1)S(1)} %bitcast.12), channel_id=1, source_target_pairs={{0,8},{4,12},{8,16},{12,20},{16,24},{20,28},{24,32},{28,36},{32,40... | collective-permute-start | bytes 393224 | tf_op jit(solution)/shard_map/ppermute | solution.py:155
  60.4 21.8 %all-to-all-start.2 = ((bf16[16,8,2048]{2,1,0:T(8,128)(2,1)}), bf16[16,8,2048]{2,1,0:T(8,128)(2,1)S(1)}, u32[]{:S(2)}, u32[]{:S(2)}) async-start(bf16[16,8,2048]{2,1,0:T(8,128)(2,1)} %fusion), calls=%async_computation.2 | async-start | bytes 1048576 | tf_op jit(solution)/shard_map/all_to_all | solution.py:152
  64.0 7.4 %collective-permute-start.5 = (bf16[128,512]{1,0:T(8,128)(2,1)S(1)}, bf16[128,512]{1,0:T(8,128)(2,1)S(1)}, u32[]{:S(2)}, u32[]{:S(2)}) collective-permute-start(bf16[128,512]{1,0:T(8,128)(2,1)S(1)} %collective-permute-done.4), channel_id=1, source_target_pairs={{0,8},{4,12},{8,16},{12,20},{16,24},{20,28},{24,32},{28,36},{32,40... | collective-permute-start | bytes 393224 | tf_op jit(solution)/shard_map/ppermute | solution.py:155
  66.7 7.5 %collective-permute-start.6 = (bf16[128,512]{1,0:T(8,128)(2,1)S(1)}, bf16[128,512]{1,0:T(8,128)(2,1)S(1)}, u32[]{:S(2)}, u32[]{:S(2)}) collective-permute-start(bf16[128,512]{1,0:T(8,128)(2,1)S(1)} %collective-permute-done.4), channel_id=1, source_target_pairs={{0,16},{4,20},{8,24},{12,28},{16,32},{20,36},{24,40},{28,44},{32,4... | collective-permute-start | bytes 393224 | tf_op jit(solution)/shard_map/ppermute | solution.py:155
  74.3 7.9 %copy-start = (s32[1,4]{1,0:T(1,128)S(1)}, s32[1,4]{1,0:T(1,128)}, u32[]{:S(2)}) copy-start(s32[1,4]{1,0:T(1,128)} %lengths.1) | copy-start | bytes 52
  74.3 3.8 %collective-permute-start.7 = (bf16[512,512]{1,0:T(8,128)(2,1)S(1)}, bf16[512,512]{1,0:T(8,128)(2,1)S(1)}, u32[]{:S(2)}, u32[]{:S(2)}) collective-permute-start(bf16[512,512]{1,0:T(8,128)(2,1)S(1)} %constant_dynamic-slice_fusion), channel_id=1, source_target_pairs={{0,4},{4,0},{8,12},{12,8},{16,20},{20,16},{24,28},{28,24},{32,36},... | collective-permute-start | bytes 1572872 | tf_op jit(solution)/shard_map/ppermute | solution.py:161
